TPU v7x, 32 devices: a whole 2x2x4 slice. The times are simulated.
32 devices in a mesh: slot: 16 (over z, y, core), blk: 2 (over x).
Axes of the slice: x: 2, y: 2, z: 4, core: 2. Of those that a mesh axis runs over, the one named last changes fastest.
Arguments:
- atom_feats: bfloat16 [48, 512, 512], P('slot', 'blk'), may hold values from -6 to 6
- pair_feats: bfloat16 [48, 64, 512, 512], P('slot', None, 'blk'), may hold values from -6 to 6
- type_ids: int32 [48, 512], P('slot', 'blk'), may hold values from 0 to 31
- mol_lengths: int32 [48, 4], P('slot'), may hold values from 1 to 509, as said below
- type_table: float32 [32, 512], replicated, may hold values from -4 to 4
- ln1_gain: float32 [512], replicated, may hold values from 0.5 to 1.5
- ln1_shift: float32 [512], replicated, may hold values from -1 to 1
- w_query: bfloat16 [512, 512], replicated, may hold values from -0.25 to 0.25
- b_query: float32 [512], replicated, may hold values from -1.5 to 1.5
- w_key: bfloat16 [512, 512], replicated, may hold values from -0.25 to 0.25
- w_value: bfloat16 [512, 512], replicated, may hold values from -0.25 to 0.25
- b_value: float32 [512], replicated, may hold values from -1.5 to 1.5
- w_out: bfloat16 [512, 512], replicated, may hold values from -2 to 2
- b_out: float32 [512], replicated, may hold values from -1.5 to 1.5
- ln2_gain: float32 [512], replicated, may hold values from 0.5 to 1.5
- ln2_shift: float32 [512], replicated, may hold values from -1 to 1
- w_up: bfloat16 [512, 2048], replicated, may hold values from -0.25 to 0.25
- b_up: float32 [2048], replicated, may hold values from -1.5 to 1.5
- w_down: bfloat16 [2048, 512], replicated, may hold values from -0.125 to 0.125
- b_down: float32 [512], replicated, may hold values from -1.5 to 1.5
- atom_cotan: bfloat16 [48, 512, 512], P('slot', 'blk'), may hold values from -6 to 6
- pair_cotan: bfloat16 [48, 64, 512, 512], P('slot', None, 'blk'), may hold values from -6 to 6
Outputs:
- atom_out: bfloat16 [48, 512, 512], P('slot', 'blk')
- pair_out: bfloat16 [48, 64, 512, 512], P('slot', None, 'blk')
- penalty: float32 [], replicated
- atom_grad: bfloat16 [48, 512, 512], P('slot', 'blk')
- pair_grad: bfloat16 [48, 64, 512, 512], P('slot', None, 'blk')
- g_type_table: float32 [32, 512], replicated
- g_ln1_gain: float32 [512], replicated
- g_ln1_shift: float32 [512], replicated
- g_w_query: float32 [512, 512], replicated
- g_b_query: float32 [512], replicated
- g_w_key: float32 [512, 512], replicated
- g_w_value: float32 [512, 512], replicated
- g_b_value: float32 [512], replicated
- g_w_out: float32 [512, 512], replicated
- g_b_out: float32 [512], replicated
- g_ln2_gain: float32 [512], replicated
- g_ln2_shift: float32 [512], replicated
- g_w_up: float32 [512, 2048], replicated
- g_b_up: float32 [2048], replicated
- g_w_down: float32 [2048, 512], replicated
- g_b_down: float32 [512], replicated
Inputs may be any that keep to these rules, and one draw needn't show every extreme that they name: `mol_lengths`: each slot holds 4 molecules that fill its 512 atoms in order with no padding; one of them, at a place drawn per slot, covers from the slot's first block of 256 atoms to its last, and the others have at most (255) // 3 atoms each. In the first slot the others have one atom each.
All inputs are finite; a program needn't handle non-finite values.
Results may differ from a plain program's by a relative error of at most 0.007.
The roundings to bfloat16 on the way count: a program that leaves them out, or rounds other values in their place, can miss the bound.
Values may be sent and summed in bfloat16 or wider, within the bound.
No kernel may reach another device: no remote copies, remote signals or barrier semaphores. Data moves between devices by JAX's collectives and lax.ppermute only.
A program may use at most 640 MiB of HBM per device.

v0:
```python
import jax
import jax.numpy as jnp
from jax import lax
from jax.sharding import PartitionSpec as P

EPSILON = 1e-05
HIGHEST = lax.Precision.HIGHEST


def norm_parts(values, gain, shift):
    center = values - jnp.mean(values, axis=-1, keepdims=True)
    inverse = lax.rsqrt(jnp.mean(center * center, axis=-1, keepdims=True) + EPSILON)
    unit_rows = center * inverse
    return (unit_rows * gain + shift, unit_rows, inverse)


def norm_back(upstream, unit_rows, inverse, gain):
    scaled = upstream * gain
    first = jnp.mean(scaled, axis=-1, keepdims=True)
    second = jnp.mean(scaled * unit_rows, axis=-1, keepdims=True)
    grad_in = inverse * (scaled - first - unit_rows * second)
    return (grad_in, jnp.sum(upstream * unit_rows, axis=0), jnp.sum(upstream, axis=0))


def gelu_slope(values):
    cumulative = 0.5 * (1.0 + lax.erf(values * 0.7071067811865476))
    density = jnp.exp(-0.5 * values * values) * 0.3989422804014327
    return cumulative + values * density


def project(left, right):
    return jnp.dot(left, right, preferred_element_type=jnp.float32)


def project_back(left, right):
    return jnp.einsum("rd,ed->re", left, right, preferred_element_type=jnp.float32)


def weight_grad(left, right):
    return jnp.einsum("rd,re->de", left, right, preferred_element_type=jnp.float32)


def local(
    atom_feats,
    pair_feats,
    type_ids,
    mol_lengths,
    type_table,
    ln1_gain,
    ln1_shift,
    w_query,
    b_query,
    w_key,
    w_value,
    b_value,
    w_out,
    b_out,
    ln2_gain,
    ln2_shift,
    w_up,
    b_up,
    w_down,
    b_down,
    atom_cotan,
    pair_cotan,
):
    slot_count, row_count, model_width = atom_feats.shape
    head_count = pair_feats.shape[1]
    slot_len = pair_feats.shape[3]
    head_size = model_width // head_count
    score_scale = head_size ** (-0.5)
    flat_rows = slot_count * row_count
    type_count = type_table.shape[0]
    onehot = (
        type_ids.reshape(flat_rows)[:, None] == jnp.arange(type_count, dtype=jnp.int32)[None, :]
    ).astype(jnp.float32)
    base = atom_feats.reshape(flat_rows, model_width).astype(jnp.float32) + jnp.dot(
        onehot, type_table, precision=HIGHEST
    )
    bounds = jnp.cumsum(mol_lengths, axis=1)
    places = jnp.arange(slot_len, dtype=jnp.int32)
    mol_ids = jnp.sum((places[None, :, None] >= bounds[:, None, :]).astype(jnp.int32), axis=2)
    row_start = lax.axis_index("blk") * row_count
    row_ids = lax.dynamic_slice_in_dim(mol_ids, row_start, row_count, 1)
    pair_mask = (row_ids[:, :, None] == mol_ids[:, None, :])[:, None, :, :]
    normed1, unit1, inverse1 = norm_parts(base, ln1_gain, ln1_shift)
    normed1_low = normed1.astype(jnp.bfloat16)
    query_low = (project(normed1_low, w_query) + b_query).astype(jnp.bfloat16)
    key_low = project(normed1_low, w_key).astype(jnp.bfloat16)
    value_low = (project(normed1_low, w_value) + b_value).astype(jnp.bfloat16)
    key_rows = key_low.reshape(slot_count, row_count, model_width)
    value_rows = value_low.reshape(slot_count, row_count, model_width)
    whole_key, whole_value = (
        lax.all_gather(key_rows, "blk", axis=1, tiled=True),
        lax.all_gather(value_rows, "blk", axis=1, tiled=True),
    )
    query_head_split = query_low.reshape(slot_count, row_count, head_count, head_size)

    def scores(key_all):
        key_head_split = key_all.reshape(slot_count, slot_len, head_count, head_size)
        raw = jnp.einsum(
            "vniu,vyiu->viny", query_head_split, key_head_split, preferred_element_type=jnp.float32
        )
        return raw * score_scale + pair_feats.astype(jnp.float32)

    logits = scores(whole_key)
    masked = jnp.where(pair_mask, logits, -1000000000.0)
    row_top = jnp.max(masked, axis=-1, keepdims=True)
    exponent = jnp.exp(masked - row_top)
    row_total = jnp.sum(exponent, axis=-1, keepdims=True)
    log_total = row_top + jnp.log(row_total)
    probability_reduced = (exponent / row_total).astype(jnp.bfloat16)
    value_head_split = whole_value.reshape(slot_count, slot_len, head_count, head_size)
    mixed = jnp.einsum(
        "cowi,ciom->cwom", probability_reduced, value_head_split, preferred_element_type=jnp.float32
    )
    mixed_low = mixed.reshape(flat_rows, model_width).astype(jnp.bfloat16)
    resid = base + project(mixed_low, w_out) + b_out
    normed2, unit2, inverse2 = norm_parts(resid, ln2_gain, ln2_shift)
    normed2_low = normed2.astype(jnp.bfloat16)
    hidden_pre = project(normed2_low, w_up) + b_up
    hidden_low = jax.nn.gelu(hidden_pre, approximate=False).astype(jnp.bfloat16)
    atom_out = resid + project(hidden_low, w_down) + b_down
    local_count = jnp.sum(pair_mask.astype(jnp.float32))
    local_pen = jnp.sum(jnp.where(pair_mask, logits * logits, 0.0))
    pair_total, pen_total = lax.psum((local_count, local_pen), ("slot", "blk"))
    penalty = pen_total / pair_total
    out_grad = atom_cotan.reshape(flat_rows, model_width)
    g_w_down = weight_grad(hidden_low, out_grad)
    g_b_down = jnp.sum(out_grad.astype(jnp.float32), axis=0)
    hidden_grad = project_back(out_grad, w_down) * gelu_slope(hidden_pre)
    hidden_grad_low = hidden_grad.astype(jnp.bfloat16)
    g_w_up = weight_grad(normed2_low, hidden_grad_low)
    g_b_up = jnp.sum(hidden_grad_low.astype(jnp.float32), axis=0)
    resid_back, g_ln2_gain, g_ln2_shift = norm_back(
        project_back(hidden_grad_low, w_up), unit2, inverse2, ln2_gain
    )
    resid_grad = out_grad.astype(jnp.float32) + resid_back
    resid_grad_low = resid_grad.astype(jnp.bfloat16)
    g_w_out = weight_grad(mixed_low, resid_grad_low)
    g_b_out = jnp.sum(resid_grad_low.astype(jnp.float32), axis=0)
    mixed_grad = project_back(resid_grad_low, w_out).astype(jnp.bfloat16)
    gradient_head_rows = mixed_grad.reshape(slot_count, row_count, head_count, head_size)
    back_key, back_value = (whole_key, whole_value)
    logits_again = scores(back_key)
    probs_soft = jnp.where(pair_mask, jnp.exp(logits_again - log_total), 0.0)
    backward_head_rows = back_value.reshape(slot_count, slot_len, head_count, head_size)
    probs_grad = jnp.einsum(
        "vniu,vyiu->viny",
        gradient_head_rows,
        backward_head_rows,
        preferred_element_type=jnp.float32,
    )
    soft_grad = probs_soft * (probs_grad - jnp.sum(probs_soft * probs_grad, axis=-1, keepdims=True))
    logit_grad = (
        soft_grad
        + pair_cotan.astype(jnp.float32)
        + jnp.where(pair_mask, 2.0 * logits_again / pair_total, 0.0)
    )
    logit_reduced_precision = logit_grad.astype(jnp.bfloat16)
    key_head_backward = back_key.reshape(slot_count, slot_len, head_count, head_size)
    query_grad = (
        jnp.einsum(
            "cowi,ciom->cwom",
            logit_reduced_precision,
            key_head_backward,
            preferred_element_type=jnp.float32,
        )
        * score_scale
    )
    query_grad = query_grad.reshape(flat_rows, model_width).astype(jnp.bfloat16)
    key_part = (
        jnp.einsum(
            "eamg,emax->egax",
            logit_reduced_precision,
            query_head_split,
            preferred_element_type=jnp.float32,
        )
        * score_scale
    )
    key_part = key_part.reshape(slot_count, slot_len, model_width)
    value_part = jnp.einsum(
        "eamg,emax->egax",
        probs_soft.astype(jnp.bfloat16),
        gradient_head_rows,
        preferred_element_type=jnp.float32,
    )
    value_part = value_part.reshape(slot_count, slot_len, model_width)
    key_sum, value_sum = (
        lax.psum_scatter(key_part, "blk", scatter_dimension=1, tiled=True),
        lax.psum_scatter(value_part, "blk", scatter_dimension=1, tiled=True),
    )
    key_grad = key_sum.reshape(flat_rows, model_width).astype(jnp.bfloat16)
    value_grad = value_sum.reshape(flat_rows, model_width).astype(jnp.bfloat16)
    g_w_query = weight_grad(normed1_low, query_grad)
    g_b_query = jnp.sum(query_grad.astype(jnp.float32), axis=0)
    g_w_key = weight_grad(normed1_low, key_grad)
    g_w_value = weight_grad(normed1_low, value_grad)
    g_b_value = jnp.sum(value_grad.astype(jnp.float32), axis=0)
    norm_in = (
        project_back(query_grad, w_query)
        + project_back(key_grad, w_key)
        + project_back(value_grad, w_value)
    )
    base_back, g_ln1_gain, g_ln1_shift = norm_back(norm_in, unit1, inverse1, ln1_gain)
    base_grad = resid_grad + base_back
    g_type_table = jnp.einsum("rt,rd->td", onehot, base_grad, precision=HIGHEST)
    (
        g_type_table,
        g_ln1_gain,
        g_ln1_shift,
        g_w_query,
        g_b_query,
        g_w_key,
        g_w_value,
        g_b_value,
        g_w_out,
        g_b_out,
        g_ln2_gain,
        g_ln2_shift,
        g_w_up,
        g_b_up,
        g_w_down,
        g_b_down,
    ) = lax.psum(
        (
            g_type_table,
            g_ln1_gain,
            g_ln1_shift,
            g_w_query,
            g_b_query,
            g_w_key,
            g_w_value,
            g_b_value,
            g_w_out,
            g_b_out,
            g_ln2_gain,
            g_ln2_shift,
            g_w_up,
            g_b_up,
            g_w_down,
            g_b_down,
        ),
        ("slot", "blk"),
    )
    return (
        atom_out.reshape(slot_count, row_count, model_width).astype(jnp.bfloat16),
        logits.astype(jnp.bfloat16),
        penalty,
        base_grad.reshape(slot_count, row_count, model_width).astype(jnp.bfloat16),
        logit_reduced_precision,
        g_type_table,
        g_ln1_gain,
        g_ln1_shift,
        g_w_query,
        g_b_query,
        g_w_key,
        g_w_value,
        g_b_value,
        g_w_out,
        g_b_out,
        g_ln2_gain,
        g_ln2_shift,
        g_w_up,
        g_b_up,
        g_w_down,
        g_b_down,
    )


def solution(mesh):
    placed = (
        P("slot", "blk", None),
        P("slot", None, "blk", None),
        P("slot", "blk"),
        P("slot", None),
        P(),
        P(),
        P(),
        P(),
        P(),
        P(),
        P(),
        P(),
        P(),
        P(),
        P(),
        P(),
        P(),
        P(),
        P(),
        P(),
        P("slot", "blk", None),
        P("slot", None, "blk", None),
    )
    return jax.shard_map(
        local,
        mesh=mesh,
        in_specs=placed,
        out_specs=(
            P("slot", "blk", None),
            P("slot", None, "blk", None),
            P(),
            P("slot", "blk", None),
            P("slot", None, "blk", None),
            P(),
            P(),
            P(),
            P(),
            P(),
            P(),
            P(),
            P(),
            P(),
            P(),
            P(),
            P(),
            P(),
            P(),
            P(),
            P(),
        ),
        check_vma=False,
    )
```

profile of v0, /device:TPU:0, one launch (start us, length us, event | category | flops | bytes accessed | tf_op | source)
XLA Modules:
  0.0 998.7 jit_solution(12140722220331976703)
XLA Ops:
  7.3 0.8 eq.44
  8.1 2.2 fusion.62
  10.3 0.3 multiply_reduce_fusion.6
  10.7 0.8 copy-done.2
  11.5 1.0 add_convert_fusion.5
  12.6 1.4 convolution_convert_fusion.1
  14.1 2.5 add_convert_fusion.4
  17.3 1.1 convert_reduce_fusion.5
  18.4 2.5 add_convert_fusion.3
  20.9 2.3 copy.62
  23.2 2.5 reshape.163
  25.7 43.1 %psum.127 = f32[]{:T(128)} all-reduce(f32[]{:T(128)} %convert_reduce_fusion.5), channel_id=1, replica_groups=mesh['slot'=16,'blk'=2] {'slot','blk'}, use_global_device_ids=true, to_apply=%region_11.12 | all-reduce | flops 1 | bytes 8 | tf_op jit(solution)/shard_map/psum | solution.py:126
  68.8 2.6 copy.63
  71.4 54.3 %select_reduce_fusion.1 = (f32[3,64,256]{2,1,0:T(8,128)}, f32[3,64,256,512]{3,2,1,0:T(8,128)}) fusion(pred[3,256,512]{2,1,0:T(8,128)(4,1)S(1)} %broadcast_compare_fusion, bf16[3,64,256,512]{3,2,1,0:T(8,128)(2,1)} %param.23, bf16[3,512,512]{1,2,0:T(8,128)(2,1)} %copy.63, bf16[3,256,64,8]{1,0,3,2:T(4,128)(2,1)S(1)} %reshape.163), kind=kOutput, calls=%fused_computation.10 | convolution fusion | flops 528433152 | bytes 153944064 | tf_op jit(solution)/shard_map/vniu,vyiu->viny/dot_general | solution.py:101
  125.8 79.5 %select_reduce_fusion = (f32[]{:T(128)}, f32[3,64,256]{2,1,0:T(8,128)S(1)}, bf16[3,64,256,512]{3,2,1,0:T(8,128)(2,1)}) fusion(f32[3,64,256,512]{3,2,1,0:T(8,128)} %get-tuple-element.58, pred[3,256,512]{2,1,0:T(8,128)(4,1)S(1)} %broadcast_compare_fusion, f32[3,64,256]{2,1,0:T(8,128)} %get-tuple-element.57), kind=kLoop, calls=%fused_computation.5 | loop fusion | flops 176111616 | bytes 151781376 | tf_op jit(solution)/shard_map/reduce_sum | solution.py:125
  205.3 0.7 log_add_fusion
  206.0 2.6 copy.61
  208.6 36.2 %fusion.43 = bf16[3,256,64,8]{1,3,2,0:T(8,128)(2,1)S(1)} fusion(f32[3,64,256,512]{3,2,1,0:T(8,128)} %get-tuple-element.58, f32[3,64,256]{2,1,0:T(8,128)S(1)} %get-tuple-element.22, f32[3,64,256]{2,1,0:T(8,128)S(1)} %copy-done.30, pred[3,256,512]{2,1,0:T(8,128)(4,1)S(1)} %broadcast_compare_fusion, bf16[3,512,512]{1,2,0:T(8,128)(2,1)} %copy.61), kind=kOutput, calls=%fused_computation.82 | convolution fusion | flops 503709696 | bytes 103809024 | tf_op jit(solution)/shard_map/cowi,ciom->cwom/dot_general | solution.py:114
  244.8 0.7 copy.88
  245.7 0.5 copy-done.3
  246.2 0.7 fusion.63
  246.9 0.3 multiply_reduce_fusion.5
  247.4 16.6 %fusion.15 = (bf16[768,2048]{1,0:T(8,128)(2,1)}, f32[768,2048]{1,0:T(8,128)S(1)}) fusion(f32[2048]{0:T(1024)S(1)} %copy-done.60, bf16[512,2048]{1,0:T(8,128)(2,1)S(1)} %copy-done, f32[768,512]{1,0:T(8,128)S(1)} %get-tuple-element.60, f32[512]{0:T(512)S(1)} %copy-done.50, f32[512]{0:T(512)S(1)} %copy-done.46, f32[768]{0:T(1024)S(1)} %add_rsqrt_fusion, ...), kind=kOutput, calls=%fused_computation.22 | convolution fusion | flops 1716387840 | bytes 13125632 | tf_op jit(solution)/shard_map/dot_general | solution.py:32
  263.9 5.0 convert_reduce_fusion
  268.9 2.8 multiply_reduce_fusion.1
  271.7 1.2 convert_reduce_fusion.2
  272.9 0.6 convolution_convert_fusion
  273.5 1.2 copy.66
  274.7 2.5 reshape.167
  277.2 1.0 copy-done.16
  278.2 35.9 %fusion.35 = f32[3,64,256,512]{3,2,1,0:T(8,128)} fusion(bf16[3,512,512]{1,2,0:T(8,128)(2,1)} %copy.61, bf16[3,256,64,8]{1,0,3,2:T(4,128)(2,1)S(1)} %reshape.167), kind=kOutput, calls=%fused_computation.51 | convolution fusion | flops 402653184 | bytes 103022592 | tf_op jit(solution)/shard_map/vniu,vyiu->viny/dot_general | solution.py:148
  314.1 299.9 %add_convert_fusion = bf16[3,64,256,512]{3,2,1,0:T(8,128)(2,1)} fusion(f32[3,64,256,512]{3,2,1,0:T(8,128)} %get-tuple-element.58, bf16[3,64,256,512]{3,2,1,0:T(8,128)(2,1)} %param.43, f32[3,64,256,512]{3,2,1,0:T(8,128)} %fusion.35, f32[]{:T(128)} %psum.127, f32[3,64,256]{2,1,0:T(8,128)S(1)} %copy-done.31, pred[3,256,512]{2,1,0:T(8,128)(4,1)S(1)} %broadcast_compare_fusion), kind=kOutput, calls=%fused_computation.1 | output fusion | flops 352371200 | bytes 302579712 | tf_op jit(solution)/shard_map/sub | solution.py:154
  614.0 20.4 %multiply_bitcast_fusion = f32[3,512,512]{1,2,0:T(8,128)} fusion(bf16[3,64,256,512]{3,2,1,0:T(8,128)(2,1)} %add_convert_fusion, bf16[3,256,64,8]{1,0,3,2:T(4,128)(2,1)S(1)} %copy-done.15), kind=kOutput, calls=%fused_computation.45 | convolution fusion | flops 403439616 | bytes 54263808 | tf_op jit(solution)/shard_map/eamg,emax->egax/dot_general | solution.py:173
  634.4 3.6 copy.70
  638.1 35.4 %fusion.29 = f32[3,512,512]{1,2,0:T(8,128)} fusion(f32[3,64,256,512]{3,2,1,0:T(8,128)} %get-tuple-element.58, f32[3,64,256]{2,1,0:T(8,128)S(1)} %copy-done.31, pred[3,256,512]{2,1,0:T(8,128)(4,1)S(1)} %broadcast_compare_fusion, bf16[3,256,64,8]{1,0,3,2:T(4,128)(2,1)S(1)} %copy-done.17), kind=kOutput, calls=%fused_computation.46 | convolution fusion | flops 478150656 | bytes 105185280 | tf_op jit(solution)/shard_map/eamg,emax->egax/dot_general | solution.py:182
  673.5 3.6 copy.72
  677.2 22.2 %convert_reduce_fusion.4 = (f32[64,8]{1,0:T(8,128)S(1)}, bf16[3,64,8,256]{3,2,1,0:T(8,128)(2,1)}) fusion(bf16[3,64,256,512]{3,2,1,0:T(8,128)(2,1)} %add_convert_fusion, bf16[3,512,512]{1,2,0:T(8,128)(2,1)S(1)} %copy-done.11), kind=kOutput, calls=%fused_computation.58 | convolution fusion | flops 404225536 | bytes 52692992 | tf_op jit(solution)/shard_map/cowi,ciom->cwom/dot_general | solution.py:163
  699.5 2.0 copy.87
  701.7 1.6 fusion.66
  703.3 1.8 fusion.64
  705.0 1.6 fusion.55
  706.7 3.9 fusion.69
  710.6 4.1 fusion.59
  714.7 1.6 convert_element_type.161
  716.3 1.6 fusion.67
  717.9 1.8 fusion.65
  719.7 7.5 reduce-scatter.5.cloned.1.call-done
  727.2 1.7 convert_reduce_fusion.3
  729.0 1.6 fusion.68
  730.6 1.3 multiply_reduce_fusion.2
  732.0 1.4 fusion.61
  733.4 1.4 fusion.50
  734.9 1.1 copy-done.26
  736.5 5.2 add_convert_fusion.1
  741.8 41.7 %all-reduce = (f32[]{:T(128)}, f32[512]{0:T(512)}, f32[512]{0:T(512)}, f32[512]{0:T(512)}, f32[512]{0:T(512)}, /*index=5*/f32[512]{0:T(512)}, f32[512]{0:T(512)}, f32[512]{0:T(512)}, f32[2048]{0:T(1024)}, f32[512]{0:T(512)}) all-reduce(f32[]{:T(128)} %get-tuple-element.21, ...), channel_id=1, replica_groups=mesh['slot'=16,'blk'=2] {'slot','blk'}, use_global_device_ids=true, to_apply=%region_9.10 | all-reduce | flops 6145 | bytes 49160 | tf_op jit(solution)/shard_map/psum | solution.py:126
  784.8 191.8 %all-reduce.4.cloned.1.call-done = (f32[32,512]{1,0:T(8,128)}, f32[512,512]{1,0:T(8,128)}, f32[512,512]{1,0:T(8,128)}, f32[512,512]{1,0:T(8,128)}, f32[512,512]{...) async-done(((f32[32,512]{1,0:T(8,128)}, f32[512,512]{1,0:T(8,128)}, f32[512,512]{1,0:T(8,128)}, f32[512,512]{1,0:T(8,128)}, f32[512,512]{1,0:T(8,128)}, ...) | async-done | bytes 12648464 | tf_op jit(solution)/shard_map/psum | solution.py:225
  976.6 1.6 copy.96
  978.2 2.4 copy.97
  980.6 2.3 copy.98
  982.9 1.0 copy.99
  983.9 1.0 copy.100
  984.8 2.1 copy.101
  987.0 1.6 copy-done.22
  988.5 2.0 copy.102
  (153 shorter events, 2.2 us)
Async XLA Ops:
  7.2 240.1 %copy-start = (bf16[512,2048]{1,0:T(8,128)(2,1)S(1)}, bf16[512,2048]{1,0:T(8,128)(2,1)}, u32[]{:S(2)}) copy-start(bf16[512,2048]{1,0:T(8,128)(2,1)} %param.38) | copy-start | bytes 6291460
  7.2 61.6 %all-gather.5.cloned.1.call-start = ((), (), s32[]{:S(2)}) async-start(), calls=%async_computation.3 | async-start | bytes 2359296 | tf_op jit(solution)/shard_map/all_gather | solution.py:94
  8.1 6.0 copy-start.48
  8.1 4.5 copy-start.35
  8.1 6.0 copy-start.61
  10.3 3.7 copy-start.42
  11.5 2.5 copy-start.44
  11.5 5.2 copy-start.58
  12.6 8.3 copy-start.12
  12.6 5.8 copy-start.62
  14.1 191.9 %all-gather.3.cloned.1.call-start = ((), (), s32[]{:S(2)}) async-start(), calls=%async_computation.2 | async-start | bytes 2359296 | tf_op jit(solution)/shard_map/all_gather | solution.py:95
  16.7 698.1 %reduce-scatter.3.cloned.1.call-start = ((), (), s32[]{:S(2)}) async-start(), calls=%async_computation.4 | async-start | bytes 4718592 | tf_op jit(solution)/shard_map/reduce_scatter | solution.py:190
  25.7 100.0 %copy-start.14 = (bf16[3,256,64,8]{1,0,3,2:T(4,128)(2,1)}, bf16[3,256,64,8]{1,0,3,2:T(4,128)(2,1)S(1)}, u32[]{:S(2)}) copy-start(bf16[3,256,64,8]{1,0,3,2:T(4,128)(2,1)S(1)} %reshape.163) | copy-start | bytes 2359300
  125.8 79.5 %copy-start.30 = (f32[3,64,256]{2,1,0:T(8,128)S(1)}, f32[3,64,256]{2,1,0:T(8,128)}, u32[]{:S(2)}) copy-start(f32[3,64,256]{2,1,0:T(8,128)} %get-tuple-element.57) | copy-start | bytes 589828
  208.5 37.2 %copy-start.29 = (bf16[512,512]{1,0:T(8,128)(2,1)S(1)}, bf16[512,512]{1,0:T(8,128)(2,1)}, u32[]{:S(2)}) copy-start(bf16[512,512]{1,0:T(8,128)(2,1)} %param.34) | copy-start | bytes 1572868
  208.5 37.2 %copy-start.55 = (f32[512]{0:T(512)S(1)}, f32[512]{0:T(512)}, u32[]{:S(2)}) copy-start(f32[512]{0:T(512)} %param.35) | copy-start | bytes 6148
  245.5 1.8 copy-start.46
  245.5 1.8 copy-start.50
  245.5 1.8 copy-start.60
  246.9 24.7 %copy-start.5 = (f32[768,512]{1,0:T(8,128)}, f32[768,512]{1,0:T(8,128)S(1)}, u32[]{:S(2)}) copy-start(f32[768,512]{1,0:T(8,128)S(1)} %get-tuple-element.60) | copy-start | bytes 4718596
  246.9 24.7 %copy-start.38 = (f32[768]{0:T(1024)}, f32[768]{0:T(1024)S(1)}, u32[]{:S(2)}) copy-start(f32[768]{0:T(1024)S(1)} %broadcast_multiply_fusion.4) | copy-start | bytes 9220
  247.3 24.3 %copy-start.40 = (f32[768]{0:T(1024)}, f32[768]{0:T(1024)S(1)}, u32[]{:S(2)}) copy-start(f32[768]{0:T(1024)S(1)} %add_rsqrt_fusion) | copy-start | bytes 9220
  247.3 16.6 %copy-start.24 = (bf16[3,256,512]{2,1,0:T(8,128)(2,1)S(1)}, bf16[3,256,512]{2,1,0:T(8,128)(2,1)}, u32[]{:S(2)}) copy-start(bf16[3,256,512]{2,1,0:T(8,128)(2,1)} %param.42) | copy-start | bytes 2359300
  247.4 16.6 %copy-start.59 = (bf16[2048,512]{1,0:T(8,128)(2,1)S(1)}, bf16[2048,512]{1,0:T(8,128)(2,1)}, u32[]{:S(2)}) copy-start(bf16[2048,512]{1,0:T(8,128)(2,1)} %param.40) | copy-start | bytes 6291460
  268.9 2.8 copy-start.27
  272.9 41.2 %copy-start.8 = (f32[768,512]{1,0:T(8,128)}, f32[768,512]{1,0:T(8,128)S(1)}, u32[]{:S(2)}) copy-start(f32[768,512]{1,0:T(8,128)S(1)} %get-tuple-element.51) | copy-start | bytes 4718596
  278.2 35.9 %copy-start.31 = (f32[3,64,256]{2,1,0:T(8,128)S(1)}, f32[3,64,256]{2,1,0:T(8,128)}, u32[]{:S(2)}) copy-start(f32[3,64,256]{2,1,0:T(8,128)} %log_add_fusion) | copy-start | bytes 589828
  314.1 299.9 %copy-start.15 = (bf16[3,256,64,8]{1,0,3,2:T(4,128)(2,1)S(1)}, bf16[3,256,64,8]{1,0,3,2:T(4,128)(2,1)}, u32[]{:S(2)}) copy-start(bf16[3,256,64,8]{1,0,3,2:T(4,128)(2,1)} %copy-done.14) | copy-start | bytes 2359300
  634.4 3.7 copy-start.17
  638.1 89.1 %reduce-scatter.5.cloned.1.call-start = ((), (), s32[]{:S(2)}) async-start(), calls=%async_computation.5 | async-start | bytes 4718592 | tf_op jit(solution)/shard_map/reduce_scatter | solution.py:191
  673.5 3.7 copy-start.11
  677.1 24.5 %copy-start.13 = (bf16[768,512]{1,0:T(8,128)(2,1)S(1)}, bf16[768,512]{1,0:T(8,128)(2,1)}, u32[]{:S(2)}) copy-start(bf16[768,512]{1,0:T(8,128)(2,1)} %copy-done.12) | copy-start | bytes 2359300
  677.1 299.4 %all-reduce.4.cloned.1.call-start = ((), (), s32[]{:S(2)}) async-start(), calls=%async_computation.6 | async-start | bytes 25296896 | tf_op jit(solution)/shard_map/psum | solution.py:225
  699.4 3.8 copy-start.34
  699.5 5.6 copy-start.9
  699.5 5.6 copy-start.19
  701.6 5.0 copy-start.25
  701.6 5.0 copy-start.64
  706.6 4.0 copy-start.6
  706.6 4.0 copy-start.28
  706.6 4.0 copy-start.39
  706.6 4.0 copy-start.41
  706.6 4.0 copy-start.47
  706.6 4.0 copy-start.51
  714.7 3.1 copy-start.36
  717.9 12.7 %copy-start.4 = (f32[768,512]{1,0:T(8,128)S(1)}, f32[768,512]{1,0:T(8,128)}, u32[]{:S(2)}) copy-start(f32[768,512]{1,0:T(8,128)} %copy-done.2) | copy-start | bytes 4718596
  717.9 12.7 %copy-start.37 = (bf16[512,512]{1,0:T(8,128)(2,1)S(1)}, bf16[512,512]{1,0:T(8,128)(2,1)}, u32[]{:S(2)}) copy-start(bf16[512,512]{1,0:T(8,128)(2,1)} %param.32) | copy-start | bytes 1572868
  717.9 12.7 %copy-start.43 = (f32[768]{0:T(1024)S(1)}, f32[768]{0:T(1024)}, u32[]{:S(2)}) copy-start(f32[768]{0:T(1024)} %copy-done.42) | copy-start | bytes 9220
  717.9 12.7 %copy-start.45 = (f32[768]{0:T(1024)S(1)}, f32[768]{0:T(1024)}, u32[]{:S(2)}) copy-start(f32[768]{0:T(1024)} %copy-done.44) | copy-start | bytes 9220
  717.9 12.7 %copy-start.52 = (f32[512]{0:T(512)S(1)}, f32[512]{0:T(512)}, u32[]{:S(2)}) copy-start(f32[512]{0:T(512)} %param.27) | copy-start | bytes 6148
  727.2 3.3 copy-start.20
  727.2 3.4 copy-start.21
  731.8 1.6 copy-start.49
  734.8 1.7 copy-start.7
  734.8 1.7 copy-start.63
  736.5 5.3 copy-start.53
  736.5 5.3 copy-start.54
  736.5 5.3 copy-start.56
  736.5 5.3 copy-start.57
  976.6 6.3 copy-start.33
  976.6 7.3 copy-start.32
  978.2 6.6 copy-start.23
  984.8 3.7 copy-start.22
  984.8 5.7 copy-start.1
  (6 other events, 7.4 us)
Sparse Core Ops, SparseCore 0:
  14.2 30.5 all-gather.4
  46.9 27.9 all-gather.2
  638.2 43.3 reduce-scatter.2
  683.8 43.3 reduce-scatter.4
  735.2 241.3 all-reduce.3
where the time goes:
time: 1000 us; the launch traced here: 999 us
  other arithmetic  390 us (39%)
  matrix products  264 us (26%)
  waiting for transfers between devices  199 us (20%)
  blocking collectives  84.8 us (8%)
  local copies, waits for them, and re-layouts  42.8 us (4%)
  between operations  17.3 us (2%)
    sub x1, other arithmetic, local(): probs_grad - jnp.sum(probs_soft * probs_grad, axis=-1, keepdims=True)  300 us
    psum x1, waiting for transfers between devices, local(): lax.psum((g_type_table, g_ln1_gain, g_ln1_shift, g_w_query, g_b_query, g_...  192 us
    psum x2, blocking collectives, local(): pair_total, pen_total = lax.psum((local_count, local_pen), ('slot', 'blk'))  84.8 us
    reduce_sum x1, other arithmetic, local(): local_pen = jnp.sum(jnp.where(pair_mask, logits * logits, 0.0))  79.5 us
    dot_general x1, matrix products, scores(): jnp.einsum('vniu,vyiu->viny', query_head_split, key_head_split, preferred...  54.3 us
    dot_general x1, matrix products, local(): jnp.einsum('cowi,ciom->cwom', probability_reduced, value_head_split, pref...  36.2 us
    dot_general x1, matrix products, local(): jnp.einsum('vniu,vyiu->viny', gradient_head_rows, backward_head_rows, pre...  35.9 us
    dot_general x1, matrix products, local(): jnp.einsum('eamg,emax->egax', probs_soft.astype(jnp.bfloat16), gradient_h...  35.4 us
  transfers between devices with their start and end apart: 5, of which 2 were waited for; matrix products, arithmetic and copies ran while one was open for 24% of the time, Pallas kernels for 0%

commit v1 on v0

v1 whole, which is shorter than its diff:
```python
import functools

import jax
import jax.numpy as jnp
from jax import lax
from jax.experimental import pallas as pl
from jax.experimental.pallas import tpu as pltpu
from jax.sharding import PartitionSpec as P

EPSILON = 1e-05
HIGHEST = lax.Precision.HIGHEST
F32 = jnp.float32
BF16 = jnp.bfloat16
BIG = 1073741824.0
TN = (((0,), (0,)), ((), ()))
NT = (((1,), (1,)), ((), ()))
NN = (((1,), (0,)), ((), ()))
STEP = 8
PAIR_LIMIT = 6.0
SAFE_LOGIT = 60.0


def dot(left, right, dims):
    return lax.dot_general(left, right, dims, preferred_element_type=F32)


def rounded(values):
    return lax.reduce_precision(values, 8, 7)


def norm_parts(values, gain, shift):
    center = values - jnp.mean(values, axis=-1, keepdims=True)
    inverse = lax.rsqrt(jnp.mean(center * center, axis=-1, keepdims=True) + EPSILON)
    unit_rows = center * inverse
    return (unit_rows * gain + shift, unit_rows, inverse)


def norm_back(upstream, unit_rows, inverse, gain):
    scaled = upstream * gain
    first = jnp.mean(scaled, axis=-1, keepdims=True)
    second = jnp.mean(scaled * unit_rows, axis=-1, keepdims=True)
    grad_in = inverse * (scaled - first - unit_rows * second)
    return (grad_in, jnp.sum(upstream * unit_rows, axis=0), jnp.sum(upstream, axis=0))


def gelu_slope(values):
    cumulative = 0.5 * (1.0 + lax.erf(values * 0.7071067811865476))
    density = jnp.exp(-0.5 * values * values) * 0.3989422804014327
    return cumulative + values * density


def project(left, right):
    return jnp.dot(left, right, preferred_element_type=F32)


def project_back(left, right):
    return jnp.einsum("rd,ed->re", left, right, preferred_element_type=F32)


def weight_grad(left, right):
    return jnp.einsum("rd,re->de", left, right, preferred_element_type=F32)


def forward_body(
    safe, pf, query, key, value, row_ids, col_ids, pair_out, mixed, top, mask, bias, kept
):
    slot = pl.program_id(0)
    group = pl.program_id(1)
    heads = pf.shape[1]

    @pl.when(group == 0)
    def _():
        same = row_ids[0] == col_ids[0]
        mask[...] = jnp.where(same, 1.0, 0.0).astype(BF16)
        bias[...] = jnp.where(same, 0.0, -BIG)

    def logits_of(h):
        logits = dot(query[0, h], key[0, h], TN) + pf[0, h].astype(F32)
        pair_out[0, h] = logits.astype(BF16)
        return logits

    def weigh(h, spot):
        mixed[0, h] = dot(value[0, h], kept[spot], NT)

    is_safe = safe[slot] == 1

    @pl.when(is_safe)
    def _():
        top[...] = jnp.zeros_like(top)

        def block(i, carry):
            for u in range(STEP):
                h = i * STEP + u
                kept[u % 2] = jnp.exp(logits_of(h)).astype(BF16) * mask[...]
                weigh(jnp.maximum(h - 1, 0), (u + 1) % 2)
            return carry

        lax.fori_loop(0, heads // STEP, block, 0)
        weigh(heads - 1, 1)

    @pl.when(jnp.logical_not(is_safe))
    def _():
        def block(i, carry):
            for u in range(STEP):
                h = i * STEP + u
                masked = logits_of(h) + bias[...]
                highest = jnp.max(masked, axis=1, keepdims=True)
                top[0, i, :, u : u + 1] = highest
                kept[0] = jnp.exp(masked - highest).astype(BF16)
                weigh(h, 0)
            return carry

        lax.fori_loop(0, heads // STEP, block, 0)


def attend(safe, pf, query, key, value, row_ids, col_ids, per_step):
    slots, heads, rows, cols = pf.shape

    def by_head(height, width):
        return pl.BlockSpec((1, per_step, height, width), lambda s, g: (s, g, 0, 0))

    return pl.pallas_call(
        forward_body,
        grid=(slots, heads // per_step),
        in_specs=[
            pl.BlockSpec(memory_space=pltpu.SMEM),
            by_head(rows, cols),
            by_head(16, rows),
            by_head(16, cols),
            by_head(16, cols),
            pl.BlockSpec((1, rows, 1), lambda s, g: (s, 0, 0)),
            pl.BlockSpec((1, 1, cols), lambda s, g: (s, 0, 0)),
        ],
        out_specs=[
            by_head(rows, cols),
            by_head(16, rows),
            pl.BlockSpec((1, per_step // STEP, rows, STEP), lambda s, g: (s, g, 0, 0)),
        ],
        out_shape=[
            jax.ShapeDtypeStruct((slots, heads, rows, cols), BF16),
            jax.ShapeDtypeStruct((slots, heads, 16, rows), F32),
            jax.ShapeDtypeStruct((slots, heads // STEP, rows, STEP), F32),
        ],
        scratch_shapes=[
            pltpu.VMEM((rows, cols), BF16),
            pltpu.VMEM((rows, cols), F32),
            pltpu.VMEM((2, rows, cols), BF16),
        ],
        compiler_params=pltpu.CompilerParams(vmem_limit_bytes=56 << 20),
        name="attend",
    )(safe, pf, query, key, value, row_ids, col_ids)


def backward_body(
    scale,
    pf,
    cotan,
    query,
    key,
    grad,
    value,
    query_mask,
    key_mask,
    log_total,
    row_ids,
    col_ids,
    held,
    pair_grad,
    query_grad,
    key_grad,
    value_grad,
    penalty,
    weight,
    probs,
):
    slot = pl.program_id(0)
    group = pl.program_id(1)
    heads = pf.shape[1]
    rows, cols = pf.shape[2:]

    @pl.when(group == 0)
    def _():
        weight[...] = jnp.where(row_ids[0] == col_ids[0], scale[0], 0.0).astype(BF16)

    @pl.when((group == 0) & (slot == 0))
    def _():
        penalty[...] = jnp.zeros_like(penalty)

    def pairs(i, u):
        h = i * STEP + u
        left = jnp.concatenate([query[0, h], query_mask[0]], 0)
        right = jnp.concatenate([key[0, h], key_mask[0]], 0)
        logits = dot(left, right, TN) + pf[0, h].astype(F32)
        probs_grad = dot(grad[0, h], value[0, h], TN).astype(BF16)
        prob = jnp.exp(logits - log_total[0, i, :, u : u + 1]).astype(BF16)
        probs[u % 2] = prob
        logits_low = logits.astype(BF16)
        pen_grad = logits_low * weight[...]
        pair_grad[0, h] = prob * probs_grad + (cotan[0, h] + pen_grad)
        squares = (pen_grad * logits_low).reshape(rows // 64, 4, 16, cols)
        penalty[...] += jnp.sum(jnp.sum(squares, axis=1).astype(F32), axis=0)

    def sums(h, spot):
        upper = dot(query[0, h], pair_grad[0, h], NN)
        key_grad[0, h] = upper[:8] + upper[8:]
        value_grad[0, h] = dot(grad[0, h], probs[spot], NN)[:8]
        query_grad[0, h] = dot(key[0, h], pair_grad[0, h], NT)[:8]

    def block(i, carry):
        for u in range(STEP):
            pairs(i, u)
            sums(jnp.maximum(i * STEP + u - 1, 0), (u + 1) % 2)
        return carry

    lax.fori_loop(0, heads // STEP, block, 0)
    sums(heads - 1, 1)


def attend_back(
    scale,
    pf,
    cotan,
    query,
    key,
    grad,
    value,
    query_mask,
    key_mask,
    log_total,
    row_ids,
    col_ids,
    held,
    first,
    count,
    per_step,
):
    slots, heads, rows, cols = pf.shape
    start = first // per_step

    def by_head(height, width):
        return pl.BlockSpec((1, per_step, height, width), lambda s, g: (s, g + start, 0, 0))

    def part(height, width):
        return pl.BlockSpec((1, per_step, height, width), lambda s, g: (s, g, 0, 0))

    def by_slot(height, width):
        return pl.BlockSpec((1, height, width), lambda s, g: (s, 0, 0))

    operands = [
        scale,
        pf,
        cotan,
        query,
        key,
        grad,
        value,
        query_mask,
        key_mask,
        log_total,
        row_ids,
        col_ids,
    ]
    in_specs = [
        pl.BlockSpec(memory_space=pltpu.SMEM),
        by_head(rows, cols),
        by_head(rows, cols),
        by_head(16, rows),
        by_head(16, cols),
        by_head(16, rows),
        by_head(16, cols),
        by_slot(16, rows),
        by_slot(16, cols),
        pl.BlockSpec((1, per_step // STEP, rows, STEP), lambda s, g: (s, g + start, 0, 0)),
        by_slot(rows, 1),
        by_slot(1, cols),
    ]
    body = backward_body
    aliases = {}
    if held is None:

        def body(*refs):
            backward_body(*refs[:12], None, *refs[12:])

    else:
        operands.append(held)
        in_specs.append(pl.BlockSpec(memory_space=pl.ANY))
        aliases = {12: 0}
    return pl.pallas_call(
        body,
        grid=(slots, count // per_step),
        in_specs=in_specs,
        out_specs=[
            by_head(rows, cols),
            part(8, rows),
            part(8, cols),
            part(8, cols),
            pl.BlockSpec((16, cols), lambda s, g: (0, 0)),
        ],
        out_shape=[
            jax.ShapeDtypeStruct((slots, heads, rows, cols), BF16),
            jax.ShapeDtypeStruct((slots, count, 8, rows), F32),
            jax.ShapeDtypeStruct((slots, count, 8, cols), F32),
            jax.ShapeDtypeStruct((slots, count, 8, cols), F32),
            jax.ShapeDtypeStruct((16, cols), F32),
        ],
        scratch_shapes=[
            pltpu.VMEM((rows, cols), BF16),
            pltpu.VMEM((2, rows, cols), BF16),
        ],
        input_output_aliases=aliases,
        compiler_params=pltpu.CompilerParams(vmem_limit_bytes=56 << 20),
        name="attend_back",
    )(*operands)


def flips(sizes):
    found = []
    for axis in ("slot", "blk"):
        bit = 1
        while bit < sizes[axis]:
            found.append((axis, bit))
            bit *= 2
    return found


def swap(values, sizes, axis, bit):
    return lax.ppermute(values, axis, [(i, i ^ bit) for i in range(sizes[axis])])


def butterfly(values, sizes, axes=("slot", "blk")):
    for axis, bit in flips(sizes):
        if axis in axes:
            values = values + swap(values, sizes, axis, bit)
    return values


def step_plan(sizes):
    whole = sizes["slot"] * sizes["blk"]
    blk = sizes["blk"]
    slot_at = lax.axis_index("slot")
    blk_at = lax.axis_index("blk")

    def partner(device, axis, bit):
        s, b = divmod(device, blk)
        return (s ^ bit) * blk + b if axis == "slot" else s * blk + (b ^ bit)

    def bit_of(axis, bit):
        return ((slot_at if axis == "slot" else blk_at) // bit) % 2

    def plain(axis, bit):
        return ([(d, partner(d, axis, bit)) for d in range(whole)], bit_of(axis, bit))

    def mixed(even, odd):
        pairs = [(d, partner(d, *(even if (d // blk) % 2 == 0 else odd))) for d in range(whole)]
        return (pairs, jnp.where(slot_at % 2 == 0, bit_of(*even), bit_of(*odd)))

    steps = flips(sizes)
    core, rest = steps[0], steps[1:]
    near_y, near_x = ("slot", 2), ("blk", 1)
    plan = [plain(*core)]
    if near_y in rest and near_x in rest:
        rest = [step for step in rest if step not in (near_y, near_x)]
        plan += [mixed(near_x, near_y), mixed(near_y, near_x)]
    return plan + [plain(*step) for step in rest]


def sum_all(values, plan):
    joint = ("slot", "blk")
    for pairs, half in plan:
        halves = values.reshape((2, values.shape[0] // 2) + values.shape[1:])
        away = lax.dynamic_index_in_dim(halves, 1 - half, 0, keepdims=False).astype(BF16)
        mine = lax.dynamic_index_in_dim(halves, half, 0, keepdims=False).astype(F32)
        values = mine + lax.ppermute(away, joint, pairs).astype(F32)
    values = values.astype(BF16)
    for pairs, half in plan[::-1]:
        came = lax.ppermute(values, joint, pairs)
        values = jnp.where(
            half == 0,
            jnp.concatenate([values, came], 0),
            jnp.concatenate([came, values], 0),
        )
    return values.astype(F32)


def local(
    sizes,
    atom_feats,
    pair_feats,
    type_ids,
    mol_lengths,
    type_table,
    ln1_gain,
    ln1_shift,
    w_query,
    b_query,
    w_key,
    w_value,
    b_value,
    w_out,
    b_out,
    ln2_gain,
    ln2_shift,
    w_up,
    b_up,
    w_down,
    b_down,
    atom_cotan,
    pair_cotan,
):
    slots, rows, width = atom_feats.shape
    heads = pair_feats.shape[1]
    cols = pair_feats.shape[3]
    head_size = width // heads
    scale = head_size ** (-0.5)
    flat = slots * rows
    types = type_table.shape[0]
    mols = mol_lengths.shape[1]
    blk_at = lax.axis_index("blk")
    row_start = blk_at * rows
    plan = step_plan(sizes)

    def own(values, axis=1):
        return lax.dynamic_slice_in_dim(values, row_start, rows, axis)

    if sizes["blk"] == 2:

        def gathered(values):
            came = swap(values, sizes, "blk", 1)
            return jnp.where(
                blk_at == 0,
                jnp.concatenate([values, came], 1),
                jnp.concatenate([came, values], 1),
            )

    else:

        def gathered(values):
            return lax.all_gather(values, "blk", axis=1, tiled=True)

    feats = gathered(atom_feats)
    all_types = gathered(type_ids)
    squares = jnp.sum(mol_lengths * mol_lengths).astype(F32)
    pair_total = butterfly(squares.reshape(1, 1), sizes, ("slot",))[0, 0]
    pen_scale = 2.0 / pair_total

    bounds = jnp.cumsum(mol_lengths, axis=1)
    places = jnp.arange(cols, dtype=jnp.int32)
    mol_ids = jnp.sum((places[None, :, None] >= bounds[:, None, :]).astype(jnp.int32), axis=2)
    row_mols = own(mol_ids)
    row_ids = row_mols[:, :, None]
    col_ids = mol_ids[:, None, :]

    def mol_rows(ids):
        return (ids[:, None, :] == jnp.arange(16, dtype=jnp.int32)[None, :, None]).astype(F32)

    query_mask = mol_rows(row_mols).astype(BF16)
    used = (jnp.arange(16) < mols)[None, :, None]
    key_mask = jnp.where(used, -BIG * (1.0 - mol_rows(mol_ids)), 0.0).astype(BF16)

    onehot = (
        all_types.reshape(slots * cols)[:, None] == jnp.arange(types, dtype=jnp.int32)[None, :]
    ).astype(F32)
    base_all = feats.reshape(slots * cols, width).astype(F32) + jnp.dot(
        onehot, type_table, precision=HIGHEST
    )
    normed1, unit1, inverse1 = norm_parts(base_all, ln1_gain, ln1_shift)
    normed1_low = normed1.astype(BF16).reshape(slots, cols, width)
    own_normed1 = own(normed1_low)

    def into_heads(weights, normed):
        turned = jnp.einsum("de,nrd->ner", weights, normed, preferred_element_type=F32)
        return turned

    query = rounded(into_heads(w_query, own_normed1) + b_query[:, None])
    key = rounded(into_heads(w_key, normed1_low)).reshape(slots, heads, head_size, cols)
    value = (into_heads(w_value, normed1_low) + b_value[:, None]).astype(BF16)
    value = value.reshape(slots, heads, head_size, cols)
    query_heads = query.reshape(slots, heads, head_size, rows)
    far_query = jnp.max(jnp.sum(query_heads * query_heads, axis=2), axis=2)
    far_key = jnp.max(jnp.sum(key * key, axis=2), axis=2)
    reach = jnp.max(scale * jnp.sqrt(far_query * far_key), axis=1) + PAIR_LIMIT
    safe = (reach <= SAFE_LOGIT).astype(jnp.int32)
    scaled = query_heads * scale
    upper = rounded(scaled)
    query_rows = jnp.concatenate([upper.astype(BF16), (scaled - upper).astype(BF16)], 2)
    key_low = key.astype(BF16)
    key_rows = jnp.concatenate([key_low, key_low], 2)
    value_rows = jnp.concatenate(
        [
            value,
            jnp.ones((slots, heads, 3, cols), BF16),
            jnp.zeros((slots, heads, 5, cols), BF16),
        ],
        2,
    )

    pair_out, weighed, top = attend(
        safe, pair_feats, query_rows, key_rows, value_rows, row_ids, col_ids, 8
    )
    totals = weighed[:, :, 8]
    mixed_turned = weighed[:, :, :8] / totals[:, :, None]
    mixed_low = (
        jnp.swapaxes(mixed_turned.reshape(slots, width, rows), 1, 2)
        .reshape(flat, width)
        .astype(BF16)
    )
    log_total = top + jnp.swapaxes(
        jnp.log(totals).reshape(slots, heads // STEP, STEP, rows), 2, 3
    )

    base = own(base_all.reshape(slots, cols, width)).reshape(flat, width)
    resid = base + project(mixed_low, w_out) + b_out
    normed2, unit2, inverse2 = norm_parts(resid, ln2_gain, ln2_shift)
    normed2_low = normed2.astype(BF16)
    hidden_pre = project(normed2_low, w_up) + b_up
    hidden_low = jax.nn.gelu(hidden_pre, approximate=False).astype(BF16)
    atom_out = resid + project(hidden_low, w_down) + b_down
    out_grad = atom_cotan.reshape(flat, width)
    g_w_down = weight_grad(hidden_low, out_grad)
    g_b_down = jnp.sum(out_grad.astype(F32), axis=0)
    hidden_grad = project_back(out_grad, w_down) * gelu_slope(hidden_pre)
    hidden_grad_low = hidden_grad.astype(BF16)
    g_w_up = weight_grad(normed2_low, hidden_grad_low)
    g_b_up = jnp.sum(hidden_grad_low.astype(F32), axis=0)
    resid_back, g_ln2_gain, g_ln2_shift = norm_back(
        project_back(hidden_grad_low, w_up), unit2, inverse2, ln2_gain
    )
    resid_grad = out_grad.astype(F32) + resid_back
    resid_grad_low = resid_grad.astype(BF16)
    g_w_out = weight_grad(mixed_low, resid_grad_low)
    g_b_out = jnp.sum(resid_grad_low.astype(F32), axis=0)
    g_w_down, g_w_up, g_w_out = (sum_all(g, plan) for g in (g_w_down, g_w_up, g_w_out))

    mixed_grad = rounded(
        jnp.einsum(
            "de,nre->ndr",
            w_out,
            resid_grad_low.reshape(slots, rows, width),
            preferred_element_type=F32,
        )
    ).reshape(slots, heads, head_size, rows)
    delta = -jnp.sum(mixed_grad * mixed_turned, axis=2)
    first = rounded(delta)
    second = rounded(delta - first)
    third = delta - first - second
    grad_rows = jnp.concatenate(
        [
            mixed_grad.astype(BF16),
            jnp.stack([first, second, third], 2).astype(BF16),
            jnp.zeros((slots, heads, 5, rows), BF16),
        ],
        2,
    )

    pair_grad, query_part, key_part, value_part, pen_tile = attend_back(
        pen_scale.reshape(1),
        pair_feats,
        pair_cotan,
        query_rows,
        key_rows,
        grad_rows,
        value_rows,
        query_mask,
        key_mask,
        log_total,
        row_ids,
        col_ids,
        None,
        0,
        heads,
        8,
    )
    penalty = 0.5 * jnp.sum(pen_tile)

    query_grad = (query_part * scale).astype(BF16).reshape(slots, width, rows)
    key_grad = key_part.astype(BF16).reshape(slots, width, cols)
    value_grad = value_part.astype(BF16).reshape(slots, width, cols)

    def turned_grad(normed, grads):
        return jnp.einsum("nrd,ner->de", normed, grads, preferred_element_type=F32)

    g_w_query = turned_grad(own_normed1, query_grad)
    g_w_key = turned_grad(normed1_low, key_grad)
    g_w_value = turned_grad(normed1_low, value_grad)
    g_b_query = jnp.sum(query_grad.astype(F32), axis=(0, 2))
    g_b_value = jnp.sum(value_part, axis=(0, 3)).reshape(width)
    g_w_query, g_w_key, g_w_value = (sum_all(g, plan) for g in (g_w_query, g_w_key, g_w_value))

    def turned_back(weights, grads):
        return jnp.einsum("de,ner->nrd", weights, grads, preferred_element_type=F32)

    norm_in = turned_back(w_key, key_grad) + turned_back(w_value, value_grad)
    query_in = turned_back(w_query, query_grad)
    norm_in = lax.dynamic_update_slice_in_dim(norm_in, own(norm_in) + query_in, row_start, 1)
    base_back, g_ln1_gain, g_ln1_shift = norm_back(
        norm_in.reshape(slots * cols, width), unit1, inverse1, ln1_gain
    )
    back_parts = base_back.reshape(slots, cols, width)
    resid_rows = resid_grad.reshape(slots, rows, width)
    table_rows = lax.dynamic_update_slice_in_dim(
        back_parts, own(back_parts) + resid_rows, row_start, 1
    )
    g_type_table = jnp.einsum(
        "rt,rd->td", onehot, table_rows.reshape(slots * cols, width), precision=HIGHEST
    )
    if sizes["blk"] == 2:
        away = lax.dynamic_slice_in_dim(back_parts, (1 - blk_at) * rows, rows, 1).astype(BF16)
        base_grad = own(back_parts) + swap(away, sizes, "blk", 1).astype(F32) + resid_rows
    else:
        base_grad = resid_rows + lax.psum_scatter(
            back_parts, "blk", scatter_dimension=1, tiled=True
        )

    small = [
        g_type_table,
        g_ln1_gain,
        g_ln1_shift,
        g_b_query,
        g_b_value,
        g_b_out,
        g_ln2_gain,
        g_ln2_shift,
        g_b_up,
        g_b_down,
    ]
    packed = jnp.concatenate(
        [g.reshape(-1, width) for g in small] + [jnp.full((1, width), penalty)], 0
    )
    packed = butterfly(packed, sizes)
    spread = []
    at = 0
    for g in small:
        high = g.size // width
        spread.append(packed[at : at + high].reshape(g.shape))
        at += high
    penalty = packed[at, 0]
    (
        g_type_table,
        g_ln1_gain,
        g_ln1_shift,
        g_b_query,
        g_b_value,
        g_b_out,
        g_ln2_gain,
        g_ln2_shift,
        g_b_up,
        g_b_down,
    ) = spread
    return (
        atom_out.reshape(slots, rows, width).astype(BF16),
        pair_out,
        penalty,
        base_grad.astype(BF16),
        pair_grad,
        g_type_table,
        g_ln1_gain,
        g_ln1_shift,
        g_w_query,
        g_b_query,
        g_w_key,
        g_w_value,
        g_b_value,
        g_w_out,
        g_b_out,
        g_ln2_gain,
        g_ln2_shift,
        g_w_up,
        g_b_up,
        g_w_down,
        g_b_down,
    )


def solution(mesh):
    atoms = P("slot", "blk", None)
    pairs = P("slot", None, "blk", None)
    sizes = {axis: mesh.shape[axis] for axis in ("slot", "blk")}
    return jax.shard_map(
        functools.partial(local, sizes),
        mesh=mesh,
        in_specs=(atoms, pairs, P("slot", "blk"), P("slot", None))
        + (P(),) * 16
        + (atoms, pairs),
        out_specs=(atoms, pairs, P(), atoms, pairs) + (P(),) * 16,
        check_vma=False,
    )
```

time: 1000 us -> 524 us (0.52)
  other arithmetic: 390 us -> 60.8 us
  matrix products: 264 us -> 76.9 us
  Pallas kernels: 0 us -> 130 us
  waiting for transfers between devices: 199 us -> 80 us
  starting transfers between devices: 0.21 us -> 100 us
  blocking collectives: 84.8 us -> 0 us
  local copies, waits for them, and re-layouts: 42.8 us -> 62 us
  between operations: 17.3 us -> 5.97 us
    sub x1 -> x0, other arithmetic: 300 us -> none  [local(): probs_grad - jnp.sum(probs_soft * probs_grad, axis=-1, keepdims=True)]
    psum x1 -> x0, waiting for transfers between devices: 192 us -> none  [local(): lax.psum((g_type_table, g_ln1_gain, g_ln1_shift, g_w_query, g_b_query, g_...]
    dot_general x25 -> x19, matrix products: 262 us -> 75.1 us  [the longest x3 33.2 us: project(): return jnp.dot(left, right, preferred_element_type=F32)]
    pallas_call x0 -> x2, Pallas kernels: none -> 130 us  [the longest x1 72.7 us: attend_back(): pl.pallas_call(body, grid=(slots, count // per_step), in_specs=in_specs,...]
    ppermute x0 -> x72, starting transfers between devices: none -> 100 us  [the longest x30 40.5 us: sum_all(): values = mine + lax.ppermute(away, joint, pairs).astype(F32)]
    psum x2 -> x0, blocking collectives: 84.8 us -> none  [local(): pair_total, pen_total = lax.psum((local_count, local_pen), ('slot', 'blk'))]
    ppermute x0 -> x72, waiting for transfers between devices: none -> 80 us  [the longest x30 49.1 us: sum_all(): values = mine + lax.ppermute(away, joint, pairs).astype(F32)]
    reduce_sum x5 -> x10, other arithmetic: 83.7 us -> 14.3 us  [the longest x1 2.12 us: local(): delta = -jnp.sum(mixed_grad * mixed_turned, axis=2)]
  transfers between devices with their start and end apart: 5 -> 72, of which waited for: 2 -> 44; matrix products, arithmetic and copies ran while one was open for 24% -> 11% of each run, Pallas kernels for 0% -> 0%
where the time goes in v1:
time: 524 us; the launch traced here: 515 us
  Pallas kernels  130 us (25%)
  starting transfers between devices  100 us (19%)
  waiting for transfers between devices  80 us (15%)
  matrix products  76.9 us (15%)
  local copies, waits for them, and re-layouts  62 us (12%)
  other arithmetic  60.8 us (12%)
  between operations  5.97 us (1%)
    pallas_call x1, Pallas kernels, attend_back(): pl.pallas_call(body, grid=(slots, count // per_step), in_specs=in_specs,...  72.7 us
    pallas_call x1, Pallas kernels, attend(): pl.pallas_call(forward_body, grid=(slots, heads // per_step), in_specs=[p...  56.9 us
    ppermute x30, waiting for transfers between devices, sum_all(): values = mine + lax.ppermute(away, joint, pairs).astype(F32)  49.1 us
    ppermute x30, starting transfers between devices, sum_all(): values = mine + lax.ppermute(away, joint, pairs).astype(F32)  40.5 us
    ppermute x30, starting transfers between devices, sum_all(): came = lax.ppermute(values, joint, pairs)  37.4 us
    dot_general x3, matrix products, project(): return jnp.dot(left, right, preferred_element_type=F32)  33.2 us
    ppermute x12, starting transfers between devices, swap(): lax.ppermute(values, axis, [(i, i ^ bit) for i in range(sizes[axis])])  22 us
    ppermute x30, waiting for transfers between devices, sum_all(): came = lax.ppermute(values, joint, pairs)  16.1 us
  transfers between devices with their start and end apart: 72, of which 44 were waited for; matrix products, arithmetic and copies ran while one was open for 11% of the time, Pallas kernels for 0%

profile of v1, /device:TPU:0, one launch (start us, length us, event | category | flops | bytes accessed | tf_op | source)
XLA Modules:
  0.0 515.4 jit_solution(11286762693261130037)
XLA Ops:
  0.7 3.0 collective-permute-start.1
  13.2 3.3 collective-permute-start.3
  17.5 3.4 collective-permute-start.4
  21.8 4.4 collective-permute-start.5
  27.9 2.0 maximum_select_fusion.2
  35.6 2.3 multiply_bitcast_fusion
  37.8 3.1 copy.88
  42.7 4.6 bitcast_reduce_fusion
  48.2 3.0 copy.90
  56.7 3.3 pad_maximum_fusion
  60.1 56.9 %attend.1 = (bf16[3,64,256,512]{3,2,1,0:T(8,128)(2,1)}, f32[3,64,16,256]{3,2,1,0:T(8,128)}, f32[3,8,256,8]{3,2,1,0:T(8,128)}) custom-call(s32[3]{0:T(128)} %compare_convert_fusion.safe, bf16[3,64,256,512]{3,2,1,0:T(8,128)(2,1)} %refs_1_.1, bf16[3,64,16,256]{3,2,1,0:T(8,128)(2,1)} %pad_maximum_fusion.1.query.refs_3_, ...), custom_call_target="tpu_custom_call" | custom-call | tf_op jit(solution)/shard_map/attend/pallas_call | solution.py:122
  117.0 2.4 slice_log_fusion
  120.1 2.6 convert_bitcast_fusion
  127.1 16.4 %fusion.11 = (bf16[2048,768]{0,1:T(8,128)(2,1)}, f32[768,2048]{1,0:T(8,128)S(1)}) fusion(f32[2048]{0:T(1024)S(1)} %copy-done.62, bf16[512,2048]{1,0:T(8,128)(2,1)S(1)} %copy-done, f32[768,512]{1,0:T(8,128)S(1)} %get-tuple-element.72, f32[512]{0:T(512)S(1)} %copy-done.49, f32[512]{0:T(512)S(1)} %copy-done.47, f32[768]{0:T(1024)S(1)} %add_rsqrt_fusion.1, ...), kind=kOutput, calls=%fused_computation.14 | convolution fusion | flops 1716387840 | bytes 13125632 | tf_op jit(solution)/shard_map/dot_general | solution.py:53
  143.5 4.3 convert_reduce_fusion
  147.8 2.8 multiply_reduce_fusion.3
  150.6 1.9 convert_reduce_fusion.2
  155.2 1.9 copy.94
  157.2 2.1 fusion.46
  159.8 2.2 copy.95
  162.0 5.0 bitcast_add_fusion.refs_9_
  167.0 4.9 concatenate.215.refs_5_
  171.9 72.7 %attend_back.1 = (bf16[3,64,256,512]{3,2,1,0:T(8,128)(2,1)}, f32[3,64,8,256]{3,2,1,0:T(8,128)}, f32[3,64,8,512]{3,2,1,0:T(8,128)}, f32[3,64,8,512]{3,2,1,0:T(8,128)}, f32[16,512]{1,0:T(8,128)}) custom-call(f32[1]{0:T(128)} %bitcast.23.refs_0_, bf16[3,64,256,512]{3,2,1,0:T(8,128)(2,1)} %refs_1_.1, bf16[3,64,256,512]{3,2,1,0:T(8,128)(2,1)} %refs_2_.1, ...), custom_call_target="tpu_custom_call" | custom-call | tf_op jit(solution)/shard_map/attend_back/pallas_call | solution.py:288
  244.7 3.1 fusion.44
  255.7 4.0 copy.101
  260.9 4.0 fusion.51
  264.9 3.6 fusion.54
  268.5 4.1 fusion.150
  272.6 16.2 %add_convert_fusion.3 = bf16[768,512]{1,0:T(8,128)(2,1)} fusion(f32[768,512]{1,0:T(8,128)S(1)} %copy-done.8, bf16[2048,512]{1,0:T(8,128)(2,1)S(1)} %copy-done.61, f32[768,2048]{1,0:T(8,128)} %copy-done.65, f32[2048]{0:T(1024)S(1)} %copy-done.62, f32[512]{0:T(512)S(1)} %copy-done.64), kind=kOutput, calls=%fused_computation.105 | convolution fusion | flops 1715601408 | bytes 10758144 | tf_op jit(solution)/shard_map/dot_general | solution.py:53
  288.8 3.5 subtract_multiply_fusion
  297.4 2.1 reduce_sum.223
  310.6 4.9 copy.116
  315.5 3.7 fusion.158
  319.2 2.0 copy-done.31
  322.9 2.7 fusion.57
  331.2 1.9 collective-permute-start.23
  341.9 1.9 collective-permute-start.24
  350.4 1.9 collective-permute-start.25
  354.4 1.9 collective-permute-start.45
  356.4 2.8 collective-permute-start.16
  359.2 2.0 collective-permute-start.26
  361.2 2.5 collective-permute-start.36
  363.9 2.1 collective-permute-start.46
  366.0 2.5 collective-permute-start.17
  370.7 2.4 collective-permute-start.37
  375.3 2.0 collective-permute-start.18
  401.1 9.4 %collective-permute-done.53 = bf16[128,2048]{1,0:T(8,128)(2,1)S(1)} collective-permute-done((bf16[128,2048]{1,0:T(8,128)(2,1)S(1)}, bf16[128,2048]{1,0:T(8,128)(2,1)S(1)}, u32[]{:S(2)}, u32[]{:S(2)}) %collective-permute-start.53) | collective-permute-done | bytes 524320 | tf_op jit(solution)/shard_map/ppermute | solution.py:373
  411.7 8.7 %collective-permute-done.63 = bf16[512,512]{1,0:T(8,128)(2,1)S(1)} collective-permute-done((bf16[512,512]{1,0:T(8,128)(2,1)S(1)}, bf16[512,512]{1,0:T(8,128)(2,1)S(1)}, u32[]{:S(2)}, u32[]{:S(2)}) %collective-permute-start.63) | collective-permute-done | bytes 524320 | tf_op jit(solution)/shard_map/ppermute | solution.py:373
  421.9 4.8 collective-permute-done.54
  428.2 4.9 collective-permute-done.64
  434.9 3.2 collective-permute-done.55
  439.8 3.9 collective-permute-done.65
  445.5 3.4 collective-permute-done.56
  450.7 3.4 collective-permute-done.66
  455.9 3.3 collective-permute-done.57
  461.1 2.2 collective-permute-start.58
  466.2 2.0 collective-permute-start.68
  469.7 2.5 add_convert_fusion.2
  482.2 3.1 collective-permute-done.7
  491.6 3.7 collective-permute-done.8
  498.9 3.6 collective-permute-done.9
  505.1 2.1 collective-permute-done.10
  509.6 2.9 fusion.35
  512.5 2.6 fusion.36
  (409 shorter events, 153.3 us)
Async XLA Ops:
  0.7 26.4 %collective-permute-start.1 = (s32[3,256]{1,0:T(4,128)}, s32[3,256]{1,0:T(4,128)S(1)}, u32[]{:S(2)}, u32[]{:S(2)}) collective-permute-start(s32[3,256]{1,0:T(4,128)} %param.24), channel_id=1, source_target_pairs={{0,1},{1,0},{2,3},{3,2},{4,5},{5,4},{6,7},{7,6},{8,9},{9,8},{10,11... | collective-permute-start | bytes 9224 | tf_op jit(solution)/shard_map/ppermute | solution.py:327
  3.7 24.2 %collective-permute-start = (bf16[3,256,512]{2,1,0:T(8,128)(2,1)}, bf16[3,256,512]{2,1,0:T(8,128)(2,1)S(1)}, u32[]{:S(2)}, u32[]{:S(2)}) collective-permute-start(bf16[3,256,512]{2,1,0:T(8,128)(2,1)} %param.22), channel_id=1, source_target_pairs={{0,1},{1,0},{2,3},{3,2},{4,5},{5,4},{6,7},{7,6},{8,9},{9,8},{10,11... | collective-permute-start | bytes 2359304 | tf_op jit(solution)/shard_map/ppermute | solution.py:327
  5.7 6.9 %collective-permute-start.2 = (f32[1,1]{1,0:T(1,128)}, f32[1,1]{1,0:T(1,128)}, u32[]{:S(2)}, u32[]{:S(2)}) collective-permute-start(f32[1,1]{1,0:T(1,128)} %bitcast.22), channel_id=1, source_target_pairs={{0,2},{2,0},{4,6},{6,4},{8,10},{10,8},{12,14},{14,12},{16,18},{18,... | collective-permute-start | bytes 20 | tf_op jit(solution)/shard_map/ppermute | solution.py:327
  21.8 4.7 collective-permute-start.5
  294.9 173.4 %collective-permute-start.11 = (bf16[3,256,512]{2,1,0:T(8,128)(2,1)}, bf16[3,256,512]{2,1,0:T(8,128)(2,1)}, u32[]{:S(2)}, u32[]{:S(2)}) collective-permute-start(bf16[3,256,512]{2,1,0:T(8,128)(2,1)} %dynamic-slice_convert_fusion.2), channel_id=1, source_target_pairs={{0,1},{1,0},{2,3},{3,2},{4,5},{5,4},{6,7},{7,6},{8,9},{9,8},{10,11... | collective-permute-start | bytes 2359304 | tf_op jit(solution)/shard_map/ppermute | solution.py:327
  303.7 23.2 %collective-permute-start.12 = (bf16[256,512]{1,0:T(8,128)(2,1)}, bf16[256,512]{1,0:T(8,128)(2,1)}, u32[]{:S(2)}, u32[]{:S(2)}) collective-permute-start(bf16[256,512]{1,0:T(8,128)(2,1)} %fusion.87), channel_id=1, source_target_pairs={{0,2},{1,3},{2,0},{3,1},{4,6},{5,7},{6,4},{7,5},{8,10},{9,11},{10,... | collective-permute-start | bytes 786440 | tf_op jit(solution)/shard_map/ppermute | solution.py:373
  305.5 22.6 %collective-permute-start.22 = (bf16[256,512]{1,0:T(8,128)(2,1)}, bf16[256,512]{1,0:T(8,128)(2,1)S(1)}, u32[]{:S(2)}, u32[]{:S(2)}) collective-permute-start(bf16[256,512]{1,0:T(8,128)(2,1)} %fusion.88), channel_id=1, source_target_pairs={{0,2},{1,3},{2,0},{3,1},{4,6},{5,7},{6,4},{7,5},{8,10},{9,11},{10,... | collective-permute-start | bytes 786440 | tf_op jit(solution)/shard_map/ppermute | solution.py:373
  307.8 22.0 %collective-permute-start.32 = (bf16[256,512]{1,0:T(8,128)(2,1)}, bf16[256,512]{1,0:T(8,128)(2,1)S(1)}, u32[]{:S(2)}, u32[]{:S(2)}) collective-permute-start(bf16[256,512]{1,0:T(8,128)(2,1)} %fusion.89), channel_id=1, source_target_pairs={{0,2},{1,3},{2,0},{3,1},{4,6},{5,7},{6,4},{7,5},{8,10},{9,11},{10,... | collective-permute-start | bytes 786440 | tf_op jit(solution)/shard_map/ppermute | solution.py:373
  322.4 8.8 %collective-permute-start.42 = (bf16[256,512]{1,0:T(8,128)(2,1)S(1)}, bf16[256,512]{1,0:T(8,128)(2,1)S(1)}, u32[]{:S(2)}, u32[]{:S(2)}) collective-permute-start(bf16[256,512]{1,0:T(8,128)(2,1)S(1)} %fusion.90), channel_id=1, source_target_pairs={{0,2},{1,3},{2,0},{3,1},{4,6},{5,7},{6,4},{7,5},{8,10},{9,11},{10,... | collective-permute-start | bytes 786440 | tf_op jit(solution)/shard_map/ppermute | solution.py:373
  326.9 69.6 %collective-permute-start.52 = (bf16[256,2048]{1,0:T(8,128)(2,1)}, bf16[256,2048]{1,0:T(8,128)(2,1)S(1)}, u32[]{:S(2)}, u32[]{:S(2)}) collective-permute-start(bf16[256,2048]{1,0:T(8,128)(2,1)} %fusion.57), channel_id=1, source_target_pairs={{0,2},{1,3},{2,0},{3,1},{4,6},{5,7},{6,4},{7,5},{8,10},{9,11},{10,... | collective-permute-start | bytes 3145736 | tf_op jit(solution)/shard_map/ppermute | solution.py:373
  328.1 71.5 %collective-permute-start.62 = (bf16[1024,512]{1,0:T(8,128)(2,1)}, bf16[1024,512]{1,0:T(8,128)(2,1)S(1)}, u32[]{:S(2)}, u32[]{:S(2)}) collective-permute-start(bf16[1024,512]{1,0:T(8,128)(2,1)} %fusion.58), channel_id=1, source_target_pairs={{0,2},{1,3},{2,0},{3,1},{4,6},{5,7},{6,4},{7,5},{8,10},{9,11},{10,... | collective-permute-start | bytes 3145736 | tf_op jit(solution)/shard_map/ppermute | solution.py:373
  329.8 5.0 collective-permute-start.13
  331.2 5.0 collective-permute-start.23
  334.8 5.0 collective-permute-start.33
  336.2 5.7 %collective-permute-start.43 = (bf16[128,512]{1,0:T(8,128)(2,1)S(1)}, bf16[128,512]{1,0:T(8,128)(2,1)S(1)}, u32[]{:S(2)}, u32[]{:S(2)}) collective-permute-start(bf16[128,512]{1,0:T(8,128)(2,1)S(1)} %fusion.97), channel_id=1, source_target_pairs={{0,1},{1,0},{2,6},{3,7},{4,5},{5,4},{6,2},{7,3},{8,9},{9,8},{10,14... | collective-permute-start | bytes 393224 | tf_op jit(solution)/shard_map/ppermute | solution.py:373
  339.8 4.3 collective-permute-start.14
  341.9 4.3 collective-permute-start.24
  344.1 4.3 collective-permute-start.34
  346.2 4.3 collective-permute-start.44
  348.3 4.0 collective-permute-start.15
  354.4 4.8 collective-permute-start.45
  356.4 4.8 collective-permute-start.16
  359.2 4.7 collective-permute-start.26
  361.2 4.7 collective-permute-start.36
  363.9 4.9 collective-permute-start.46
  366.0 4.7 collective-permute-start.17
  368.8 4.6 collective-permute-start.27
  370.7 4.6 collective-permute-start.37
  373.4 4.6 collective-permute-start.47
  375.3 4.1 collective-permute-start.18
  383.4 5.0 collective-permute-start.19
  385.9 5.0 collective-permute-start.29
  388.5 5.0 collective-permute-start.39
  390.9 4.3 collective-permute-start.49
  393.5 5.0 collective-permute-start.20
  395.3 65.8 %collective-permute-start.30 = (bf16[128,512]{1,0:T(8,128)(2,1)S(1)}, bf16[128,512]{1,0:T(8,128)(2,1)S(1)}, u32[]{:S(2)}, u32[]{:S(2)}) collective-permute-start(bf16[128,512]{1,0:T(8,128)(2,1)S(1)} %maximum_select_fusion.18), channel_id=1, source_target_pairs={{0,1},{1,0},{2,6},{3,7},{4,5},{5,4},{6,2},{7,3},{8,9},{9,8},{10,14... | collective-permute-start | bytes 393224 | tf_op jit(solution)/shard_map/ppermute | solution.py:376
  396.5 81.4 %collective-permute-start.40 = (bf16[128,512]{1,0:T(8,128)(2,1)S(1)}, bf16[128,512]{1,0:T(8,128)(2,1)S(1)}, u32[]{:S(2)}, u32[]{:S(2)}) collective-permute-start(bf16[128,512]{1,0:T(8,128)(2,1)S(1)} %maximum_select_fusion.19), channel_id=1, source_target_pairs={{0,1},{1,0},{2,6},{3,7},{4,5},{5,4},{6,2},{7,3},{8,9},{9,8},{10,14... | collective-permute-start | bytes 393224 | tf_op jit(solution)/shard_map/ppermute | solution.py:376
  398.5 12.0 %collective-permute-start.53 = (bf16[128,2048]{1,0:T(8,128)(2,1)S(1)}, bf16[128,2048]{1,0:T(8,128)(2,1)S(1)}, u32[]{:S(2)}, u32[]{:S(2)}) collective-permute-start(bf16[128,2048]{1,0:T(8,128)(2,1)S(1)} %fusion.71), channel_id=1, source_target_pairs={{0,1},{1,0},{2,6},{3,7},{4,5},{5,4},{6,2},{7,3},{8,9},{9,8},{10,14... | collective-permute-start | bytes 1572872 | tf_op jit(solution)/shard_map/ppermute | solution.py:373
  399.6 79.9 %collective-permute-start.50 = (bf16[128,512]{1,0:T(8,128)(2,1)S(1)}, bf16[128,512]{1,0:T(8,128)(2,1)}, u32[]{:S(2)}, u32[]{:S(2)}) collective-permute-start(bf16[128,512]{1,0:T(8,128)(2,1)S(1)} %maximum_select_fusion.20), channel_id=1, source_target_pairs={{0,1},{1,0},{2,6},{3,7},{4,5},{5,4},{6,2},{7,3},{8,9},{9,8},{10,14... | collective-permute-start | bytes 393224 | tf_op jit(solution)/shard_map/ppermute | solution.py:376
  410.5 9.9 %collective-permute-start.63 = (bf16[512,512]{1,0:T(8,128)(2,1)S(1)}, bf16[512,512]{1,0:T(8,128)(2,1)S(1)}, u32[]{:S(2)}, u32[]{:S(2)}) collective-permute-start(bf16[512,512]{1,0:T(8,128)(2,1)S(1)} %fusion.72), channel_id=1, source_target_pairs={{0,1},{1,0},{2,6},{3,7},{4,5},{5,4},{6,2},{7,3},{8,9},{9,8},{10,14... | collective-permute-start | bytes 1572872 | tf_op jit(solution)/shard_map/ppermute | solution.py:373
  420.3 6.4 %collective-permute-start.54 = (bf16[64,2048]{1,0:T(8,128)(2,1)S(1)}, bf16[64,2048]{1,0:T(8,128)(2,1)S(1)}, u32[]{:S(2)}, u32[]{:S(2)}) collective-permute-start(bf16[64,2048]{1,0:T(8,128)(2,1)S(1)} %fusion.91), channel_id=1, source_target_pairs={{0,4},{1,5},{2,3},{3,2},{4,0},{5,1},{6,7},{7,6},{8,12},{9,13},{10,... | collective-permute-start | bytes 786440 | tf_op jit(solution)/shard_map/ppermute | solution.py:373
  426.7 6.4 %collective-permute-start.64 = (bf16[256,512]{1,0:T(8,128)(2,1)S(1)}, bf16[256,512]{1,0:T(8,128)(2,1)S(1)}, u32[]{:S(2)}, u32[]{:S(2)}) collective-permute-start(bf16[256,512]{1,0:T(8,128)(2,1)S(1)} %fusion.92), channel_id=1, source_target_pairs={{0,4},{1,5},{2,3},{3,2},{4,0},{5,1},{6,7},{7,6},{8,12},{9,13},{10,... | collective-permute-start | bytes 786440 | tf_op jit(solution)/shard_map/ppermute | solution.py:373
  433.1 5.0 collective-permute-start.55
  438.0 5.7 %collective-permute-start.65 = (bf16[128,512]{1,0:T(8,128)(2,1)S(1)}, bf16[128,512]{1,0:T(8,128)(2,1)S(1)}, u32[]{:S(2)}, u32[]{:S(2)}) collective-permute-start(bf16[128,512]{1,0:T(8,128)(2,1)S(1)} %fusion.99), channel_id=1, source_target_pairs={{0,8},{1,9},{2,10},{3,11},{4,12},{5,13},{6,14},{7,15},{8,0},{9,1},... | collective-permute-start | bytes 393224 | tf_op jit(solution)/shard_map/ppermute | solution.py:373
  443.7 5.2 %collective-permute-start.56 = (bf16[16,2048]{1,0:T(8,128)(2,1)S(1)}, bf16[16,2048]{1,0:T(8,128)(2,1)S(1)}, u32[]{:S(2)}, u32[]{:S(2)}) collective-permute-start(bf16[16,2048]{1,0:T(8,128)(2,1)S(1)} %fusion.106), channel_id=1, source_target_pairs={{0,16},{1,17},{2,18},{3,19},{4,20},{5,21},{6,22},{7,23},{8,24},{9,... | collective-permute-start | bytes 196616 | tf_op jit(solution)/shard_map/ppermute | solution.py:373
  448.9 5.2 %collective-permute-start.66 = (bf16[64,512]{1,0:T(8,128)(2,1)S(1)}, bf16[64,512]{1,0:T(8,128)(2,1)S(1)}, u32[]{:S(2)}, u32[]{:S(2)}) collective-permute-start(bf16[64,512]{1,0:T(8,128)(2,1)S(1)} %fusion.107), channel_id=1, source_target_pairs={{0,16},{1,17},{2,18},{3,19},{4,20},{5,21},{6,22},{7,23},{8,24},{9,... | collective-permute-start | bytes 196616 | tf_op jit(solution)/shard_map/ppermute | solution.py:373
  454.1 5.2 %collective-permute-start.57 = (bf16[16,2048]{1,0:T(8,128)(2,1)S(1)}, bf16[16,2048]{1,0:T(8,128)(2,1)S(1)}, u32[]{:S(2)}, u32[]{:S(2)}) collective-permute-start(bf16[16,2048]{1,0:T(8,128)(2,1)S(1)} %fusion.101), channel_id=1, source_target_pairs={{0,16},{1,17},{2,18},{3,19},{4,20},{5,21},{6,22},{7,23},{8,24},{9,... | collective-permute-start | bytes 196616 | tf_op jit(solution)/shard_map/ppermute | solution.py:376
  459.2 5.2 %collective-permute-start.67 = (bf16[64,512]{1,0:T(8,128)(2,1)S(1)}, bf16[64,512]{1,0:T(8,128)(2,1)S(1)}, u32[]{:S(2)}, u32[]{:S(2)}) collective-permute-start(bf16[64,512]{1,0:T(8,128)(2,1)S(1)} %fusion.100), channel_id=1, source_target_pairs={{0,16},{1,17},{2,18},{3,19},{4,20},{5,21},{6,22},{7,23},{8,24},{9,... | collective-permute-start | bytes 196616 | tf_op jit(solution)/shard_map/ppermute | solution.py:376
  461.1 5.2 %collective-permute-start.58 = (bf16[32,2048]{1,0:T(8,128)(2,1)S(1)}, bf16[32,2048]{1,0:T(8,128)(2,1)S(1)}, u32[]{:S(2)}, u32[]{:S(2)}) collective-permute-start(bf16[32,2048]{1,0:T(8,128)(2,1)S(1)} %maximum_select_fusion.21), channel_id=1, source_target_pairs={{0,8},{1,9},{2,10},{3,11},{4,12},{5,13},{6,14},{7,15},{8,0},{9,1},... | collective-permute-start | bytes 393224 | tf_op jit(solution)/shard_map/ppermute | solution.py:376
  464.4 24.4 %collective-permute-start.21 = (bf16[256,512]{1,0:T(8,128)(2,1)S(1)}, bf16[256,512]{1,0:T(8,128)(2,1)S(1)}, u32[]{:S(2)}, u32[]{:S(2)}) collective-permute-start(bf16[256,512]{1,0:T(8,128)(2,1)S(1)} %maximum_select_fusion.11), channel_id=1, source_target_pairs={{0,2},{1,3},{2,0},{3,1},{4,6},{5,7},{6,4},{7,5},{8,10},{9,11},{10,... | collective-permute-start | bytes 786440 | tf_op jit(solution)/shard_map/ppermute | solution.py:376
  466.2 6.0 %collective-permute-start.68 = (bf16[128,512]{1,0:T(8,128)(2,1)S(1)}, bf16[128,512]{1,0:T(8,128)(2,1)S(1)}, u32[]{:S(2)}, u32[]{:S(2)}) collective-permute-start(bf16[128,512]{1,0:T(8,128)(2,1)S(1)} %maximum_select_fusion.22), channel_id=1, source_target_pairs={{0,8},{1,9},{2,10},{3,11},{4,12},{5,13},{6,14},{7,15},{8,0},{9,1},... | collective-permute-start | bytes 393224 | tf_op jit(solution)/shard_map/ppermute | solution.py:376
  468.3 6.4 %collective-permute-start.59 = (bf16[64,2048]{1,0:T(8,128)(2,1)S(1)}, bf16[64,2048]{1,0:T(8,128)(2,1)S(1)}, u32[]{:S(2)}, u32[]{:S(2)}) collective-permute-start(bf16[64,2048]{1,0:T(8,128)(2,1)S(1)} %maximum_select_fusion.15), channel_id=1, source_target_pairs={{0,4},{1,5},{2,3},{3,2},{4,0},{5,1},{6,7},{7,6},{8,12},{9,13},{10,... | collective-permute-start | bytes 786440 | tf_op jit(solution)/shard_map/ppermute | solution.py:376
  472.4 13.1 %collective-permute-start.69 = (bf16[256,512]{1,0:T(8,128)(2,1)S(1)}, bf16[256,512]{1,0:T(8,128)(2,1)S(1)}, u32[]{:S(2)}, u32[]{:S(2)}) collective-permute-start(bf16[256,512]{1,0:T(8,128)(2,1)S(1)} %maximum_select_fusion.16), channel_id=1, source_target_pairs={{0,4},{1,5},{2,3},{3,2},{4,0},{5,1},{6,7},{7,6},{8,12},{9,13},{10,... | collective-permute-start | bytes 786440 | tf_op jit(solution)/shard_map/ppermute | solution.py:376
  474.9 12.8 %collective-permute-start.60 = (bf16[128,2048]{1,0:T(8,128)(2,1)S(1)}, bf16[128,2048]{1,0:T(8,128)(2,1)S(1)}, u32[]{:S(2)}, u32[]{:S(2)}) collective-permute-start(bf16[128,2048]{1,0:T(8,128)(2,1)S(1)} %maximum_select_fusion.9), channel_id=1, source_target_pairs={{0,1},{1,0},{2,6},{3,7},{4,5},{5,4},{6,2},{7,3},{8,9},{9,8},{10,14... | collective-permute-start | bytes 1572872 | tf_op jit(solution)/shard_map/ppermute | solution.py:376
  479.3 11.0 %collective-permute-start.31 = (bf16[256,512]{1,0:T(8,128)(2,1)S(1)}, bf16[256,512]{1,0:T(8,128)(2,1)S(1)}, u32[]{:S(2)}, u32[]{:S(2)}) collective-permute-start(bf16[256,512]{1,0:T(8,128)(2,1)S(1)} %maximum_select_fusion.12), channel_id=1, source_target_pairs={{0,2},{1,3},{2,0},{3,1},{4,6},{5,7},{6,4},{7,5},{8,10},{9,11},{10,... | collective-permute-start | bytes 786440 | tf_op jit(solution)/shard_map/ppermute | solution.py:376
  479.5 5.8 %collective-permute-start.7 = (f32[45,512]{1,0:T(8,128)S(1)}, f32[45,512]{1,0:T(8,128)S(1)}, u32[]{:S(2)}, u32[]{:S(2)}) collective-permute-start(f32[45,512]{1,0:T(8,128)S(1)} %add.407), channel_id=1, source_target_pairs={{0,4},{2,6},{4,0},{6,2},{8,12},{10,14},{12,8},{14,10},{16,20},{18,... | collective-permute-start | bytes 276488 | tf_op jit(solution)/shard_map/ppermute | solution.py:327
  485.3 12.4 %collective-permute-start.41 = (bf16[256,512]{1,0:T(8,128)(2,1)S(1)}, bf16[256,512]{1,0:T(8,128)(2,1)S(1)}, u32[]{:S(2)}, u32[]{:S(2)}) collective-permute-start(bf16[256,512]{1,0:T(8,128)(2,1)S(1)} %maximum_select_fusion.13), channel_id=1, source_target_pairs={{0,2},{1,3},{2,0},{3,1},{4,6},{5,7},{6,4},{7,5},{8,10},{9,11},{10,... | collective-permute-start | bytes 786440 | tf_op jit(solution)/shard_map/ppermute | solution.py:376
  486.1 17.8 %collective-permute-start.51 = (bf16[256,512]{1,0:T(8,128)(2,1)S(1)}, bf16[256,512]{1,0:T(8,128)(2,1)S(1)}, u32[]{:S(2)}, u32[]{:S(2)}) collective-permute-start(bf16[256,512]{1,0:T(8,128)(2,1)S(1)} %maximum_select_fusion.14), channel_id=1, source_target_pairs={{0,2},{1,3},{2,0},{3,1},{4,6},{5,7},{6,4},{7,5},{8,10},{9,11},{10,... | collective-permute-start | bytes 786440 | tf_op jit(solution)/shard_map/ppermute | solution.py:376
  487.7 9.4 %collective-permute-start.70 = (bf16[512,512]{1,0:T(8,128)(2,1)S(1)}, bf16[512,512]{1,0:T(8,128)(2,1)S(1)}, u32[]{:S(2)}, u32[]{:S(2)}) collective-permute-start(bf16[512,512]{1,0:T(8,128)(2,1)S(1)} %maximum_select_fusion.10), channel_id=1, source_target_pairs={{0,1},{1,0},{2,6},{3,7},{4,5},{5,4},{6,2},{7,3},{8,9},{9,8},{10,14... | collective-permute-start | bytes 1572872 | tf_op jit(solution)/shard_map/ppermute | solution.py:376
  488.9 20.8 %collective-permute-start.61 = (bf16[256,2048]{1,0:T(8,128)(2,1)S(1)}, bf16[256,2048]{1,0:T(8,128)(2,1)S(1)}, u32[]{:S(2)}, u32[]{:S(2)}) collective-permute-start(bf16[256,2048]{1,0:T(8,128)(2,1)S(1)} %maximum_select_fusion.3), channel_id=1, source_target_pairs={{0,2},{1,3},{2,0},{3,1},{4,6},{5,7},{6,4},{7,5},{8,10},{9,11},{10,... | collective-permute-start | bytes 3145736 | tf_op jit(solution)/shard_map/ppermute | solution.py:376
  490.3 5.0 collective-permute-start.8
  495.3 7.2 %collective-permute-start.9 = (f32[45,512]{1,0:T(8,128)S(1)}, f32[45,512]{1,0:T(8,128)S(1)}, u32[]{:S(2)}, u32[]{:S(2)}) collective-permute-start(f32[45,512]{1,0:T(8,128)S(1)} %add.409), channel_id=1, source_target_pairs={{0,16},{2,18},{4,20},{6,22},{8,24},{10,26},{12,28},{14,30},{16,0},... | collective-permute-start | bytes 276488 | tf_op jit(solution)/shard_map/ppermute | solution.py:327
  497.6 14.9 %collective-permute-start.71 = (bf16[1024,512]{1,0:T(8,128)(2,1)S(1)}, bf16[1024,512]{1,0:T(8,128)(2,1)S(1)}, u32[]{:S(2)}, u32[]{:S(2)}) collective-permute-start(bf16[1024,512]{1,0:T(8,128)(2,1)S(1)} %maximum_select_fusion.4), channel_id=1, source_target_pairs={{0,2},{1,3},{2,0},{3,1},{4,6},{5,7},{6,4},{7,5},{8,10},{9,11},{10,... | collective-permute-start | bytes 3145736 | tf_op jit(solution)/shard_map/ppermute | solution.py:376
  502.5 4.7 collective-permute-start.10
  (74 other events, 656.2 us)

commit v2 on v1

v2 whole, which is shorter than its diff:
```python
import functools

import jax
import jax.numpy as jnp
from jax import lax
from jax.experimental import pallas as pl
from jax.experimental.pallas import tpu as pltpu
from jax.sharding import PartitionSpec as P

EPSILON = 1e-05
F32 = jnp.float32
BF16 = jnp.bfloat16
BIG = 1073741824.0
TN = (((0,), (0,)), ((), ()))
NT = (((1,), (1,)), ((), ()))
NN = (((1,), (0,)), ((), ()))
TT = (((0,), (1,)), ((), ()))
STEP = 8
CHUNK = 512
PAIR_LIMIT = 6.0
SAFE_LOGIT = 40.0


def dot(left, right, dims):
    return lax.dot_general(left, right, dims, preferred_element_type=F32)


def rounded(values):
    return lax.reduce_precision(values, 8, 7)


def unit_of(values):
    center = values - jnp.mean(values, axis=-1, keepdims=True)
    inverse = lax.rsqrt(jnp.mean(center * center, axis=-1, keepdims=True) + EPSILON)
    return center * inverse, inverse


def norm_back(upstream, unit, inverse, gain):
    scaled = upstream * gain
    first = jnp.mean(scaled, axis=-1, keepdims=True)
    second = jnp.mean(scaled * unit, axis=-1, keepdims=True)
    return inverse * (scaled - first - unit * second)


def column_sum(values):
    return jnp.sum(values, axis=0, keepdims=True)


def onehot_of(ids, types, copies):
    lane = lax.broadcasted_iota(jnp.int32, (ids.shape[0], types * copies), 1)
    hit = lane == ids
    for i in range(1, copies):
        hit = hit | (lane == ids + i * types)
    return jnp.where(hit, 1.0, 0.0).astype(BF16)


def whole(shape):
    return pl.BlockSpec(shape, lambda *grid: (0,) * len(shape))


def by_slot(*shape):
    return pl.BlockSpec((1,) + shape, lambda s: (s,) + (0,) * len(shape))


def prepare_body(
    start,
    feats,
    types,
    table,
    gain,
    shift,
    w_query,
    b_query,
    w_key,
    w_value,
    b_value,
    base_out,
    normed_out,
    query_out,
    key_out,
    value_out,
    reach,
):
    heads, _, rows = query_out.shape[1:]
    cols, width = feats.shape[1:]
    size = width // heads
    base = feats[0].astype(F32) + dot(
        onehot_of(types[0], table.shape[0] // 3, 3), table[...], NN
    )
    base_out[0] = base
    unit, _ = unit_of(base)
    normed = (unit * gain[...] + shift[...]).astype(BF16)
    normed_out[0] = normed

    def split_heads(values):
        return values.reshape(heads, size, values.shape[1])

    def far(values):
        return jnp.max(jnp.sum(values * values, axis=1), axis=1, keepdims=True)

    key = split_heads(dot(w_key[...], normed, TT).astype(BF16).astype(F32))
    key_out[0] = jnp.concatenate([key, key], 1).astype(BF16)
    value = split_heads(dot(w_value[...], normed, TT) + b_value[...])
    line = lax.broadcasted_iota(jnp.int32, (heads, size, cols), 1)
    value_out[0] = jnp.concatenate([value, jnp.where(line < 3, 1.0, 0.0)], 1).astype(BF16)
    own = normed_out[0, pl.ds(pl.multiple_of(start[0], rows), rows), :]
    query = split_heads((dot(w_query[...], own, TT) + b_query[...]).astype(BF16).astype(F32))
    scaled = query * size ** (-0.5)
    upper = scaled.astype(BF16).astype(F32)
    query_out[0] = jnp.concatenate([upper, scaled - upper], 1).astype(BF16)
    reach[0] = jnp.broadcast_to(jnp.max(far(query) * far(key)), reach.shape[1:])


def prepare(start, feats, types, table, gain, shift, w_query, b_query, w_key, w_value, b_value, heads, rows):
    slots, cols, width = feats.shape
    square = whole((width, width))
    row, column = whole((1, width)), whole((width, 1))
    shapes = [
        ((cols, width), F32),
        ((cols, width), BF16),
        ((heads, 16, rows), BF16),
        ((heads, 16, cols), BF16),
        ((heads, 16, cols), BF16),
        ((8, 128), F32),
    ]
    return pl.pallas_call(
        prepare_body,
        grid=(slots,),
        in_specs=[
            pl.BlockSpec(memory_space=pltpu.SMEM),
            by_slot(cols, width),
            by_slot(cols, 1),
            whole(table.shape),
            row,
            row,
            square,
            column,
            square,
            square,
            column,
        ],
        out_specs=[by_slot(*shape) for shape, _ in shapes],
        out_shape=[jax.ShapeDtypeStruct((slots,) + shape, kind) for shape, kind in shapes],
        compiler_params=pltpu.CompilerParams(vmem_limit_bytes=56 << 20),
        name="prepare",
    )(start, feats, types, table, gain, shift, w_query, b_query, w_key, w_value, b_value)


def feed_body(
    weighed,
    top,
    base,
    cotan,
    w_out,
    b_out,
    gain,
    shift,
    w_up,
    b_up,
    w_down,
    b_down,
    atom_out,
    grad_rows,
    log_total,
    resid_grad_out,
    g_weights,
    g_b_up,
    g_rows,
    total,
):
    slot = pl.program_id(0)
    heads, _, rows = weighed.shape[1:]
    width = base.shape[2]
    size = width // heads
    hidden_width = w_up.shape[1]

    @pl.when(slot == 0)
    def _():
        for ref in (total, g_b_up, g_rows):
            ref[...] = jnp.zeros_like(ref)

    totals = weighed[0, :, size : size + 1, :]
    mixed = weighed[0, :, :size, :] / totals
    logs = jnp.log(totals).reshape(heads, rows)
    for g in range(heads // STEP):
        log_total[0, g] = top[0, g] + logs[g * STEP : (g + 1) * STEP].T
    mixed_low = mixed.reshape(width, rows).astype(BF16)
    resid = base[0] + dot(mixed_low, w_out[...], TN) + b_out[...]
    unit, inverse = unit_of(resid)
    normed = (unit * gain[...] + shift[...]).astype(BF16)
    grad = cotan[0]
    down = jnp.zeros((rows, width), F32)
    back = jnp.zeros((rows, width), F32)
    for at in range(0, hidden_width, CHUNK):
        part = slice(at, at + CHUNK)
        pre = dot(normed, w_up[:, part], NN) + b_up[:, part]
        cumulative = 0.5 * (1.0 + lax.erf(pre * 0.7071067811865476))
        density = jnp.exp(-0.5 * pre * pre) * 0.3989422804014327
        hidden = (pre * cumulative).astype(BF16)
        down += dot(hidden, w_down[part, :], NN)
        total[part, :] += dot(hidden, grad, TN)
        hidden_grad = (
            dot(grad, w_down[part, :], NT) * (cumulative + pre * density)
        ).astype(BF16)
        back += dot(hidden_grad, w_up[:, part], NT)
        total[hidden_width + width + at : hidden_width + 2 * width + at] += dot(
            normed, hidden_grad, TN
        )
        g_b_up[:, part] += column_sum(hidden_grad.astype(F32))
    atom_out[0] = (resid + down + b_down[...]).astype(BF16)
    resid_grad = grad.astype(F32) + norm_back(back, unit, inverse, gain[...])
    resid_grad_out[0] = resid_grad
    low = resid_grad.astype(BF16)
    total[hidden_width : hidden_width + width] += dot(mixed_low, low, NN)
    g_rows[0:1] += column_sum(low.astype(F32))
    g_rows[1:2] += column_sum(back * unit)
    g_rows[2:3] += column_sum(back)
    g_rows[3:4] += column_sum(grad.astype(F32))
    mixed_grad = dot(w_out[...], low, NT).astype(BF16).astype(F32).reshape(heads, size, rows)
    delta = -jnp.sum(mixed_grad * mixed, axis=1, keepdims=True)
    first = delta.astype(BF16).astype(F32)
    second = (delta - first).astype(BF16).astype(F32)
    line = lax.broadcasted_iota(jnp.int32, (heads, size, rows), 1)
    extra = jnp.where(
        line == 0,
        first,
        jnp.where(line == 1, second, jnp.where(line == 2, delta - first - second, 0.0)),
    )
    grad_rows[0] = jnp.concatenate([mixed_grad, extra], 1).astype(BF16)

    @pl.when(slot == pl.num_programs(0) - 1)
    def _():
        g_weights[...] = total[...].astype(BF16)


def feed(weighed, top, base, cotan, w_out, b_out, gain, shift, w_up, b_up, w_down, b_down):
    slots, heads, _, rows = weighed.shape
    width, hidden = w_up.shape
    row = whole((1, width))
    own = [
        ((rows, width), BF16),
        ((heads, 16, rows), BF16),
        ((heads // STEP, rows, STEP), F32),
        ((rows, width), F32),
    ]
    shared = [
        ((2 * hidden + width, width), BF16),
        ((1, hidden), F32),
        ((4, width), F32),
    ]
    return pl.pallas_call(
        feed_body,
        grid=(slots,),
        in_specs=[
            by_slot(heads, 16, rows),
            by_slot(heads // STEP, rows, STEP),
            by_slot(rows, width),
            by_slot(rows, width),
            whole((width, width)),
            row,
            row,
            row,
            whole((width, hidden)),
            whole((1, hidden)),
            whole((hidden, width)),
            row,
        ],
        out_specs=[by_slot(*shape) for shape, _ in own] + [whole(shape) for shape, _ in shared],
        out_shape=[jax.ShapeDtypeStruct((slots,) + shape, kind) for shape, kind in own]
        + [jax.ShapeDtypeStruct(shape, kind) for shape, kind in shared],
        scratch_shapes=[pltpu.VMEM(shared[0][0], F32)],
        compiler_params=pltpu.CompilerParams(vmem_limit_bytes=60 << 20),
        name="feed",
    )(weighed, top, base, cotan, w_out, b_out, gain, shift, w_up, b_up, w_down, b_down)


def finish_body(
    start,
    query_part,
    key_part,
    value_part,
    base,
    normed,
    types,
    resid_grad,
    gain,
    w_query,
    w_key,
    w_value,
    back_out,
    g_weights,
    g_table,
    g_rows,
    g_columns,
    g_turned,
    upstream,
):
    slot = pl.program_id(0)
    rows, width = resid_grad.shape[1:]
    cols = base.shape[1]
    heads, size = query_part.shape[1:3]
    own = pl.ds(pl.multiple_of(start[0], rows), rows)

    @pl.when(slot == 0)
    def _():
        for ref in (g_turned, g_table, g_rows, g_columns):
            ref[...] = jnp.zeros_like(ref)

    query_wide = (query_part[0] * size ** (-0.5)).reshape(width, rows)
    value_wide = value_part[0].reshape(width, cols)
    query_grad = query_wide.astype(BF16)
    key_grad = key_part[0].reshape(width, cols).astype(BF16)
    value_grad = value_wide.astype(BF16)
    g_turned[0] += dot(query_grad, normed[0, own, :], NN)
    g_turned[1] += dot(key_grad, normed[0], NN)
    g_turned[2] += dot(value_grad, normed[0], NN)
    g_columns[0] += jnp.sum(query_grad.astype(F32), axis=1, keepdims=True)
    g_columns[1] += jnp.sum(value_wide, axis=1, keepdims=True)
    upstream[...] = dot(key_grad, w_key[...], TT) + dot(value_grad, w_value[...], TT)
    upstream[own, :] += dot(query_grad, w_query[...], TT)
    unit, inverse = unit_of(base[0])
    received = upstream[...]
    g_rows[0:1] += column_sum(received * unit)
    g_rows[1:2] += column_sum(received)
    upstream[...] = norm_back(received, unit, inverse, gain[...])
    back_out[0] = upstream[...]
    upstream[own, :] += resid_grad[0]
    total = upstream[...]
    upper = total.astype(BF16)
    lower = (total - upper.astype(F32)).astype(BF16)
    onehot = onehot_of(types[0], g_table.shape[0], 1)
    g_table[...] += dot(onehot, upper, TN) + dot(onehot, lower, TN)

    @pl.when(slot == pl.num_programs(0) - 1)
    def _():
        for i in range(3):
            g_weights[i * width : (i + 1) * width] = g_turned[i].T


def finish(
    start,
    query_part,
    key_part,
    value_part,
    base,
    normed,
    types,
    resid_grad,
    gain,
    w_query,
    w_key,
    w_value,
    type_count,
):
    slots, heads, size, rows = query_part.shape
    cols, width = base.shape[1:]
    square = whole((width, width))
    shared = [
        ((3 * width, width), F32),
        ((type_count, width), F32),
        ((2, width), F32),
        ((2, width, 1), F32),
    ]
    return pl.pallas_call(
        finish_body,
        grid=(slots,),
        in_specs=[
            pl.BlockSpec(memory_space=pltpu.SMEM),
            by_slot(heads, size, rows),
            by_slot(heads, size, cols),
            by_slot(heads, size, cols),
            by_slot(cols, width),
            by_slot(cols, width),
            by_slot(cols, 1),
            by_slot(rows, width),
            whole((1, width)),
            square,
            square,
            square,
        ],
        out_specs=[by_slot(cols, width)] + [whole(shape) for shape, _ in shared],
        out_shape=[jax.ShapeDtypeStruct((slots, cols, width), F32)]
        + [jax.ShapeDtypeStruct(shape, kind) for shape, kind in shared],
        scratch_shapes=[pltpu.VMEM((3, width, width), F32), pltpu.VMEM((cols, width), F32)],
        compiler_params=pltpu.CompilerParams(vmem_limit_bytes=56 << 20),
        name="finish",
    )(
        start,
        query_part,
        key_part,
        value_part,
        base,
        normed,
        types,
        resid_grad,
        gain,
        w_query,
        w_key,
        w_value,
    )


def forward_body(
    safe, pf, query, key, value, row_ids, col_ids, mixed, top, mask, bias, kept
):
    slot = pl.program_id(0)
    group = pl.program_id(1)
    heads = pf.shape[1]

    @pl.when(group == 0)
    def _():
        same = row_ids[0] == col_ids[0]
        mask[...] = jnp.where(same, 1.0, 0.0).astype(BF16)
        bias[...] = jnp.where(same, 0.0, -BIG)

    def logits_of(h):
        return dot(query[0, h], key[0, h], TN) + pf[0, h].astype(F32)

    def weigh(h, spot):
        mixed[0, h] = dot(value[0, h], kept[spot], NT)

    is_safe = safe[slot] == 1

    @pl.when(is_safe)
    def _():
        top[...] = jnp.zeros_like(top)

        for h in range(heads):
            kept[h % 2] = jnp.exp(logits_of(h)).astype(BF16) * mask[...]
            if h:
                weigh(h - 1, (h - 1) % 2)
        weigh(heads - 1, (heads - 1) % 2)

    @pl.when(jnp.logical_not(is_safe))
    def _():
        def block(i, carry):
            for u in range(STEP):
                h = i * STEP + u
                masked = logits_of(h) + bias[...]
                highest = jnp.max(masked, axis=1, keepdims=True)
                top[0, i, :, u : u + 1] = highest
                kept[0] = jnp.exp(masked - highest).astype(BF16)
                weigh(h, 0)
            return carry

        lax.fori_loop(0, heads // STEP, block, 0)


def attend(safe, pf, query, key, value, row_ids, col_ids, per_step):
    slots, heads, rows, cols = pf.shape

    def by_head(height, width):
        return pl.BlockSpec((1, per_step, height, width), lambda s, g: (s, g, 0, 0))

    return pl.pallas_call(
        forward_body,
        grid=(slots, heads // per_step),
        in_specs=[
            pl.BlockSpec(memory_space=pltpu.SMEM),
            by_head(rows, cols),
            by_head(16, rows),
            by_head(16, cols),
            by_head(16, cols),
            pl.BlockSpec((1, rows, 1), lambda s, g: (s, 0, 0)),
            pl.BlockSpec((1, 1, cols), lambda s, g: (s, 0, 0)),
        ],
        out_specs=[
            by_head(16, rows),
            pl.BlockSpec((1, per_step // STEP, rows, STEP), lambda s, g: (s, g, 0, 0)),
        ],
        out_shape=[
            jax.ShapeDtypeStruct((slots, heads, 16, rows), F32),
            jax.ShapeDtypeStruct((slots, heads // STEP, rows, STEP), F32),
        ],
        scratch_shapes=[
            pltpu.VMEM((rows, cols), BF16),
            pltpu.VMEM((rows, cols), F32),
            pltpu.VMEM((2, rows, cols), BF16),
        ],
        compiler_params=pltpu.CompilerParams(vmem_limit_bytes=56 << 20),
        name="attend",
    )(safe, pf, query, key, value, row_ids, col_ids)


def backward_body(
    safe,
    scale,
    pf,
    cotan,
    query,
    key,
    grad,
    value,
    log_total,
    row_ids,
    col_ids,
    pair_out,
    pair_grad,
    query_grad,
    key_grad,
    value_grad,
    penalty,
    weight,
    mask,
    bias,
    probs,
):
    slot = pl.program_id(0)
    group = pl.program_id(1)
    heads = pf.shape[1]
    rows, cols = pf.shape[2:]

    @pl.when(group == 0)
    def _():
        same = row_ids[0] == col_ids[0]
        weight[...] = jnp.where(same, scale[0], 0.0).astype(BF16)
        mask[...] = jnp.where(same, 1.0, 0.0).astype(BF16)
        bias[...] = jnp.where(same, 0.0, -BIG)

    @pl.when((group == 0) & (slot == 0))
    def _():
        penalty[...] = jnp.zeros_like(penalty)

    def pairs(i, u, safe):
        h = i * STEP + u
        logits = dot(query[0, h], key[0, h], TN) + pf[0, h].astype(F32)
        logits_low = logits.astype(BF16)
        pair_out[0, h] = logits_low
        probs_grad = dot(grad[0, h], value[0, h], TN).astype(BF16)
        shifted = logits - log_total[0, i, :, u : u + 1]
        if safe:
            prob = jnp.exp(shifted).astype(BF16) * mask[...]
        else:
            prob = jnp.exp(shifted + bias[...]).astype(BF16)
        probs[h % 2] = prob
        pen_grad = logits_low * weight[...]
        pair_grad[0, h] = prob * probs_grad + (cotan[0, h] + pen_grad)
        squares = pen_grad * logits_low
        while squares.shape[0] > 16:
            half = squares.shape[0] // 2
            squares = squares[:half] + squares[half:]
        penalty[...] += squares.astype(F32)

    def sums(h, spot):
        upper = dot(query[0, h], pair_grad[0, h], NN)
        key_grad[0, h] = upper[:8] + upper[8:]
        value_grad[0, h] = dot(grad[0, h], probs[spot], NN)[:8]
        query_grad[0, h] = dot(key[0, h], pair_grad[0, h], NT)[:8]

    is_safe = safe[slot] == 1

    @pl.when(is_safe)
    def _():
        for h in range(heads):
            pairs(h // STEP, h % STEP, True)
            if h:
                sums(h - 1, (h - 1) % 2)
        sums(heads - 1, (heads - 1) % 2)

    @pl.when(jnp.logical_not(is_safe))
    def _():
        for h in range(heads):
            pairs(h // STEP, h % STEP, False)
            sums(h, h % 2)


def attend_back(
    safe, scale, pf, cotan, query, key, grad, value, log_total, row_ids, col_ids, per_step
):
    slots, heads, rows, cols = pf.shape

    def by_head(height, width):
        return pl.BlockSpec((1, per_step, height, width), lambda s, g: (s, g, 0, 0))

    return pl.pallas_call(
        backward_body,
        grid=(slots, heads // per_step),
        in_specs=[
            pl.BlockSpec(memory_space=pltpu.SMEM),
            pl.BlockSpec(memory_space=pltpu.SMEM),
            by_head(rows, cols),
            by_head(rows, cols),
            by_head(16, rows),
            by_head(16, cols),
            by_head(16, rows),
            by_head(16, cols),
            pl.BlockSpec((1, per_step // STEP, rows, STEP), lambda s, g: (s, g, 0, 0)),
            pl.BlockSpec((1, rows, 1), lambda s, g: (s, 0, 0)),
            pl.BlockSpec((1, 1, cols), lambda s, g: (s, 0, 0)),
        ],
        out_specs=[
            by_head(rows, cols),
            by_head(rows, cols),
            by_head(8, rows),
            by_head(8, cols),
            by_head(8, cols),
            pl.BlockSpec((16, cols), lambda s, g: (0, 0)),
        ],
        out_shape=[
            jax.ShapeDtypeStruct((slots, heads, rows, cols), BF16),
            jax.ShapeDtypeStruct((slots, heads, rows, cols), BF16),
            jax.ShapeDtypeStruct((slots, heads, 8, rows), F32),
            jax.ShapeDtypeStruct((slots, heads, 8, cols), F32),
            jax.ShapeDtypeStruct((slots, heads, 8, cols), F32),
            jax.ShapeDtypeStruct((16, cols), F32),
        ],
        scratch_shapes=[
            pltpu.VMEM((rows, cols), BF16),
            pltpu.VMEM((rows, cols), BF16),
            pltpu.VMEM((rows, cols), F32),
            pltpu.VMEM((2, rows, cols), BF16),
        ],
        compiler_params=pltpu.CompilerParams(vmem_limit_bytes=60 << 20),
        name="attend_back",
    )(safe, scale, pf, cotan, query, key, grad, value, log_total, row_ids, col_ids)


def flips(sizes):
    found = []
    for axis in ("slot", "blk"):
        bit = 1
        while bit < sizes[axis]:
            found.append((axis, bit))
            bit *= 2
    return found


def swap(values, sizes, axis, bit):
    return lax.ppermute(values, axis, [(i, i ^ bit) for i in range(sizes[axis])])


def butterfly(values, sizes, axes=("slot", "blk")):
    for axis, bit in flips(sizes):
        if axis in axes:
            values = values + swap(values, sizes, axis, bit)
    return values


def step_plan(sizes):
    whole = sizes["slot"] * sizes["blk"]
    blk = sizes["blk"]
    slot_at = lax.axis_index("slot")
    blk_at = lax.axis_index("blk")

    def partner(device, axis, bit):
        s, b = divmod(device, blk)
        return (s ^ bit) * blk + b if axis == "slot" else s * blk + (b ^ bit)

    def bit_of(axis, bit):
        return ((slot_at if axis == "slot" else blk_at) // bit) % 2

    def plain(axis, bit):
        return ([(d, partner(d, axis, bit)) for d in range(whole)], bit_of(axis, bit))

    def mixed(even, odd):
        pairs = [(d, partner(d, *(even if (d // blk) % 2 == 0 else odd))) for d in range(whole)]
        return (pairs, jnp.where(slot_at % 2 == 0, bit_of(*even), bit_of(*odd)))

    steps = flips(sizes)
    core, rest = steps[0], steps[1:]
    near_y, near_x = ("slot", 2), ("blk", 1)
    plan = [plain(*core)]
    if near_y in rest and near_x in rest:
        rest = [step for step in rest if step not in (near_y, near_x)]
        plan += [mixed(near_x, near_y), mixed(near_y, near_x)]
    return plan + [plain(*step) for step in rest]


def sum_all(wide, small, plan):
    joint = ("slot", "blk")
    rows, extra = wide.shape[1], small.shape[1]

    def parcel(wide, small):
        upper = rounded(small)
        parts = [wide.astype(BF16), upper.astype(BF16), (small - upper).astype(BF16)]
        return jnp.concatenate(parts, 1)

    def unpack(values):
        values = values.astype(F32)
        return values[:, :rows], values[:, rows : rows + extra] + values[:, rows + extra :]

    def pick(values, half):
        halves = values.reshape((2, values.shape[0] // 2) + values.shape[1:])
        return lax.dynamic_index_in_dim(halves, half, 0, keepdims=False)

    for pairs, half in plan:
        away = parcel(pick(wide, 1 - half), pick(small, 1 - half))
        came_wide, came_small = unpack(lax.ppermute(away, joint, pairs))
        wide = pick(wide, half) + came_wide
        small = pick(small, half) + came_small
    values = parcel(wide, small)
    for pairs, half in plan[::-1]:
        came = lax.ppermute(values, joint, pairs)
        values = jnp.where(
            half == 0,
            jnp.concatenate([values, came], 0),
            jnp.concatenate([came, values], 0),
        )
    return unpack(values)


def sum_wide(values, sizes):
    joint = ("slot", "blk")
    count = sizes["slot"] * sizes["blk"]
    terms = lax.all_to_all(values, joint, 0, 0, tiled=True)
    terms = terms.reshape((count, values.shape[0] // count, values.shape[1]))
    return lax.all_gather(jnp.sum(terms.astype(F32), axis=0).astype(BF16), joint, tiled=True)


def local(
    sizes,
    atom_feats,
    pair_feats,
    type_ids,
    mol_lengths,
    type_table,
    ln1_gain,
    ln1_shift,
    w_query,
    b_query,
    w_key,
    w_value,
    b_value,
    w_out,
    b_out,
    ln2_gain,
    ln2_shift,
    w_up,
    b_up,
    w_down,
    b_down,
    atom_cotan,
    pair_cotan,
):
    slots, rows, width = atom_feats.shape
    heads = pair_feats.shape[1]
    cols = pair_feats.shape[3]
    types = type_table.shape[0]
    blk_at = lax.axis_index("blk")
    row_start = blk_at * rows
    plan = step_plan(sizes)

    def own(values, axis=1):
        return lax.dynamic_slice_in_dim(values, row_start, rows, axis)

    if sizes["blk"] == 2:

        def gathered(values):
            came = swap(values, sizes, "blk", 1)
            return jnp.where(
                blk_at == 0,
                jnp.concatenate([values, came], 1),
                jnp.concatenate([came, values], 1),
            )

    else:

        def gathered(values):
            return lax.all_gather(values, "blk", axis=1, tiled=True)

    feats = gathered(atom_feats)
    all_types = gathered(type_ids)
    squares = jnp.sum(mol_lengths * mol_lengths).astype(F32)
    pair_total = butterfly(squares.reshape(1, 1), sizes, ("slot",))[0, 0]
    pen_scale = 2.0 / pair_total
    feats, pen_scale = lax.optimization_barrier((feats, pen_scale))

    bounds = jnp.cumsum(mol_lengths, axis=1)
    places = jnp.arange(cols, dtype=jnp.int32)
    mol_ids = jnp.sum((places[None, :, None] >= bounds[:, None, :]).astype(jnp.int32), axis=2)
    row_mols = own(mol_ids)
    row_ids = row_mols[:, :, None]
    col_ids = mol_ids[:, None, :]

    first = rounded(type_table)
    second = rounded(type_table - first)
    table = jnp.concatenate([first, second, type_table - first - second], 0).astype(BF16)
    types_column = all_types[:, :, None]
    start = row_start.astype(jnp.int32).reshape(1)

    def line(values):
        return values.reshape(1, -1)

    def column(values):
        return values.reshape(-1, 1)

    base, normed, query_rows, key_rows, value_rows, reach = prepare(
        start,
        feats,
        types_column,
        table,
        line(ln1_gain),
        line(ln1_shift),
        w_query,
        column(b_query),
        w_key,
        w_value,
        column(b_value),
        heads,
        rows,
    )
    furthest = (width // heads) ** (-0.5) * jnp.sqrt(reach[:, 0, 0]) + PAIR_LIMIT
    safe = (furthest <= SAFE_LOGIT).astype(jnp.int32)

    weighed, top = attend(
        safe, pair_feats, query_rows, key_rows, value_rows, row_ids, col_ids, 16
    )
    atom_out, grad_rows, log_total, resid_grad, g_feed, g_b_up, feed_rows = feed(
        weighed,
        top,
        own(base),
        atom_cotan,
        w_out,
        line(b_out),
        line(ln2_gain),
        line(ln2_shift),
        w_up,
        line(b_up),
        w_down,
        line(b_down),
    )
    g_feed = sum_wide(g_feed, sizes)

    pair_out, pair_grad, query_part, key_part, value_part, pen_tile = attend_back(
        safe,
        pen_scale.reshape(1),
        pair_feats,
        pair_cotan,
        query_rows,
        key_rows,
        grad_rows,
        value_rows,
        log_total,
        row_ids,
        col_ids,
        16,
    )
    penalty = 0.5 * jnp.sum(pen_tile)

    back, g_weights, g_type_table, norm_rows, bias_columns = finish(
        start,
        query_part,
        key_part,
        value_part,
        base,
        normed,
        types_column,
        resid_grad,
        line(ln1_gain),
        w_query,
        w_key,
        w_value,
        types,
    )
    if sizes["blk"] == 2:
        away = lax.dynamic_slice_in_dim(back, (1 - blk_at) * rows, rows, 1).astype(BF16)
        base_grad = own(back) + swap(away, sizes, "blk", 1).astype(F32) + resid_grad
    else:
        base_grad = resid_grad + lax.psum_scatter(back, "blk", scatter_dimension=1, tiled=True)
    parts = [g_type_table, norm_rows, bias_columns.reshape(2, width), feed_rows]
    parts += [g_b_up.reshape(-1, width), jnp.full((1, width), penalty)]
    used = sum(part.shape[0] for part in parts)
    devices = sizes["slot"] * sizes["blk"]
    parts.append(jnp.zeros((-used % devices, width), F32))
    g_weights, packed = sum_all(
        g_weights.reshape(devices, -1, width),
        jnp.concatenate(parts, 0).reshape(devices, -1, width),
        plan,
    )
    g_weights = g_weights.reshape(3 * width, width)
    packed = packed.reshape(-1, width)[:used]
    at = types
    (
        g_ln1_gain,
        g_ln1_shift,
        g_b_query,
        g_b_value,
        g_b_out,
        g_ln2_gain,
        g_ln2_shift,
        g_b_down,
    ) = (packed[at + i] for i in range(8))
    hidden = w_up.shape[1]
    g_w_up = jnp.concatenate(
        [g_feed[at : at + width] for at in range(hidden + width, 2 * hidden + width, width)], 1
    )
    return (
        atom_out,
        pair_out,
        packed[-1, 0],
        base_grad.astype(BF16),
        pair_grad,
        packed[:types],
        g_ln1_gain,
        g_ln1_shift,
        g_weights[:width],
        g_b_query,
        g_weights[width : 2 * width],
        g_weights[2 * width :],
        g_b_value,
        g_feed[hidden : hidden + width].astype(F32),
        g_b_out,
        g_ln2_gain,
        g_ln2_shift,
        g_w_up.astype(F32),
        packed[at + 8 : used - 1].reshape(-1),
        g_feed[:hidden].astype(F32),
        g_b_down,
    )


def solution(mesh):
    atoms = P("slot", "blk", None)
    pairs = P("slot", None, "blk", None)
    sizes = {axis: mesh.shape[axis] for axis in ("slot", "blk")}
    return jax.shard_map(
        functools.partial(local, sizes),
        mesh=mesh,
        in_specs=(atoms, pairs, P("slot", "blk"), P("slot", None))
        + (P(),) * 16
        + (atoms, pairs),
        out_specs=(atoms, pairs, P(), atoms, pairs) + (P(),) * 16,
        check_vma=False,
    )
```

time: 524 us -> 338 us (0.65)
  matrix products: 76.9 us -> 0 us
  starting transfers between devices: 100 us -> 43.2 us
  local copies, waits for them, and re-layouts: 62 us -> 19.6 us
  Pallas kernels: 130 us -> 170 us
  other arithmetic: 60.8 us -> 29.5 us
  waiting for transfers between devices: 80 us -> 49.9 us
  between operations: 5.97 us -> 19.3 us
    dot_general x20 -> x0, matrix products: 76.9 us -> none  [the longest x3 33.2 us: project(): return jnp.dot(left, right, preferred_element_type=F32)]
    pallas_call x1 -> x4, Pallas kernels: 72.7 us -> 137 us  [the longest x1 86.9 us: attend_back(): pl.pallas_call(backward_body, grid=(slots, heads // per_step), in_specs=[...]
    ppermute x30 -> x5, starting transfers between devices: 40.5 us -> 7.85 us  [sum_all(): came_wide, came_small = unpack(lax.ppermute(away, joint, pairs))]
    ppermute x30 -> x5, waiting for transfers between devices: 49.1 us -> 17 us  [sum_all(): came_wide, came_small = unpack(lax.ppermute(away, joint, pairs))]
    ppermute x30 -> x5, starting transfers between devices: 37.4 us -> 13.9 us  [sum_all(): came = lax.ppermute(values, joint, pairs)]
    pallas_call x1, Pallas kernels: 56.9 us -> 33.5 us  [attend(): pl.pallas_call(forward_body, grid=(slots, heads // per_step), in_specs=[p...]
    unnamed x136 -> x24, local copies, waits for them, and re-layouts: 14.4 us -> 1.22 us
    dot_general x4 -> x0, local copies, waits for them, and re-layouts: 11.8 us -> none  [the longest x2 6.01 us: weight_grad(): return jnp.einsum('rd,re->de', left, right, preferred_element_type=F32)]
  transfers between devices with their start and end apart: 72 -> 19, of which waited for: 44 -> 12; matrix products, arithmetic and copies ran while one was open for 11% -> 10% of each run, Pallas kernels for 0% -> 31%
where the time goes in v2:
time: 338 us; the launch traced here: 332 us
  Pallas kernels  170 us (50%)
  waiting for transfers between devices  49.9 us (15%)
  starting transfers between devices  43.2 us (13%)
  other arithmetic  29.5 us (9%)
  local copies, waits for them, and re-layouts  19.6 us (6%)
  between operations  19.3 us (6%)
    pallas_call x1, Pallas kernels, attend_back(): pl.pallas_call(backward_body, grid=(slots, heads // per_step), in_specs=[...  86.9 us
    pallas_call x1, Pallas kernels, attend(): pl.pallas_call(forward_body, grid=(slots, heads // per_step), in_specs=[p...  33.5 us
    pallas_call x1, Pallas kernels, feed(): pl.pallas_call(feed_body, grid=(slots,), in_specs=[by_slot(heads, 16, row...  25.6 us
    ppermute x5, waiting for transfers between devices, sum_all(): came = lax.ppermute(values, joint, pairs)  24.4 us
    ppermute x5, waiting for transfers between devices, sum_all(): came_wide, came_small = unpack(lax.ppermute(away, joint, pairs))  17 us
    ppermute x7, starting transfers between devices, swap(): lax.ppermute(values, axis, [(i, i ^ bit) for i in range(sizes[axis])])  15.1 us
    pallas_call x1, Pallas kernels, finish(): pl.pallas_call(finish_body, grid=(slots,), in_specs=[pl.BlockSpec(memory_...  14.9 us
    ppermute x5, starting transfers between devices, sum_all(): came = lax.ppermute(values, joint, pairs)  13.9 us
  transfers between devices with their start and end apart: 19, of which 12 were waited for; matrix products, arithmetic and copies ran while one was open for 10% of the time, Pallas kernels for 31%

profile of v2, /device:TPU:0, one launch (start us, length us, event | category | flops | bytes accessed | tf_op | source)
XLA Modules:
  0.0 331.8 jit_solution(10229058179489538502)
XLA Ops:
  7.2 3.0 collective-permute-start
  10.2 1.3 multiply_reduce_fusion
  12.2 0.9 collective-permute-start.1
  13.1 0.9 reduce_window_sum.11
  14.1 0.9 reduce-precision_convert_fusion.2
  15.0 0.6 pad_maximum_fusion.4.table
  15.6 0.6 broadcast_in_dim.16.col_ids
  16.2 0.9 copy.86
  17.1 1.5 copy.90.b_query
  18.6 1.5 copy.91.b_value
  20.1 0.9 copy.92.row_ids
  21.8 3.3 %collective-permute-start.2 = (f32[1,1]{1,0:T(1,128)}, f32[1,1]{1,0:T(1,128)}, u32[]{:S(2)}, u32[]{:S(2)}) collective-permute-start(f32[1,1]{1,0:T(1,128)} %add.158), channel_id=1, source_target_pairs={{0,4},{2,6},{4,0},{6,2},{8,12},{10,14},{12,8},{14,10},{16,20},{18,... | collective-permute-start | bytes 20 | tf_op jit(solution)/shard_map/ppermute | solution.py:629
  26.0 3.4 %collective-permute-start.3 = (f32[1,1]{1,0:T(1,128)}, f32[1,1]{1,0:T(1,128)}, u32[]{:S(2)}, u32[]{:S(2)}) collective-permute-start(f32[1,1]{1,0:T(1,128)} %add.159), channel_id=1, source_target_pairs={{0,8},{2,10},{4,12},{6,14},{8,0},{10,2},{12,4},{14,6},{16,24},{18,... | collective-permute-start | bytes 20 | tf_op jit(solution)/shard_map/ppermute | solution.py:629
  30.3 4.4 %collective-permute-start.4 = (f32[1,1]{1,0:T(1,128)}, f32[1,1]{1,0:T(1,128)}, u32[]{:S(2)}, u32[]{:S(2)}) collective-permute-start(f32[1,1]{1,0:T(1,128)} %add.160), channel_id=1, source_target_pairs={{0,16},{2,18},{4,20},{6,22},{8,24},{10,26},{12,28},{14,30},{16,0},... | collective-permute-start | bytes 20 | tf_op jit(solution)/shard_map/ppermute | solution.py:629
  35.8 1.0 add_select_fusion.types
  36.8 1.7 maximum_select_fusion.1.feats
  38.5 9.3 %prepare.1 = (f32[3,512,512]{2,1,0:T(8,128)}, bf16[3,512,512]{2,1,0:T(8,128)(2,1)}, bf16[3,64,16,256]{3,2,1,0:T(8,128)(2,1)}, bf16[3,64,16,512]{3,2,1,0:T(8,128)...) custom-call(s32[1]{0:T(128)} %bitcast.start, bf16[3,512,512]{2,1,0:T(8,128)(2,1)} %maximum_select_fusion.1.feats, ...), custom_call_target="tpu_custom_call" | custom-call | tf_op jit(solution)/shard_map/prepare/pallas_call | solution.py:126
  47.8 1.4 fusion.21.safe
  49.2 2.7 constant_dynamic-slice_fusion.11.base
  51.9 33.5 %attend.1 = (f32[3,64,16,256]{3,2,1,0:T(8,128)}, f32[3,8,256,8]{3,2,1,0:T(8,128)}) custom-call(s32[3]{0:T(128)} %fusion.21.safe, bf16[3,64,256,512]{3,2,1,0:T(8,128)(2,1)} %pf.3, bf16[3,64,16,256]{3,2,1,0:T(8,128)(2,1)} %get-tuple-element.51.query, bf16[3,64,16,512]{3,2,1,0:T(8,128)(2,1)} %get-tuple-element.52.key, ...), custom_call_target="tpu_custom_call" | custom-call | tf_op jit(solution)/shard_map/attend/pallas_call | solution.py:455
  85.5 25.6 %feed.1 = (bf16[3,256,512]{2,1,0:T(8,128)(2,1)}, bf16[3,64,16,256]{3,2,1,0:T(8,128)(2,1)}, f32[3,8,256,8]{3,2,1,0:T(8,128)}, f32[3,256,512]{2,1,0:T(8,128)}, bf1...) custom-call(f32[3,64,16,256]{3,2,1,0:T(8,128)} %get-tuple-element.54.weighed, ...), custom_call_target="tpu_custom_call" | custom-call | tf_op jit(solution)/shard_map/feed/pallas_call | solution.py:251
  111.1 6.3 %all-to-all-start = ((bf16[32,144,512]{2,1,0:T(8,128)(2,1)}), bf16[32,144,512]{2,1,0:T(8,128)(2,1)}, u32[]{:S(2)}, u32[]{:S(2)}) async-start(bf16[32,144,512]{2,1,0:T(8,128)(2,1)} %bitcast.79), calls=%async_computation | async-start | bytes 9437184 | tf_op jit(solution)/shard_map/all_to_all | solution.py:705
  117.5 86.9 %attend_back.1 = (bf16[3,64,256,512]{3,2,1,0:T(8,128)(2,1)}, bf16[3,64,256,512]{3,2,1,0:T(8,128)(2,1)}, f32[3,64,8,256]{3,2,1,0:T(8,128)}, f32[3,64,8,512]{3,2,1...) custom-call(s32[3]{0:T(128)} %fusion.21.safe, f32[1]{0:T(128)} %bitcast.15.scale, ...), custom_call_target="tpu_custom_call" | custom-call | tf_op jit(solution)/shard_map/attend_back/pallas_call | solution.py:575
  204.4 14.9 %finish.1 = (f32[3,512,512]{2,1,0:T(8,128)}, f32[1536,512]{1,0:T(8,128)}, f32[32,512]{1,0:T(8,128)}, f32[2,512]{1,0:T(2,128)}, f32[2,512,1]{2,1,0:T(8,128)}) custom-call(s32[1]{0:T(128)} %bitcast.start, f32[3,64,8,256]{3,2,1,0:T(8,128)} %get-tuple-element.62.query_part, f32[3,64,8,512]{3,2,1,0:T(8,128)} %get-tuple-element.63.key_part, ...), custom_call_target="tpu_custom_call" | custom-call | tf_op jit(solution)/shard_map/finish/pallas_call | solution.py:364
  219.4 1.6 constant_dynamic-slice_fusion.9
  220.9 0.4 copy.122
  221.6 0.5 broadcast.44
  222.1 0.7 reduce.8
  222.8 0.6 reduce_sum.41
  224.5 1.0 pad_maximum_fusion
  225.7 3.9 %reduce_sum.42 = bf16[144,512]{1,0:T(8,128)(2,1)} reduce(bf16[32,144,512]{2,1,0:T(8,128)(2,1)} %all-to-all-done, bf16[]{:T(256)} %constant.186.clone.1), dimensions={0}, to_apply=%region_4.5 | reduce | flops 2285568 | bytes 4866050 | tf_op jit(solution)/shard_map/reduce_sum | solution.py:707
  229.8 1.4 convert_element_type.123
  231.2 1.0 fusion.1
  232.6 1.7 collective-permute-start.7
  234.4 6.8 %collective-permute-done.7 = bf16[8,52,512]{2,1,0:T(8,128)(2,1)S(1)} collective-permute-done((bf16[8,52,512]{2,1,0:T(8,128)(2,1)S(1)}, bf16[8,52,512]{2,1,0:T(8,128)(2,1)S(1)}, u32[]{:S(2)}, u32[]{:S(2)}) %collective-permute-start.7) | collective-permute-done | bytes 426016 | tf_op jit(solution)/shard_map/ppermute | solution.py:688
  241.3 0.5 slice_add_fusion.1
  241.9 1.7 collective-permute-start.8
  243.6 4.4 %collective-permute-done.8 = bf16[4,52,512]{2,1,0:T(8,128)(2,1)S(1)} collective-permute-done((bf16[4,52,512]{2,1,0:T(8,128)(2,1)S(1)}, bf16[4,52,512]{2,1,0:T(8,128)(2,1)S(1)}, u32[]{:S(2)}, u32[]{:S(2)}) %collective-permute-start.8) | collective-permute-done | bytes 213024 | tf_op jit(solution)/shard_map/ppermute | solution.py:688
  248.2 1.7 collective-permute-start.9
  249.9 3.2 collective-permute-done.9
  253.3 2.6 collective-permute-start.10
  255.8 2.6 collective-permute-done.10
  258.6 3.4 %collective-permute-start.11 = (bf16[1,52,512]{2,1,0:T(8,128)(2,1)S(1)}, bf16[1,52,512]{2,1,0:T(8,128)(2,1)S(1)}, u32[]{:S(2)}, u32[]{:S(2)}) collective-permute-start(bf16[1,52,512]{2,1,0:T(8,128)(2,1)S(1)} %pad_maximum_fusion.6), channel_id=1, source_target_pairs={{0,16},{1,17},{2,18},{3,19},{4,20},{5,21},{6,22},{7,23},{8,24},{9,... | collective-permute-start | bytes 159752 | tf_op jit(solution)/shard_map/ppermute | solution.py:693
  262.0 3.2 collective-permute-done.11
  265.2 5.0 %collective-permute-start.12 = (bf16[2,52,512]{2,1,0:T(8,128)(2,1)S(1)}, bf16[2,52,512]{2,1,0:T(8,128)(2,1)S(1)}, u32[]{:S(2)}, u32[]{:S(2)}) collective-permute-start(bf16[2,52,512]{2,1,0:T(8,128)(2,1)S(1)} %maximum_select_fusion.5), channel_id=1, source_target_pairs={{0,8},{1,9},{2,10},{3,11},{4,12},{5,13},{6,14},{7,15},{8,0},{9,1},... | collective-permute-start | bytes 319496 | tf_op jit(solution)/shard_map/ppermute | solution.py:693
  270.3 2.8 collective-permute-done.12
  273.1 1.7 collective-permute-start.13
  274.7 10.6 %collective-permute-done.13 = bf16[4,52,512]{2,1,0:T(8,128)(2,1)S(1)} collective-permute-done((bf16[4,52,512]{2,1,0:T(8,128)(2,1)S(1)}, bf16[4,52,512]{2,1,0:T(8,128)(2,1)S(1)}, u32[]{:S(2)}, u32[]{:S(2)}) %collective-permute-start.13) | collective-permute-done | bytes 213024 | tf_op jit(solution)/shard_map/ppermute | solution.py:693
  285.4 3.7 %collective-permute-start.14 = (bf16[8,52,512]{2,1,0:T(8,128)(2,1)S(1)}, bf16[8,52,512]{2,1,0:T(8,128)(2,1)S(1)}, u32[]{:S(2)}, u32[]{:S(2)}) collective-permute-start(bf16[8,52,512]{2,1,0:T(8,128)(2,1)S(1)} %maximum_select_fusion.3), channel_id=1, source_target_pairs={{0,1},{1,0},{2,6},{3,7},{4,5},{5,4},{6,2},{7,3},{8,9},{9,8},{10,14... | collective-permute-start | bytes 1277960 | tf_op jit(solution)/shard_map/ppermute | solution.py:693
  289.1 2.4 dynamic-slice_convert_fusion
  291.6 7.8 %collective-permute-done.14 = bf16[8,52,512]{2,1,0:T(8,128)(2,1)S(1)} collective-permute-done((bf16[8,52,512]{2,1,0:T(8,128)(2,1)S(1)}, bf16[8,52,512]{2,1,0:T(8,128)(2,1)S(1)}, u32[]{:S(2)}, u32[]{:S(2)}) %collective-permute-start.14) | collective-permute-done | bytes 426016 | tf_op jit(solution)/shard_map/ppermute | solution.py:693
  299.9 7.9 %collective-permute-done.16 = bf16[3,256,512]{2,1,0:T(8,128)(2,1)S(1)} collective-permute-done((bf16[3,256,512]{2,1,0:T(8,128)(2,1)}, bf16[3,256,512]{2,1,0:T(8,128)(2,1)S(1)}, u32[]{:S(2)}, u32[]{:S(2)}) %collective-permute-start.16) | collective-permute-done | bytes 786464 | tf_op jit(solution)/shard_map/ppermute | solution.py:629
  307.8 1.3 add_convert_fusion
  309.1 0.5 copy.103
  309.6 0.4 fusion
  310.0 0.4 slice.194
  310.7 0.5 slice.190
  311.2 0.7 slice.153
  311.9 0.6 copy.107
  312.5 0.6 fusion.25
  313.1 1.7 fusion.24
  314.8 3.0 fusion.23
  317.8 2.6 maximum_convert_fusion
  320.3 4.2 %slice_convert_fusion = f32[2048,512]{1,0:T(8,128)} fusion(bf16[4608,512]{1,0:T(8,128)(2,1)} %all-gather.2.cloned.1.call-done), kind=kLoop, calls=%fused_computation | loop fusion | flops 1048576 | bytes 6291456 | tf_op jit(solution)/shard_map/convert_element_type | solution.py:907
  (86 shorter events, 3.7 us)
Async XLA Ops:
  7.2 29.6 %copy-start.3 = (bf16[3,256,512]{2,1,0:T(8,128)(2,1)S(1)}, bf16[3,256,512]{2,1,0:T(8,128)(2,1)}, u32[]{:S(2)}) copy-start(bf16[3,256,512]{2,1,0:T(8,128)(2,1)} %param.22) | copy-start | bytes 2359300
  7.2 29.6 %collective-permute-start = (bf16[3,256,512]{2,1,0:T(8,128)(2,1)}, bf16[3,256,512]{2,1,0:T(8,128)(2,1)S(1)}, u32[]{:S(2)}, u32[]{:S(2)}) collective-permute-start(bf16[3,256,512]{2,1,0:T(8,128)(2,1)} %param.22), channel_id=1, source_target_pairs={{0,1},{1,0},{2,3},{3,2},{4,5},{5,4},{6,7},{7,6},{8,9},{9,8},{10,11... | collective-permute-start | bytes 2359304 | tf_op jit(solution)/shard_map/ppermute | solution.py:629
  12.2 8.9 %collective-permute-start.1 = (f32[1,1]{1,0:T(1,128)}, f32[1,1]{1,0:T(1,128)}, u32[]{:S(2)}, u32[]{:S(2)}) collective-permute-start(f32[1,1]{1,0:T(1,128)} %bitcast.1), channel_id=1, source_target_pairs={{0,2},{2,0},{4,6},{6,4},{8,10},{10,8},{12,14},{14,12},{16,18},{18,... | collective-permute-start | bytes 20 | tf_op jit(solution)/shard_map/ppermute | solution.py:629
  13.1 22.5 %collective-permute-start.5 = (s32[3,256]{1,0:T(4,128)}, s32[3,256]{1,0:T(4,128)S(1)}, u32[]{:S(2)}, u32[]{:S(2)}) collective-permute-start(s32[3,256]{1,0:T(4,128)} %param.24), channel_id=1, source_target_pairs={{0,1},{1,0},{2,3},{3,2},{4,5},{5,4},{6,7},{7,6},{8,9},{9,8},{10,11... | collective-permute-start | bytes 9224 | tf_op jit(solution)/shard_map/ppermute | solution.py:629
  21.8 3.6 %collective-permute-start.2 = (f32[1,1]{1,0:T(1,128)}, f32[1,1]{1,0:T(1,128)}, u32[]{:S(2)}, u32[]{:S(2)}) collective-permute-start(f32[1,1]{1,0:T(1,128)} %add.158), channel_id=1, source_target_pairs={{0,4},{2,6},{4,0},{6,2},{8,12},{10,14},{12,8},{14,10},{16,20},{18,... | collective-permute-start | bytes 20 | tf_op jit(solution)/shard_map/ppermute | solution.py:629
  26.0 3.6 %collective-permute-start.3 = (f32[1,1]{1,0:T(1,128)}, f32[1,1]{1,0:T(1,128)}, u32[]{:S(2)}, u32[]{:S(2)}) collective-permute-start(f32[1,1]{1,0:T(1,128)} %add.159), channel_id=1, source_target_pairs={{0,8},{2,10},{4,12},{6,14},{8,0},{10,2},{12,4},{14,6},{16,24},{18,... | collective-permute-start | bytes 20 | tf_op jit(solution)/shard_map/ppermute | solution.py:629
  30.3 4.6 %collective-permute-start.4 = (f32[1,1]{1,0:T(1,128)}, f32[1,1]{1,0:T(1,128)}, u32[]{:S(2)}, u32[]{:S(2)}) collective-permute-start(f32[1,1]{1,0:T(1,128)} %add.160), channel_id=1, source_target_pairs={{0,16},{2,18},{4,20},{6,22},{8,24},{10,26},{12,28},{14,30},{16,0},... | collective-permute-start | bytes 20 | tf_op jit(solution)/shard_map/ppermute | solution.py:629
  111.1 114.6 %all-to-all-start = ((bf16[32,144,512]{2,1,0:T(8,128)(2,1)}), bf16[32,144,512]{2,1,0:T(8,128)(2,1)}, u32[]{:S(2)}, u32[]{:S(2)}) async-start(bf16[32,144,512]{2,1,0:T(8,128)(2,1)} %bitcast.79), calls=%async_computation | async-start | bytes 9437184 | tf_op jit(solution)/shard_map/all_to_all | solution.py:705
  117.4 197.4 %all-gather.2.cloned.1.call-start = ((), (), s32[]{:S(2)}) async-start(), calls=%async_computation.1 | async-start | bytes 4866048 | tf_op jit(solution)/shard_map/all_gather | solution.py:707
  219.3 2.1 copy-start.4
  219.3 2.8 copy-start.8
  219.3 3.5 %copy-start.6 = (f32[16,512]{1,0:T(8,128)S(1)}, f32[16,512]{1,0:T(8,128)}, u32[]{:S(2)}) copy-start(f32[16,512]{1,0:T(8,128)} %get-tuple-element.73) | copy-start | bytes 98308
  219.3 4.8 %copy-start.5 = (f32[32,512]{1,0:T(8,128)S(1)}, f32[32,512]{1,0:T(8,128)}, u32[]{:S(2)}) copy-start(f32[32,512]{1,0:T(8,128)} %get-tuple-element.68) | copy-start | bytes 196612
  219.3 4.8 %copy-start.7 = (f32[4,512]{1,0:T(4,128)S(1)}, f32[4,512]{1,0:T(4,128)}, u32[]{:S(2)}) copy-start(f32[4,512]{1,0:T(4,128)} %get-tuple-element.71) | copy-start | bytes 24580
  219.3 4.8 %copy-start.9 = (f32[2,512]{1,0:T(2,128)S(1)}, f32[2,512]{1,0:T(2,128)}, u32[]{:S(2)}) copy-start(f32[2,512]{1,0:T(2,128)} %get-tuple-element.69) | copy-start | bytes 12292
  225.5 4.1 %copy-start.2 = (f32[1536,512]{1,0:T(8,128)S(1)}, f32[1536,512]{1,0:T(8,128)}, u32[]{:S(2)}) copy-start(f32[1536,512]{1,0:T(8,128)} %get-tuple-element.67) | copy-start | bytes 9437188
  225.5 4.3 %collective-permute-start.6 = (bf16[16,52,512]{2,0,1:T(8,128)(2,1)}, bf16[16,52,512]{2,0,1:T(8,128)(2,1)}, u32[]{:S(2)}, u32[]{:S(2)}) collective-permute-start(bf16[16,52,512]{2,0,1:T(8,128)(2,1)} %pad_maximum_fusion), channel_id=1, source_target_pairs={{0,2},{1,3},{2,0},{3,1},{4,6},{5,7},{6,4},{7,5},{8,10},{9,11},{10,... | collective-permute-start | bytes 2555912 | tf_op jit(solution)/shard_map/ppermute | solution.py:688
  232.6 8.6 %collective-permute-start.7 = (bf16[8,52,512]{2,1,0:T(8,128)(2,1)S(1)}, bf16[8,52,512]{2,1,0:T(8,128)(2,1)S(1)}, u32[]{:S(2)}, u32[]{:S(2)}) collective-permute-start(bf16[8,52,512]{2,1,0:T(8,128)(2,1)S(1)} %pad_maximum_fusion.1), channel_id=1, source_target_pairs={{0,1},{1,0},{2,6},{3,7},{4,5},{5,4},{6,2},{7,3},{8,9},{9,8},{10,14... | collective-permute-start | bytes 1277960 | tf_op jit(solution)/shard_map/ppermute | solution.py:688
  241.9 6.1 %collective-permute-start.8 = (bf16[4,52,512]{2,1,0:T(8,128)(2,1)S(1)}, bf16[4,52,512]{2,1,0:T(8,128)(2,1)S(1)}, u32[]{:S(2)}, u32[]{:S(2)}) collective-permute-start(bf16[4,52,512]{2,1,0:T(8,128)(2,1)S(1)} %pad_maximum_fusion.2), channel_id=1, source_target_pairs={{0,4},{1,5},{2,3},{3,2},{4,0},{5,1},{6,7},{7,6},{8,12},{9,13},{10,... | collective-permute-start | bytes 638984 | tf_op jit(solution)/shard_map/ppermute | solution.py:688
  248.2 4.9 %collective-permute-start.9 = (bf16[2,52,512]{2,1,0:T(8,128)(2,1)S(1)}, bf16[2,52,512]{2,1,0:T(8,128)(2,1)S(1)}, u32[]{:S(2)}, u32[]{:S(2)}) collective-permute-start(bf16[2,52,512]{2,1,0:T(8,128)(2,1)S(1)} %pad_maximum_fusion.3), channel_id=1, source_target_pairs={{0,8},{1,9},{2,10},{3,11},{4,12},{5,13},{6,14},{7,15},{8,0},{9,1},... | collective-permute-start | bytes 319496 | tf_op jit(solution)/shard_map/ppermute | solution.py:688
  253.3 5.2 %collective-permute-start.10 = (bf16[1,52,512]{2,1,0:T(8,128)(2,1)S(1)}, bf16[1,52,512]{2,1,0:T(8,128)(2,1)S(1)}, u32[]{:S(2)}, u32[]{:S(2)}) collective-permute-start(bf16[1,52,512]{2,1,0:T(8,128)(2,1)S(1)} %pad_maximum_fusion.5), channel_id=1, source_target_pairs={{0,16},{1,17},{2,18},{3,19},{4,20},{5,21},{6,22},{7,23},{8,24},{9,... | collective-permute-start | bytes 159752 | tf_op jit(solution)/shard_map/ppermute | solution.py:688
  258.6 6.6 %collective-permute-start.11 = (bf16[1,52,512]{2,1,0:T(8,128)(2,1)S(1)}, bf16[1,52,512]{2,1,0:T(8,128)(2,1)S(1)}, u32[]{:S(2)}, u32[]{:S(2)}) collective-permute-start(bf16[1,52,512]{2,1,0:T(8,128)(2,1)S(1)} %pad_maximum_fusion.6), channel_id=1, source_target_pairs={{0,16},{1,17},{2,18},{3,19},{4,20},{5,21},{6,22},{7,23},{8,24},{9,... | collective-permute-start | bytes 159752 | tf_op jit(solution)/shard_map/ppermute | solution.py:693
  265.2 7.8 %collective-permute-start.12 = (bf16[2,52,512]{2,1,0:T(8,128)(2,1)S(1)}, bf16[2,52,512]{2,1,0:T(8,128)(2,1)S(1)}, u32[]{:S(2)}, u32[]{:S(2)}) collective-permute-start(bf16[2,52,512]{2,1,0:T(8,128)(2,1)S(1)} %maximum_select_fusion.5), channel_id=1, source_target_pairs={{0,8},{1,9},{2,10},{3,11},{4,12},{5,13},{6,14},{7,15},{8,0},{9,1},... | collective-permute-start | bytes 319496 | tf_op jit(solution)/shard_map/ppermute | solution.py:693
  273.1 34.7 %copy-start = (f32[3,256,512]{2,1,0:T(8,128)S(1)}, f32[3,256,512]{2,1,0:T(8,128)}, u32[]{:S(2)}) copy-start(f32[3,256,512]{2,1,0:T(8,128)} %get-tuple-element.66.resid_grad) | copy-start | bytes 4718596
  273.1 12.3 %collective-permute-start.13 = (bf16[4,52,512]{2,1,0:T(8,128)(2,1)S(1)}, bf16[4,52,512]{2,1,0:T(8,128)(2,1)S(1)}, u32[]{:S(2)}, u32[]{:S(2)}) collective-permute-start(bf16[4,52,512]{2,1,0:T(8,128)(2,1)S(1)} %maximum_select_fusion.4), channel_id=1, source_target_pairs={{0,4},{1,5},{2,3},{3,2},{4,0},{5,1},{6,7},{7,6},{8,12},{9,13},{10,... | collective-permute-start | bytes 638984 | tf_op jit(solution)/shard_map/ppermute | solution.py:693
  285.4 13.9 %collective-permute-start.14 = (bf16[8,52,512]{2,1,0:T(8,128)(2,1)S(1)}, bf16[8,52,512]{2,1,0:T(8,128)(2,1)S(1)}, u32[]{:S(2)}, u32[]{:S(2)}) collective-permute-start(bf16[8,52,512]{2,1,0:T(8,128)(2,1)S(1)} %maximum_select_fusion.3), channel_id=1, source_target_pairs={{0,1},{1,0},{2,6},{3,7},{4,5},{5,4},{6,2},{7,3},{8,9},{9,8},{10,14... | collective-permute-start | bytes 1277960 | tf_op jit(solution)/shard_map/ppermute | solution.py:693
  291.5 16.3 %collective-permute-start.16 = (bf16[3,256,512]{2,1,0:T(8,128)(2,1)}, bf16[3,256,512]{2,1,0:T(8,128)(2,1)S(1)}, u32[]{:S(2)}, u32[]{:S(2)}) collective-permute-start(bf16[3,256,512]{2,1,0:T(8,128)(2,1)} %dynamic-slice_convert_fusion), channel_id=1, source_target_pairs={{0,1},{1,0},{2,3},{3,2},{4,5},{5,4},{6,7},{7,6},{8,9},{9,8},{10,11... | collective-permute-start | bytes 2359304 | tf_op jit(solution)/shard_map/ppermute | solution.py:629
  291.6 16.3 %copy-start.1 = (f32[3,512,512]{2,1,0:T(8,128)S(1)}, f32[3,512,512]{2,1,0:T(8,128)}, u32[]{:S(2)}) copy-start(f32[3,512,512]{2,1,0:T(8,128)} %get-tuple-element.74) | copy-start | bytes 9437188
  299.8 9.3 %collective-permute-start.15 = (bf16[16,52,512]{2,0,1:T(8,128)(2,1)S(1)}, bf16[16,52,512]{2,0,1:T(8,128)(2,1)S(1)}, u32[]{:S(2)}, u32[]{:S(2)}) collective-permute-start(bf16[16,52,512]{2,0,1:T(8,128)(2,1)S(1)} %copy.102), channel_id=1, source_target_pairs={{0,2},{1,3},{2,0},{3,1},{4,6},{5,7},{6,4},{7,5},{8,10},{9,11},{10,... | collective-permute-start | bytes 2555912 | tf_op jit(solution)/shard_map/ppermute | solution.py:693
Sparse Core Ops, SparseCore 0:
  229.7 72.1 all-gather.1

commit v3 on v2

--- a/solution.py
+++ b/solution.py
@@ -47,11 +47,15 @@
 
 
 def onehot_of(ids, types, copies):
-    lane = lax.broadcasted_iota(jnp.int32, (ids.shape[0], types * copies), 1)
-    hit = lane == ids
+    line = lax.broadcasted_iota(jnp.int32, (types * copies, ids.shape[1]), 0)
+    hit = line == ids
     for i in range(1, copies):
-        hit = hit | (lane == ids + i * types)
+        hit = hit | (line == ids + i * types)
     return jnp.where(hit, 1.0, 0.0).astype(BF16)
+
+
+def upright(values):
+    return jnp.broadcast_to(values.astype(F32), (8, values.shape[1])).T[:, :1]
 
 
 def whole(shape):
@@ -62,30 +66,19 @@
     return pl.BlockSpec((1,) + shape, lambda s: (s,) + (0,) * len(shape))
 
 
-def prepare_body(
-    start,
-    feats,
-    types,
-    table,
-    gain,
-    shift,
-    w_query,
-    b_query,
-    w_key,
-    w_value,
-    b_value,
-    base_out,
-    normed_out,
-    query_out,
-    key_out,
-    value_out,
-    reach,
-):
-    heads, _, rows = query_out.shape[1:]
-    cols, width = feats.shape[1:]
+def prepare_body(first, at, start, *refs):
+    feats, types, table, gain, shift, w_key, w_value, b_value = refs[:8]
+    if first:
+        w_query, b_query = refs[8:10]
+        base_out, normed_out, key_out, value_out, reach, far_out, query_out = refs[10:]
+    else:
+        far_query = refs[8]
+        base_out, normed_out, key_out, value_out, reach = refs[13:]
+    heads, _, cols = key_out.shape[1:]
+    width = feats.shape[2]
     size = width // heads
     base = feats[0].astype(F32) + dot(
-        onehot_of(types[0], table.shape[0] // 3, 3), table[...], NN
+        onehot_of(types[0], table.shape[0] // 3, 3), table[...], TN
     )
     base_out[0] = base
     unit, _ = unit_of(base)
@@ -100,55 +93,78 @@
 
     key = split_heads(dot(w_key[...], normed, TT).astype(BF16).astype(F32))
     key_out[0] = jnp.concatenate([key, key], 1).astype(BF16)
-    value = split_heads(dot(w_value[...], normed, TT) + b_value[...])
+    value = split_heads(dot(w_value[...], normed, TT) + upright(b_value[...]))
     line = lax.broadcasted_iota(jnp.int32, (heads, size, cols), 1)
     value_out[0] = jnp.concatenate([value, jnp.where(line < 3, 1.0, 0.0)], 1).astype(BF16)
-    own = normed_out[0, pl.ds(pl.multiple_of(start[0], rows), rows), :]
-    query = split_heads((dot(w_query[...], own, TT) + b_query[...]).astype(BF16).astype(F32))
-    scaled = query * size ** (-0.5)
-    upper = scaled.astype(BF16).astype(F32)
-    query_out[0] = jnp.concatenate([upper, scaled - upper], 1).astype(BF16)
-    reach[0] = jnp.broadcast_to(jnp.max(far(query) * far(key)), reach.shape[1:])
-
-
-def prepare(start, feats, types, table, gain, shift, w_query, b_query, w_key, w_value, b_value, heads, rows):
-    slots, cols, width = feats.shape
+    if first:
+        rows = query_out.shape[3]
+        own = normed_out[0, pl.ds(pl.multiple_of(start[0], rows), rows), :]
+        query = split_heads((dot(w_query[...], own, TT) + upright(b_query[...])).astype(BF16).astype(F32))
+        scaled = query * size ** (-0.5)
+        upper = scaled.astype(BF16).astype(F32)
+        query_out[0] = jnp.concatenate([upper, scaled - upper], 1).astype(BF16)
+        furthest = jnp.broadcast_to(far(query), far_out.shape[1:])
+        far_out[0] = furthest
+    else:
+        furthest = far_query[0]
+    reach[0] = jnp.broadcast_to(jnp.max(furthest * far(key)), reach.shape[1:])
+
+
+def prepare(at, start, feats, types, shared, heads, rows, cols, extra):
+    slots, part, width = feats.shape
+    first = len(extra) == 2
     square = whole((width, width))
-    row, column = whole((1, width)), whole((width, 1))
-    shapes = [
-        ((cols, width), F32),
-        ((cols, width), BF16),
-        ((heads, 16, rows), BF16),
-        ((heads, 16, cols), BF16),
-        ((heads, 16, cols), BF16),
-        ((8, 128), F32),
+    row = whole((1, width))
+
+    def across(s, at, start):
+        return (s, at[0], 0)
+
+    def along(s, at, start):
+        return (s, 0, 0, at[0])
+
+    def fixed(*shape):
+        return pl.BlockSpec((1,) + shape, lambda s, at, start: (s,) + (0,) * len(shape))
+
+    kept = pl.BlockSpec(memory_space=pl.ANY)
+    outs = [
+        ((cols, width), F32, pl.BlockSpec((1, part, width), across)),
+        ((cols, width), BF16, pl.BlockSpec((1, part, width), across)),
+        ((heads, 16, cols), BF16, pl.BlockSpec((1, heads, 16, part), along)),
+        ((heads, 16, cols), BF16, pl.BlockSpec((1, heads, 16, part), along)),
+        ((8, 128), F32, fixed(8, 128)),
     ]
+    if first:
+        outs.append(((heads, 128), F32, fixed(heads, 128)))
+        outs.append(((heads, 16, rows), BF16, fixed(heads, 16, rows)))
     return pl.pallas_call(
-        prepare_body,
-        grid=(slots,),
-        in_specs=[
-            pl.BlockSpec(memory_space=pltpu.SMEM),
-            by_slot(cols, width),
-            by_slot(cols, 1),
-            whole(table.shape),
-            row,
-            row,
-            square,
-            column,
-            square,
-            square,
-            column,
-        ],
-        out_specs=[by_slot(*shape) for shape, _ in shapes],
-        out_shape=[jax.ShapeDtypeStruct((slots,) + shape, kind) for shape, kind in shapes],
+        functools.partial(prepare_body, first),
+        grid_spec=pltpu.PrefetchScalarGridSpec(
+            num_scalar_prefetch=2,
+            grid=(slots,),
+            in_specs=[
+                fixed(part, width),
+                fixed(1, part),
+                whole(shared[0].shape),
+                row,
+                row,
+                square,
+                square,
+                row,
+            ]
+            + ([square, row] if first else [fixed(heads, 128)] + [kept] * 4),
+            out_specs=[spec for _, _, spec in outs],
+        ),
+        out_shape=[jax.ShapeDtypeStruct((slots,) + shape, kind) for shape, kind, _ in outs],
+        input_output_aliases={} if first else {11 + i: i for i in range(4)},
         compiler_params=pltpu.CompilerParams(vmem_limit_bytes=56 << 20),
         name="prepare",
-    )(start, feats, types, table, gain, shift, w_query, b_query, w_key, w_value, b_value)
+    )(at, start, feats, types, *shared, *extra)
 
 
 def feed_body(
+    at,
+    top,
     weighed,
-    top,
     base,
     cotan,
     w_out,
@@ -233,7 +249,7 @@
         g_weights[...] = total[...].astype(BF16)
 
 
-def feed(weighed, top, base, cotan, w_out, b_out, gain, shift, w_up, b_up, w_down, b_down):
+def feed(at, top, weighed, base, cotan, w_out, b_out, gain, shift, w_up, b_up, w_down, b_down):
     slots, heads, _, rows = weighed.shape
     width, hidden = w_up.shape
     row = whole((1, width))
@@ -248,13 +264,19 @@
         ((1, hidden), F32),
         ((4, width), F32),
     ]
+
+    def by_slot(*shape):
+        return pl.BlockSpec((1,) + shape, lambda s, at: (s,) + (0,) * len(shape))
+
     return pl.pallas_call(
         feed_body,
-        grid=(slots,),
-        in_specs=[
-            by_slot(heads, 16, rows),
-            by_slot(heads // STEP, rows, STEP),
-            by_slot(rows, width),
+        grid_spec=pltpu.PrefetchScalarGridSpec(
+            num_scalar_prefetch=1,
+            grid=(slots,),
+            in_specs=[
+                by_slot(heads // STEP, rows, STEP),
+                by_slot(heads, 16, rows),
+                pl.BlockSpec((1, rows, width), lambda s, at: (s, at[0], 0)),
             by_slot(rows, width),
             whole((width, width)),
             row,
@@ -266,12 +288,13 @@
             row,
         ],
         out_specs=[by_slot(*shape) for shape, _ in own] + [whole(shape) for shape, _ in shared],
+            scratch_shapes=[pltpu.VMEM(shared[0][0], F32)],
+        ),
         out_shape=[jax.ShapeDtypeStruct((slots,) + shape, kind) for shape, kind in own]
         + [jax.ShapeDtypeStruct(shape, kind) for shape, kind in shared],
-        scratch_shapes=[pltpu.VMEM(shared[0][0], F32)],
         compiler_params=pltpu.CompilerParams(vmem_limit_bytes=60 << 20),
         name="feed",
-    )(weighed, top, base, cotan, w_out, b_out, gain, shift, w_up, b_up, w_down, b_down)
+    )(at, top, weighed, base, cotan, w_out, b_out, gain, shift, w_up, b_up, w_down, b_down)
 
 
 def finish_body(
@@ -287,14 +310,12 @@
     w_query,
     w_key,
     w_value,
-    back_out,
-    g_weights,
-    g_table,
-    g_rows,
-    g_columns,
-    g_turned,
-    upstream,
+    feed_rows,
+    g_b_up,
+    pen_tile,
+    *rest,
 ):
+    *backs, g_weights, short, g_table, g_rows, g_columns, g_turned, upstream = rest
     slot = pl.program_id(0)
     rows, width = resid_grad.shape[1:]
     cols = base.shape[1]
@@ -323,18 +344,33 @@
     g_rows[0:1] += column_sum(received * unit)
     g_rows[1:2] += column_sum(received)
     upstream[...] = norm_back(received, unit, inverse, gain[...])
-    back_out[0] = upstream[...]
+    if len(backs) == 1:
+        backs[0][0] = upstream[...]
+    else:
+        backs[1][0] = upstream[pl.ds(pl.multiple_of(start[1], rows), rows), :].astype(BF16)
     upstream[own, :] += resid_grad[0]
+    if len(backs) == 2:
+        backs[0][0] = upstream[own, :]
     total = upstream[...]
     upper = total.astype(BF16)
     lower = (total - upper.astype(F32)).astype(BF16)
     onehot = onehot_of(types[0], g_table.shape[0], 1)
-    g_table[...] += dot(onehot, upper, TN) + dot(onehot, lower, TN)
+    g_table[...] += dot(onehot, upper, NN) + dot(onehot, lower, NN)
 
     @pl.when(slot == pl.num_programs(0) - 1)
     def _():
         for i in range(3):
             g_weights[i * width : (i + 1) * width] = g_turned[i].T
+        lines = [g_table[...], g_rows[...]]
+        lines += [jnp.broadcast_to(g_columns[i], (width, 128)).T[:1] for i in range(2)]
+        lines += [feed_rows[...]]
+        lines += [g_b_up[:, i : i + width] for i in range(0, g_b_up.shape[1], width)]
+        lines += [jnp.full((1, width), 0.5 * jnp.sum(pen_tile[...]))]
+        at = 0
+        short[...] = jnp.zeros_like(short)
+        for values in lines:
+            short[at : at + values.shape[0]] = values
+            at += values.shape[0]
 
 
 def finish(
@@ -350,17 +386,18 @@
     w_query,
     w_key,
     w_value,
+    feed_rows,
+    g_b_up,
+    pen_tile,
     type_count,
+    lines,
+    halves,
 ):
     slots, heads, size, rows = query_part.shape
     cols, width = base.shape[1:]
     square = whole((width, width))
-    shared = [
-        ((3 * width, width), F32),
-        ((type_count, width), F32),
-        ((2, width), F32),
-        ((2, width, 1), F32),
-    ]
+    backs = [((rows, width), F32), ((rows, width), BF16)] if halves else [((cols, width), F32)]
+    shared = [((3 * width, width), F32), ((lines, width), F32)]
     return pl.pallas_call(
         finish_body,
         grid=(slots,),
@@ -371,17 +408,26 @@
             by_slot(heads, size, cols),
             by_slot(cols, width),
             by_slot(cols, width),
-            by_slot(cols, 1),
+            by_slot(1, cols),
             by_slot(rows, width),
             whole((1, width)),
             square,
             square,
             square,
+            whole(feed_rows.shape),
+            whole(g_b_up.shape),
+            whole(pen_tile.shape),
         ],
-        out_specs=[by_slot(cols, width)] + [whole(shape) for shape, _ in shared],
-        out_shape=[jax.ShapeDtypeStruct((slots, cols, width), F32)]
+        out_specs=[by_slot(*shape) for shape, _ in backs] + [whole(shape) for shape, _ in shared],
+        out_shape=[jax.ShapeDtypeStruct((slots,) + shape, kind) for shape, kind in backs]
         + [jax.ShapeDtypeStruct(shape, kind) for shape, kind in shared],
-        scratch_shapes=[pltpu.VMEM((3, width, width), F32), pltpu.VMEM((cols, width), F32)],
+        scratch_shapes=[
+            pltpu.VMEM((type_count, width), F32),
+            pltpu.VMEM((2, width), F32),
+            pltpu.VMEM((2, width, 1), F32),
+            pltpu.VMEM((3, width, width), F32),
+            pltpu.VMEM((cols, width), F32),
+        ],
         compiler_params=pltpu.CompilerParams(vmem_limit_bytes=56 << 20),
         name="finish",
     )(
@@ -397,6 +443,9 @@
         w_query,
         w_key,
         w_value,
+        feed_rows,
+        g_b_up,
+        pen_tile,
     )
 
 
@@ -409,7 +458,7 @@
 
     @pl.when(group == 0)
     def _():
-        same = row_ids[0] == col_ids[0]
+        same = upright(row_ids[0]) == col_ids[0].astype(F32)
         mask[...] = jnp.where(same, 1.0, 0.0).astype(BF16)
         bias[...] = jnp.where(same, 0.0, -BIG)
 
@@ -461,7 +510,7 @@
             by_head(16, rows),
             by_head(16, cols),
             by_head(16, cols),
-            pl.BlockSpec((1, rows, 1), lambda s, g: (s, 0, 0)),
+            pl.BlockSpec((1, 1, rows), lambda s, g: (s, 0, 0)),
             pl.BlockSpec((1, 1, cols), lambda s, g: (s, 0, 0)),
         ],
         out_specs=[
@@ -512,7 +561,7 @@
 
     @pl.when(group == 0)
     def _():
-        same = row_ids[0] == col_ids[0]
+        same = upright(row_ids[0]) == col_ids[0].astype(F32)
         weight[...] = jnp.where(same, scale[0], 0.0).astype(BF16)
         mask[...] = jnp.where(same, 1.0, 0.0).astype(BF16)
         bias[...] = jnp.where(same, 0.0, -BIG)
@@ -585,7 +634,7 @@
             by_head(16, rows),
             by_head(16, cols),
             pl.BlockSpec((1, per_step // STEP, rows, STEP), lambda s, g: (s, g, 0, 0)),
-            pl.BlockSpec((1, rows, 1), lambda s, g: (s, 0, 0)),
+            pl.BlockSpec((1, 1, rows), lambda s, g: (s, 0, 0)),
             pl.BlockSpec((1, 1, cols), lambda s, g: (s, 0, 0)),
         ],
         out_specs=[
@@ -699,12 +748,14 @@
     return unpack(values)
 
 
-def sum_wide(values, sizes):
+def sum_wide(values, sizes, after):
     joint = ("slot", "blk")
     count = sizes["slot"] * sizes["blk"]
     terms = lax.all_to_all(values, joint, 0, 0, tiled=True)
+    terms, after = lax.optimization_barrier((terms, after))
     terms = terms.reshape((count, values.shape[0] // count, values.shape[1]))
-    return lax.all_gather(jnp.sum(terms.astype(F32), axis=0).astype(BF16), joint, tiled=True)
+    total = jnp.sum(terms.astype(F32), axis=0).astype(BF16)
+    return lax.all_gather(total, joint, tiled=True), after
 
 
 def local(
@@ -743,72 +794,97 @@
     def own(values, axis=1):
         return lax.dynamic_slice_in_dim(values, row_start, rows, axis)
 
-    if sizes["blk"] == 2:
-
-        def gathered(values):
-            came = swap(values, sizes, "blk", 1)
-            return jnp.where(
-                blk_at == 0,
-                jnp.concatenate([values, came], 1),
-                jnp.concatenate([came, values], 1),
-            )
-
-    else:
-
-        def gathered(values):
-            return lax.all_gather(values, "blk", axis=1, tiled=True)
-
-    feats = gathered(atom_feats)
-    all_types = gathered(type_ids)
-    squares = jnp.sum(mol_lengths * mol_lengths).astype(F32)
-    pair_total = butterfly(squares.reshape(1, 1), sizes, ("slot",))[0, 0]
-    pen_scale = 2.0 / pair_total
-    feats, pen_scale = lax.optimization_barrier((feats, pen_scale))
-
     bounds = jnp.cumsum(mol_lengths, axis=1)
     places = jnp.arange(cols, dtype=jnp.int32)
     mol_ids = jnp.sum((places[None, :, None] >= bounds[:, None, :]).astype(jnp.int32), axis=2)
     row_mols = own(mol_ids)
-    row_ids = row_mols[:, :, None]
+    row_ids = row_mols[:, None, :]
     col_ids = mol_ids[:, None, :]
 
     first = rounded(type_table)
     second = rounded(type_table - first)
     table = jnp.concatenate([first, second, type_table - first - second], 0).astype(BF16)
-    types_column = all_types[:, :, None]
     start = row_start.astype(jnp.int32).reshape(1)
+    here = blk_at.astype(jnp.int32).reshape(1)
 
     def line(values):
         return values.reshape(1, -1)
 
-    def column(values):
-        return values.reshape(-1, 1)
-
-    base, normed, query_rows, key_rows, value_rows, reach = prepare(
-        start,
-        feats,
-        types_column,
-        table,
-        line(ln1_gain),
-        line(ln1_shift),
-        w_query,
-        column(b_query),
-        w_key,
-        w_value,
-        column(b_value),
-        heads,
-        rows,
-    )
-    furthest = (width // heads) ** (-0.5) * jnp.sqrt(reach[:, 0, 0]) + PAIR_LIMIT
-    safe = (furthest <= SAFE_LOGIT).astype(jnp.int32)
-
+    shared = (table, line(ln1_gain), line(ln1_shift), w_key, w_value, line(b_value))
+    asking = (w_query, line(b_query))
+
+    def safe_of(reach):
+        furthest = (width // heads) ** (-0.5) * jnp.sqrt(reach[:, 0, 0]) + PAIR_LIMIT
+        return (furthest <= SAFE_LOGIT).astype(jnp.int32)
+
+    count = jnp.sum(mol_lengths * mol_lengths).astype(F32).reshape(1, 1)
+    if sizes["blk"] == 2:
+        there = 1 - here
+        came_feats = swap(atom_feats, sizes, "blk", 1)
+        came_types = swap(type_ids, sizes, "blk", 1)
+        near = [swap(count, sizes, "slot", bit) for bit in (1, 2, 3)]
+        base, normed, key_rows, value_rows, reach, far_query, query_rows = prepare(
+            here,
+            jnp.zeros((1,), jnp.int32),
+            atom_feats,
+            type_ids[:, None, :],
+            shared,
+            heads,
+            rows,
+            cols,
+            asking,
+        )
+        safe = safe_of(reach)
+        near, reach = lax.optimization_barrier((near, reach))
+        count = count + near[0] + (near[1] + near[2])
+        far = [swap(count, sizes, "slot", bit) for bit in range(4, sizes["slot"], 4)]
+        base, normed, key_rows, value_rows, reach = prepare(
+            there,
+            start,
+            came_feats,
+            came_types[:, None, :],
+            shared,
+            heads,
+            rows,
+            cols,
+            (far_query, base, normed, key_rows, value_rows),
+        )
+        safe = safe * safe_of(reach)
+        far, safe = lax.optimization_barrier((far, safe))
+        pair_total = count + sum(far)
+        all_types = jnp.where(
+            blk_at == 0,
+            jnp.concatenate([type_ids, came_types], 1),
+            jnp.concatenate([came_types, type_ids], 1),
+        )
+    else:
+        feats = lax.all_gather(atom_feats, "blk", axis=1, tiled=True)
+        all_types = lax.all_gather(type_ids, "blk", axis=1, tiled=True)
+        zero = jnp.zeros((1,), jnp.int32)
+        base, normed, key_rows, value_rows, reach, _, query_rows = prepare(
+            zero,
+            start,
+            feats,
+            all_types[:, None, :],
+            shared,
+            heads,
+            rows,
+            cols,
+            asking,
+        )
+        safe = safe_of(reach)
+        pair_total = butterfly(count, sizes, ("slot",))
+    pen_scale = (2.0 / pair_total).reshape(1)
     weighed, top = attend(
         safe, pair_feats, query_rows, key_rows, value_rows, row_ids, col_ids, 16
     )
+    types_row = all_types[:, None, :]
+
     atom_out, grad_rows, log_total, resid_grad, g_feed, g_b_up, feed_rows = feed(
+        here,
+        top,
         weighed,
-        top,
-        own(base),
+        base,
         atom_cotan,
         w_out,
         line(b_out),
@@ -819,11 +895,10 @@
         w_down,
         line(b_down),
     )
-    g_feed = sum_wide(g_feed, sizes)
 
     pair_out, pair_grad, query_part, key_part, value_part, pen_tile = attend_back(
         safe,
-        pen_scale.reshape(1),
+        pen_scale,
         pair_feats,
         pair_cotan,
         query_rows,
@@ -835,37 +910,43 @@
         col_ids,
         16,
     )
-    penalty = 0.5 * jnp.sum(pen_tile)
-
-    back, g_weights, g_type_table, norm_rows, bias_columns = finish(
-        start,
+
+    devices = sizes["slot"] * sizes["blk"]
+    used = types + 9 + g_b_up.shape[1] // width
+    halves = sizes["blk"] == 2
+    *backs, g_weights, short = finish(
+        jnp.concatenate([start, rows - start]),
         query_part,
         key_part,
         value_part,
         base,
         normed,
-        types_column,
+        types_row,
         resid_grad,
         line(ln1_gain),
         w_query,
         w_key,
         w_value,
+        feed_rows,
+        g_b_up,
+        pen_tile,
         types,
+        used + -used % devices,
+        halves,
     )
-    if sizes["blk"] == 2:
-        away = lax.dynamic_slice_in_dim(back, (1 - blk_at) * rows, rows, 1).astype(BF16)
-        base_grad = own(back) + swap(away, sizes, "blk", 1).astype(F32) + resid_grad
+    g_feed, short = sum_wide(g_feed, sizes, short)
+    if halves:
+        base_grad = backs[0] + swap(backs[1], sizes, "blk", 1).astype(F32)
     else:
-        base_grad = resid_grad + lax.psum_scatter(back, "blk", scatter_dimension=1, tiled=True)
-    parts = [g_type_table, norm_rows, bias_columns.reshape(2, width), feed_rows]
-    parts += [g_b_up.reshape(-1, width), jnp.full((1, width), penalty)]
-    used = sum(part.shape[0] for part in parts)
-    devices = sizes["slot"] * sizes["blk"]
-    parts.append(jnp.zeros((-used % devices, width), F32))
+        base_grad = resid_grad + lax.psum_scatter(backs[0], "blk", scatter_dimension=1, tiled=True)
+    hidden = w_up.shape[1]
+    g_w_up = jnp.concatenate(
+        [g_feed[at : at + width] for at in range(hidden + width, 2 * hidden + width, width)], 1
+    ).astype(F32)
+    g_w_down = g_feed[:hidden].astype(F32)
+    g_w_out = g_feed[hidden : hidden + width].astype(F32)
     g_weights, packed = sum_all(
-        g_weights.reshape(devices, -1, width),
-        jnp.concatenate(parts, 0).reshape(devices, -1, width),
-        plan,
+        g_weights.reshape(devices, -1, width), short.reshape(devices, -1, width), plan
     )
     g_weights = g_weights.reshape(3 * width, width)
     packed = packed.reshape(-1, width)[:used]
@@ -880,10 +961,6 @@
         g_ln2_shift,
         g_b_down,
     ) = (packed[at + i] for i in range(8))
-    hidden = w_up.shape[1]
-    g_w_up = jnp.concatenate(
-        [g_feed[at : at + width] for at in range(hidden + width, 2 * hidden + width, width)], 1
-    )
     return (
         atom_out,
         pair_out,
@@ -898,13 +975,13 @@
         g_weights[width : 2 * width],
         g_weights[2 * width :],
         g_b_value,
-        g_feed[hidden : hidden + width].astype(F32),
+        g_w_out,
         g_b_out,
         g_ln2_gain,
         g_ln2_shift,
-        g_w_up.astype(F32),
+        g_w_up,
         packed[at + 8 : used - 1].reshape(-1),
-        g_feed[:hidden].astype(F32),
+        g_w_down,
         g_b_down,
     )
 

time: 338 us -> 335 us (level)
  local copies, waits for them, and re-layouts: 19.6 us -> 11.9 us
  Pallas kernels: 170 us -> 174 us
    pallas_call x2 -> x3, Pallas kernels: 35 us -> 38.9 us  [the longest x1 25.7 us: feed(): pl.pallas_call(feed_body, grid_spec=pltpu.PrefetchScalarGridSpec(num_scal...]
    ppermute x7 -> x9, starting transfers between devices: 15.1 us -> 17 us  [swap(): lax.ppermute(values, axis, [(i, i ^ bit) for i in range(sizes[axis])])]
    convert_element_type x3 -> x2, other arithmetic: 8.14 us -> 6.75 us  [the longest x1 4.2 us: local(): g_w_down = g_feed[:hidden].astype(F32)]
    ppermute x7 -> x9, waiting for transfers between devices: 8.5 us -> 7.94 us  [swap(): lax.ppermute(values, axis, [(i, i ^ bit) for i in range(sizes[axis])])]
  transfers between devices with their start and end apart: 19 -> 21, of which waited for: 12 -> 9; matrix products, arithmetic and copies ran while one was open for 10% -> 8% of each run, Pallas kernels for 31% -> 35%
where the time goes in v3:
time: 335 us; the launch traced here: 329 us
  Pallas kernels  174 us (52%)
  waiting for transfers between devices  51.8 us (15%)
  starting transfers between devices  44.4 us (13%)
  other arithmetic  26.4 us (8%)
  between operations  19.6 us (6%)
  local copies, waits for them, and re-layouts  11.9 us (4%)
    pallas_call x1, Pallas kernels, attend_back(): pl.pallas_call(backward_body, grid=(slots, heads // per_step), in_specs=[...  86.9 us
    pallas_call x1, Pallas kernels, attend(): pl.pallas_call(forward_body, grid=(slots, heads // per_step), in_specs=[p...  33.9 us
    ppermute x5, waiting for transfers between devices, sum_all(): came = lax.ppermute(values, joint, pairs)  26.8 us
    pallas_call x1, Pallas kernels, feed(): pl.pallas_call(feed_body, grid_spec=pltpu.PrefetchScalarGridSpec(num_scal...  25.7 us
    ppermute x5, waiting for transfers between devices, sum_all(): came_wide, came_small = unpack(lax.ppermute(away, joint, pairs))  17 us
    ppermute x9, starting transfers between devices, swap(): lax.ppermute(values, axis, [(i, i ^ bit) for i in range(sizes[axis])])  17 us
    pallas_call x1, Pallas kernels, finish(): pl.pallas_call(finish_body, grid=(slots,), in_specs=[pl.BlockSpec(memory_...  14.7 us
    ppermute x5, starting transfers between devices, sum_all(): came = lax.ppermute(values, joint, pairs)  13.8 us
  transfers between devices with their start and end apart: 21, of which 9 were waited for; matrix products, arithmetic and copies ran while one was open for 8% of the time, Pallas kernels for 35%

profile of v3, /device:TPU:0, one launch (start us, length us, event | category | flops | bytes accessed | tf_op | source)
XLA Modules:
  0.0 328.5 jit_solution(5762118603603670035)
XLA Ops:
  7.2 3.0 collective-permute-start.6
  10.2 1.3 multiply_reduce_fusion
  12.2 0.9 collective-permute-start
  13.1 2.8 collective-permute-start.1
  15.9 1.3 collective-permute-start.2
  17.2 0.5 collective-permute-start.7
  17.7 0.9 reduce_window_sum.11
  18.7 0.9 reduce-precision_convert_fusion.2
  19.5 0.6 pad_maximum_fusion.4.refs_2_
  20.2 1.3 broadcast_in_dim.15.refs_1_
  21.4 0.6 broadcast_in_dim.18.col_ids
  22.0 0.6 broadcast_in_dim.17.row_ids
  22.6 7.1 %prepare.2 = (f32[3,512,512]{2,1,0:T(8,128)}, bf16[3,512,512]{2,1,0:T(8,128)(2,1)}, bf16[3,64,16,512]{3,2,1,0:T(8,128)(2,1)}, bf16[3,64,16,512]{3,2,1,0:T(8,128)...) custom-call(s32[1]{0:T(128)} %bitcast.at, s32[1]{0:T(128)} %constant.173.clone.1.start, ...), custom_call_target="tpu_custom_call" | custom-call | tf_op jit(solution)/shard_map/prepare/pallas_call | solution.py:139
  31.7 2.9 collective-permute-start.3
  34.6 3.9 %collective-permute-start.4 = (f32[1,1]{1,0:T(1,128)}, f32[1,1]{1,0:T(1,128)}, u32[]{:S(2)}, u32[]{:S(2)}) collective-permute-start(f32[1,1]{1,0:T(1,128)} %add.162), channel_id=1, source_target_pairs={{0,16},{2,18},{4,20},{6,22},{8,24},{10,26},{12,28},{14,30},{16,0},... | collective-permute-start | bytes 20 | tf_op jit(solution)/shard_map/ppermute | solution.py:678
  38.5 1.5 collective-permute-start.5
  40.0 0.6 broadcast_in_dim.16.refs_1_
  40.6 0.9 copy-done.2
  41.5 6.0 %prepare.3 = (f32[3,512,512]{2,1,0:T(8,128)}, bf16[3,512,512]{2,1,0:T(8,128)(2,1)}, bf16[3,64,16,512]{3,2,1,0:T(8,128)(2,1)}, bf16[3,64,16,512]{3,2,1,0:T(8,128)(2,1)}, f32[3,8,128]{2,1,0:T(8,128)}) custom-call(s32[1]{0:T(128)S(6)} %sub.67.at, s32[1]{0:T(128)} %bitcast.6.start, ...), custom_call_target="tpu_custom_call", output_to_operand_aliasing={{0}: (11, {}), {1}: (12, {}), {2}: (13, {}), {3}: (14, {})} | custom-call | tf_op jit(solution)/shard_map/prepare/pallas_call | solution.py:139
  47.6 1.4 fusion.20.safe
  49.0 33.9 %attend.1 = (f32[3,64,16,256]{3,2,1,0:T(8,128)}, f32[3,8,256,8]{3,2,1,0:T(8,128)}) custom-call(s32[3]{0:T(128)} %fusion.20.safe, bf16[3,64,256,512]{3,2,1,0:T(8,128)(2,1)} %pf.3, bf16[3,64,16,256]{3,2,1,0:T(8,128)(2,1)} %get-tuple-element.72.query, bf16[3,64,16,512]{3,2,1,0:T(8,128)(2,1)} %get-tuple-element.73.key, ...), custom_call_target="tpu_custom_call" | custom-call | tf_op jit(solution)/shard_map/attend/pallas_call | solution.py:504
  82.9 25.7 %feed.1 = (bf16[3,256,512]{2,1,0:T(8,128)(2,1)}, bf16[3,64,16,256]{3,2,1,0:T(8,128)(2,1)}, f32[3,8,256,8]{3,2,1,0:T(8,128)}, f32[3,256,512]{2,1,0:T(8,128)}, bf1...) custom-call(s32[1]{0:T(128)} %bitcast.at, f32[3,8,256,8]{3,2,1,0:T(8,128)} %get-tuple-element.75.top, ...), custom_call_target="tpu_custom_call" | custom-call | tf_op jit(solution)/shard_map/feed/pallas_call | solution.py:271
  108.7 5.7 %all-to-all-start = ((bf16[32,144,512]{2,1,0:T(8,128)(2,1)}), bf16[32,144,512]{2,1,0:T(8,128)(2,1)}, u32[]{:S(2)}, u32[]{:S(2)}) async-start(bf16[32,144,512]{2,1,0:T(8,128)(2,1)} %bitcast.77), calls=%async_computation | async-start | bytes 9437184 | tf_op jit(solution)/shard_map/all_to_all | solution.py:754
  114.5 0.6 pad_add_fusion.start
  115.1 0.6 broadcast_select_fusion.types
  117.6 86.9 %attend_back.1 = (bf16[3,64,256,512]{3,2,1,0:T(8,128)(2,1)}, bf16[3,64,256,512]{3,2,1,0:T(8,128)(2,1)}, f32[3,64,8,256]{3,2,1,0:T(8,128)}, f32[3,64,8,512]{3,2,1...) custom-call(s32[3]{0:T(128)} %fusion.20.safe, f32[1]{0:T(128)} %bitcast.12.scale, ...), custom_call_target="tpu_custom_call" | custom-call | tf_op jit(solution)/shard_map/attend_back/pallas_call | solution.py:624
  204.5 14.7 %finish.1 = (f32[3,256,512]{2,1,0:T(8,128)}, bf16[3,256,512]{2,1,0:T(8,128)(2,1)}, f32[1536,512]{1,0:T(8,128)}, f32[64,512]{1,0:T(8,128)}) custom-call(s32[2]{0:T(128)} %pad_add_fusion.start, f32[3,64,8,256]{3,2,1,0:T(8,128)} %get-tuple-element.85.query_part, f32[3,64,8,512]{3,2,1,0:T(8,128)} %get-tuple-element.86.key_part, ...), custom_call_target="tpu_custom_call" | custom-call | tf_op jit(solution)/shard_map/finish/pallas_call | solution.py:401
  219.2 1.6 constant_dynamic-slice_fusion.8
  220.8 0.4 copy.90
  221.4 1.0 pad_maximum_fusion
  222.6 3.9 %reduce_sum.32 = bf16[144,512]{1,0:T(8,128)(2,1)} reduce(bf16[32,144,512]{2,1,0:T(8,128)(2,1)} %bitcast.44, bf16[]{:T(256)} %constant.188.clone.1), dimensions={0}, to_apply=%region_3.4 | reduce | flops 2285568 | bytes 4866050 | tf_op jit(solution)/shard_map/reduce_sum | solution.py:757
  226.7 1.4 convert_element_type.121
  228.1 1.0 fusion.1
  229.5 1.7 collective-permute-start.9
  231.3 6.8 %collective-permute-done.9 = bf16[8,52,512]{2,1,0:T(8,128)(2,1)S(1)} collective-permute-done((bf16[8,52,512]{2,1,0:T(8,128)(2,1)S(1)}, bf16[8,52,512]{2,1,0:T(8,128)(2,1)S(1)}, u32[]{:S(2)}, u32[]{:S(2)}) %collective-permute-start.9) | collective-permute-done | bytes 426016 | tf_op jit(solution)/shard_map/ppermute | solution.py:737
  238.2 0.5 slice_add_fusion.1
  238.8 1.7 collective-permute-start.10
  240.5 4.4 %collective-permute-done.10 = bf16[4,52,512]{2,1,0:T(8,128)(2,1)S(1)} collective-permute-done((bf16[4,52,512]{2,1,0:T(8,128)(2,1)S(1)}, bf16[4,52,512]{2,1,0:T(8,128)(2,1)S(1)}, u32[]{:S(2)}, u32[]{:S(2)}) %collective-permute-start.10) | collective-permute-done | bytes 213024 | tf_op jit(solution)/shard_map/ppermute | solution.py:737
  245.2 1.7 collective-permute-start.11
  246.8 3.2 collective-permute-done.11
  250.2 2.6 collective-permute-start.12
  252.8 2.6 collective-permute-done.12
  255.5 3.4 %collective-permute-start.13 = (bf16[1,52,512]{2,1,0:T(8,128)(2,1)S(1)}, bf16[1,52,512]{2,1,0:T(8,128)(2,1)S(1)}, u32[]{:S(2)}, u32[]{:S(2)}) collective-permute-start(bf16[1,52,512]{2,1,0:T(8,128)(2,1)S(1)} %pad_maximum_fusion.6), channel_id=1, source_target_pairs={{0,16},{1,17},{2,18},{3,19},{4,20},{5,21},{6,22},{7,23},{8,24},{9,... | collective-permute-start | bytes 159752 | tf_op jit(solution)/shard_map/ppermute | solution.py:742
  258.9 3.2 collective-permute-done.13
  262.2 5.0 %collective-permute-start.14 = (bf16[2,52,512]{2,1,0:T(8,128)(2,1)S(1)}, bf16[2,52,512]{2,1,0:T(8,128)(2,1)S(1)}, u32[]{:S(2)}, u32[]{:S(2)}) collective-permute-start(bf16[2,52,512]{2,1,0:T(8,128)(2,1)S(1)} %maximum_select_fusion.4), channel_id=1, source_target_pairs={{0,8},{1,9},{2,10},{3,11},{4,12},{5,13},{6,14},{7,15},{8,0},{9,1},... | collective-permute-start | bytes 319496 | tf_op jit(solution)/shard_map/ppermute | solution.py:742
  267.2 2.8 collective-permute-done.14
  270.0 1.7 collective-permute-start.15
  271.6 10.7 %collective-permute-done.15 = bf16[4,52,512]{2,1,0:T(8,128)(2,1)S(1)} collective-permute-done((bf16[4,52,512]{2,1,0:T(8,128)(2,1)S(1)}, bf16[4,52,512]{2,1,0:T(8,128)(2,1)S(1)}, u32[]{:S(2)}, u32[]{:S(2)}) %collective-permute-start.15) | collective-permute-done | bytes 213024 | tf_op jit(solution)/shard_map/ppermute | solution.py:742
  282.4 3.7 %collective-permute-start.16 = (bf16[8,52,512]{2,1,0:T(8,128)(2,1)S(1)}, bf16[8,52,512]{2,1,0:T(8,128)(2,1)S(1)}, u32[]{:S(2)}, u32[]{:S(2)}) collective-permute-start(bf16[8,52,512]{2,1,0:T(8,128)(2,1)S(1)} %maximum_select_fusion.2), channel_id=1, source_target_pairs={{0,1},{1,0},{2,6},{3,7},{4,5},{5,4},{6,2},{7,3},{8,9},{9,8},{10,14... | collective-permute-start | bytes 1277960 | tf_op jit(solution)/shard_map/ppermute | solution.py:742
  286.1 10.2 %collective-permute-done.16 = bf16[8,52,512]{2,1,0:T(8,128)(2,1)S(1)} collective-permute-done((bf16[8,52,512]{2,1,0:T(8,128)(2,1)S(1)}, bf16[8,52,512]{2,1,0:T(8,128)(2,1)S(1)}, u32[]{:S(2)}, u32[]{:S(2)}) %collective-permute-start.16) | collective-permute-done | bytes 426016 | tf_op jit(solution)/shard_map/ppermute | solution.py:742
  296.5 0.3 copy.70
  296.8 7.9 %collective-permute-done.18 = bf16[3,256,512]{2,1,0:T(8,128)(2,1)S(1)} collective-permute-done((bf16[3,256,512]{2,1,0:T(8,128)(2,1)}, bf16[3,256,512]{2,1,0:T(8,128)(2,1)S(1)}, u32[]{:S(2)}, u32[]{:S(2)}) %collective-permute-start.18) | collective-permute-done | bytes 786464 | tf_op jit(solution)/shard_map/ppermute | solution.py:678
  304.7 1.1 add_convert_fusion
  305.9 0.5 copy.71
  306.4 0.4 fusion
  306.8 0.4 slice.198
  307.4 0.5 slice.194
  307.9 0.7 slice.157
  308.6 0.6 copy.75
  309.2 0.6 fusion.24
  309.8 1.7 fusion.23
  311.5 3.0 fusion.22
  314.5 2.6 maximum_convert_fusion
  317.0 4.2 %slice_convert_fusion = f32[2048,512]{1,0:T(8,128)} fusion(bf16[4608,512]{1,0:T(8,128)(2,1)} %all-gather.2.cloned.1.call-done), kind=kLoop, calls=%fused_computation | loop fusion | flops 1048576 | bytes 6291456 | tf_op jit(solution)/shard_map/convert_element_type | solution.py:946
  (71 shorter events, 2.2 us)
Async XLA Ops:
  7.2 33.5 %collective-permute-start.6 = (bf16[3,256,512]{2,1,0:T(8,128)(2,1)}, bf16[3,256,512]{2,1,0:T(8,128)(2,1)S(1)}, u32[]{:S(2)}, u32[]{:S(2)}) collective-permute-start(bf16[3,256,512]{2,1,0:T(8,128)(2,1)} %refs_0_.1), channel_id=1, source_target_pairs={{0,1},{1,0},{2,3},{3,2},{4,5},{5,4},{6,7},{7,6},{8,9},{9,8},{10,11... | collective-permute-start | bytes 2359304 | tf_op jit(solution)/shard_map/ppermute | solution.py:678
  12.2 17.6 %collective-permute-start = (f32[1,1]{1,0:T(1,128)}, f32[1,1]{1,0:T(1,128)}, u32[]{:S(2)}, u32[]{:S(2)}) collective-permute-start(f32[1,1]{1,0:T(1,128)} %bitcast.1), channel_id=1, source_target_pairs={{0,2},{2,0},{4,6},{6,4},{8,10},{10,8},{12,14},{14,12},{16,18},{18,... | collective-permute-start | bytes 20 | tf_op jit(solution)/shard_map/ppermute | solution.py:678
  13.1 16.7 %collective-permute-start.1 = (f32[1,1]{1,0:T(1,128)}, f32[1,1]{1,0:T(1,128)}, u32[]{:S(2)}, u32[]{:S(2)}) collective-permute-start(f32[1,1]{1,0:T(1,128)} %bitcast.1), channel_id=1, source_target_pairs={{0,4},{2,6},{4,0},{6,2},{8,12},{10,14},{12,8},{14,10},{16,20},{18,... | collective-permute-start | bytes 20 | tf_op jit(solution)/shard_map/ppermute | solution.py:678
  15.9 13.9 %collective-permute-start.2 = (f32[1,1]{1,0:T(1,128)}, f32[1,1]{1,0:T(1,128)}, u32[]{:S(2)}, u32[]{:S(2)}) collective-permute-start(f32[1,1]{1,0:T(1,128)} %bitcast.1), channel_id=1, source_target_pairs={{0,6},{2,4},{4,2},{6,0},{8,14},{10,12},{12,10},{14,8},{16,22},{18,... | collective-permute-start | bytes 20 | tf_op jit(solution)/shard_map/ppermute | solution.py:678
  17.2 22.9 %collective-permute-start.7 = (s32[3,256]{1,0:T(4,128)}, s32[3,256]{1,0:T(4,128)S(1)}, u32[]{:S(2)}, u32[]{:S(2)}) collective-permute-start(s32[3,256]{1,0:T(4,128)} %param.24), channel_id=1, source_target_pairs={{0,1},{1,0},{2,3},{3,2},{4,5},{5,4},{6,7},{7,6},{8,9},{9,8},{10,11... | collective-permute-start | bytes 9224 | tf_op jit(solution)/shard_map/ppermute | solution.py:678
  31.7 17.3 %collective-permute-start.3 = (f32[1,1]{1,0:T(1,128)}, f32[1,1]{1,0:T(1,128)}, u32[]{:S(2)}, u32[]{:S(2)}) collective-permute-start(f32[1,1]{1,0:T(1,128)} %add.162), channel_id=1, source_target_pairs={{0,8},{2,10},{4,12},{6,14},{8,0},{10,2},{12,4},{14,6},{16,24},{18,... | collective-permute-start | bytes 20 | tf_op jit(solution)/shard_map/ppermute | solution.py:678
  34.6 14.3 %collective-permute-start.4 = (f32[1,1]{1,0:T(1,128)}, f32[1,1]{1,0:T(1,128)}, u32[]{:S(2)}, u32[]{:S(2)}) collective-permute-start(f32[1,1]{1,0:T(1,128)} %add.162), channel_id=1, source_target_pairs={{0,16},{2,18},{4,20},{6,22},{8,24},{10,26},{12,28},{14,30},{16,0},... | collective-permute-start | bytes 20 | tf_op jit(solution)/shard_map/ppermute | solution.py:678
  38.5 10.4 %collective-permute-start.5 = (f32[1,1]{1,0:T(1,128)}, f32[1,1]{1,0:T(1,128)}, u32[]{:S(2)}, u32[]{:S(2)}) collective-permute-start(f32[1,1]{1,0:T(1,128)} %add.162), channel_id=1, source_target_pairs={{0,24},{2,26},{4,28},{6,30},{8,16},{10,18},{12,20},{14,22},{16,8},... | collective-permute-start | bytes 20 | tf_op jit(solution)/shard_map/ppermute | solution.py:678
  40.6 0.9 copy-start.2
  108.7 6.4 %copy-start.4 = (s32[3,1,256]{2,1,0:T(1,128)S(1)}, s32[3,1,256]{2,1,0:T(1,128)}, u32[]{:S(2)}) copy-start(s32[3,1,256]{2,1,0:T(1,128)} %broadcast_in_dim.16.refs_1_) | copy-start | bytes 9220
  108.7 6.4 %copy-start.5 = (s32[3,1,256]{2,1,0:T(1,128)S(1)}, s32[3,1,256]{2,1,0:T(1,128)}, u32[]{:S(2)}) copy-start(s32[3,1,256]{2,1,0:T(1,128)} %broadcast_in_dim.15.refs_1_) | copy-start | bytes 9220
  108.7 112.6 %all-to-all-start = ((bf16[32,144,512]{2,1,0:T(8,128)(2,1)}), bf16[32,144,512]{2,1,0:T(8,128)(2,1)}, u32[]{:S(2)}, u32[]{:S(2)}) async-start(bf16[32,144,512]{2,1,0:T(8,128)(2,1)} %bitcast.77), calls=%async_computation | async-start | bytes 9437184 | tf_op jit(solution)/shard_map/all_to_all | solution.py:754
  114.4 197.1 %all-gather.2.cloned.1.call-start = ((), (), s32[]{:S(2)}) async-start(), calls=%async_computation.1 | async-start | bytes 4866048 | tf_op jit(solution)/shard_map/all_gather | solution.py:758
  219.2 2.0 copy-start.3
  222.4 4.1 %copy-start = (f32[1536,512]{1,0:T(8,128)S(1)}, f32[1536,512]{1,0:T(8,128)}, u32[]{:S(2)}) copy-start(f32[1536,512]{1,0:T(8,128)} %get-tuple-element.93) | copy-start | bytes 9437188
  222.4 4.3 %collective-permute-start.8 = (bf16[16,52,512]{2,0,1:T(8,128)(2,1)}, bf16[16,52,512]{2,0,1:T(8,128)(2,1)}, u32[]{:S(2)}, u32[]{:S(2)}) collective-permute-start(bf16[16,52,512]{2,0,1:T(8,128)(2,1)} %pad_maximum_fusion), channel_id=1, source_target_pairs={{0,2},{1,3},{2,0},{3,1},{4,6},{5,7},{6,4},{7,5},{8,10},{9,11},{10,... | collective-permute-start | bytes 2555912 | tf_op jit(solution)/shard_map/ppermute | solution.py:737
  229.5 8.6 %collective-permute-start.9 = (bf16[8,52,512]{2,1,0:T(8,128)(2,1)S(1)}, bf16[8,52,512]{2,1,0:T(8,128)(2,1)S(1)}, u32[]{:S(2)}, u32[]{:S(2)}) collective-permute-start(bf16[8,52,512]{2,1,0:T(8,128)(2,1)S(1)} %pad_maximum_fusion.1), channel_id=1, source_target_pairs={{0,1},{1,0},{2,6},{3,7},{4,5},{5,4},{6,2},{7,3},{8,9},{9,8},{10,14... | collective-permute-start | bytes 1277960 | tf_op jit(solution)/shard_map/ppermute | solution.py:737
  238.8 6.1 %collective-permute-start.10 = (bf16[4,52,512]{2,1,0:T(8,128)(2,1)S(1)}, bf16[4,52,512]{2,1,0:T(8,128)(2,1)S(1)}, u32[]{:S(2)}, u32[]{:S(2)}) collective-permute-start(bf16[4,52,512]{2,1,0:T(8,128)(2,1)S(1)} %pad_maximum_fusion.2), channel_id=1, source_target_pairs={{0,4},{1,5},{2,3},{3,2},{4,0},{5,1},{6,7},{7,6},{8,12},{9,13},{10,... | collective-permute-start | bytes 638984 | tf_op jit(solution)/shard_map/ppermute | solution.py:737
  245.2 4.9 %collective-permute-start.11 = (bf16[2,52,512]{2,1,0:T(8,128)(2,1)S(1)}, bf16[2,52,512]{2,1,0:T(8,128)(2,1)S(1)}, u32[]{:S(2)}, u32[]{:S(2)}) collective-permute-start(bf16[2,52,512]{2,1,0:T(8,128)(2,1)S(1)} %pad_maximum_fusion.3), channel_id=1, source_target_pairs={{0,8},{1,9},{2,10},{3,11},{4,12},{5,13},{6,14},{7,15},{8,0},{9,1},... | collective-permute-start | bytes 319496 | tf_op jit(solution)/shard_map/ppermute | solution.py:737
  250.1 54.6 %copy-start.1 = (f32[3,256,512]{2,1,0:T(8,128)S(1)}, f32[3,256,512]{2,1,0:T(8,128)}, u32[]{:S(2)}) copy-start(f32[3,256,512]{2,1,0:T(8,128)} %get-tuple-element.97) | copy-start | bytes 4718596
  250.2 5.2 %collective-permute-start.12 = (bf16[1,52,512]{2,1,0:T(8,128)(2,1)S(1)}, bf16[1,52,512]{2,1,0:T(8,128)(2,1)S(1)}, u32[]{:S(2)}, u32[]{:S(2)}) collective-permute-start(bf16[1,52,512]{2,1,0:T(8,128)(2,1)S(1)} %pad_maximum_fusion.5), channel_id=1, source_target_pairs={{0,16},{1,17},{2,18},{3,19},{4,20},{5,21},{6,22},{7,23},{8,24},{9,... | collective-permute-start | bytes 159752 | tf_op jit(solution)/shard_map/ppermute | solution.py:737
  255.5 6.6 %collective-permute-start.13 = (bf16[1,52,512]{2,1,0:T(8,128)(2,1)S(1)}, bf16[1,52,512]{2,1,0:T(8,128)(2,1)S(1)}, u32[]{:S(2)}, u32[]{:S(2)}) collective-permute-start(bf16[1,52,512]{2,1,0:T(8,128)(2,1)S(1)} %pad_maximum_fusion.6), channel_id=1, source_target_pairs={{0,16},{1,17},{2,18},{3,19},{4,20},{5,21},{6,22},{7,23},{8,24},{9,... | collective-permute-start | bytes 159752 | tf_op jit(solution)/shard_map/ppermute | solution.py:742
  262.2 7.8 %collective-permute-start.14 = (bf16[2,52,512]{2,1,0:T(8,128)(2,1)S(1)}, bf16[2,52,512]{2,1,0:T(8,128)(2,1)S(1)}, u32[]{:S(2)}, u32[]{:S(2)}) collective-permute-start(bf16[2,52,512]{2,1,0:T(8,128)(2,1)S(1)} %maximum_select_fusion.4), channel_id=1, source_target_pairs={{0,8},{1,9},{2,10},{3,11},{4,12},{5,13},{6,14},{7,15},{8,0},{9,1},... | collective-permute-start | bytes 319496 | tf_op jit(solution)/shard_map/ppermute | solution.py:742
  270.0 12.3 %collective-permute-start.15 = (bf16[4,52,512]{2,1,0:T(8,128)(2,1)S(1)}, bf16[4,52,512]{2,1,0:T(8,128)(2,1)S(1)}, u32[]{:S(2)}, u32[]{:S(2)}) collective-permute-start(bf16[4,52,512]{2,1,0:T(8,128)(2,1)S(1)} %maximum_select_fusion.3), channel_id=1, source_target_pairs={{0,4},{1,5},{2,3},{3,2},{4,0},{5,1},{6,7},{7,6},{8,12},{9,13},{10,... | collective-permute-start | bytes 638984 | tf_op jit(solution)/shard_map/ppermute | solution.py:742
  282.4 13.9 %collective-permute-start.16 = (bf16[8,52,512]{2,1,0:T(8,128)(2,1)S(1)}, bf16[8,52,512]{2,1,0:T(8,128)(2,1)S(1)}, u32[]{:S(2)}, u32[]{:S(2)}) collective-permute-start(bf16[8,52,512]{2,1,0:T(8,128)(2,1)S(1)} %maximum_select_fusion.2), channel_id=1, source_target_pairs={{0,1},{1,0},{2,6},{3,7},{4,5},{5,4},{6,2},{7,3},{8,9},{9,8},{10,14... | collective-permute-start | bytes 1277960 | tf_op jit(solution)/shard_map/ppermute | solution.py:742
  286.1 18.7 %collective-permute-start.18 = (bf16[3,256,512]{2,1,0:T(8,128)(2,1)}, bf16[3,256,512]{2,1,0:T(8,128)(2,1)S(1)}, u32[]{:S(2)}, u32[]{:S(2)}) collective-permute-start(bf16[3,256,512]{2,1,0:T(8,128)(2,1)} %get-tuple-element.98), channel_id=1, source_target_pairs={{0,1},{1,0},{2,3},{3,2},{4,5},{5,4},{6,7},{7,6},{8,9},{9,8},{10,11... | collective-permute-start | bytes 2359304 | tf_op jit(solution)/shard_map/ppermute | solution.py:678
  296.7 9.1 %collective-permute-start.17 = (bf16[16,52,512]{2,0,1:T(8,128)(2,1)S(1)}, bf16[16,52,512]{2,0,1:T(8,128)(2,1)S(1)}, u32[]{:S(2)}, u32[]{:S(2)}) collective-permute-start(bf16[16,52,512]{2,0,1:T(8,128)(2,1)S(1)} %copy.70), channel_id=1, source_target_pairs={{0,2},{1,3},{2,0},{3,1},{4,6},{5,7},{6,4},{7,5},{8,10},{9,11},{10,... | collective-permute-start | bytes 2555912 | tf_op jit(solution)/shard_map/ppermute | solution.py:742
Sparse Core Ops, SparseCore 0:
  226.6 72.2 all-gather.1
